TPU v7x, 32 devices: a whole 2x2x4 slice. The times are simulated.
32 devices in a mesh: expert: 8 (over y, x, core), dp: 4 (over z).
Axes of the slice: x: 2, y: 2, z: 4, core: 2. Of those that a mesh axis runs over, the one named last changes fastest.
Arguments:
- tokens: bfloat16 [4096, 2048], P(('dp', 'expert')), parts along dimension 0, may hold values from -6 to 6
- expert_ids: int32 [4096, 4], P(('dp', 'expert')), parts along dimension 0, may hold values from 0 to 7, all different within a row; in each aligned block of 128 rows (0 to 127, 128 to 255, ...) at most 96 rows name the same one
- gate_weights: bfloat16 [4096, 4], P(('dp', 'expert')), parts along dimension 0, may hold values from 0.049804688 to 1
- w_gate: bfloat16 [8, 2048, 768], P('expert'), may hold values from -0.125 to 0.125
- w_up: bfloat16 [8, 2048, 768], P('expert'), may hold values from -0.125 to 0.125
- w_down: bfloat16 [8, 768, 2048], P('expert'), may hold values from -0.21875 to 0.21875
Outputs:
- mixed: bfloat16 [4096, 2048], P(('dp', 'expert')), parts along dimension 0
There are 4 independent parts, one for each index of `dp`. A program takes and returns all parts, laid end to end along the dimension named above; an argument that names none is the same for every part. Nothing has to cross between parts.
Inputs may be any that keep to these rules, and one draw needn't show every extreme that they name: `expert_ids`: each row names 4 different experts. In each aligned block of 128 rows (the rows of one device) no expert is named by more than 96 rows, a bound that some block reaches.
All inputs are finite; a program needn't handle non-finite values.
Results may differ from a plain program's by a relative error of at most 0.0049.
Values may be sent and summed in bfloat16 or wider, within the bound.
No kernel may reach another device: no remote copies, remote signals or barrier semaphores. Data moves between devices by JAX's collectives and lax.ppermute only.
A program may use at most 128 MiB of HBM per device.

v0:
```python
import jax
import jax.numpy as jnp
from jax import lax
from jax.sharding import PartitionSpec as P


def slot_table(routed, capacity):
    counted = routed.astype(jnp.int32)
    position = jnp.cumsum(counted, axis=1) - 1
    slot_ids = jnp.arange(capacity, dtype=jnp.int32)
    chosen = routed[:, None, :] & (position[:, None, :] == slot_ids[None, :, None])
    row_ids = jnp.arange(routed.shape[1], dtype=jnp.int32)
    slot_index = jnp.sum(jnp.where(chosen, row_ids[None, None, :], 0), axis=2)
    filled = jnp.any(chosen, axis=2)
    return (slot_index, filled)


def expert_ffn(slot_block, w_gate, w_up, w_down):
    width = slot_block.shape[-1]
    flat_rows = slot_block.reshape(-1, width)
    gate_act = jnp.dot(flat_rows, w_gate[0], preferred_element_type=jnp.float32)
    up_act = jnp.dot(flat_rows, w_up[0], preferred_element_type=jnp.float32)
    hidden = (jax.nn.silu(gate_act) * up_act).astype(jnp.bfloat16)
    expert_out = jnp.dot(hidden, w_down[0], preferred_element_type=jnp.float32)
    return expert_out.reshape(slot_block.shape[:-1] + (w_down.shape[2],))


def send_back(expert_out):
    return lax.all_to_all(expert_out, "expert", split_axis=0, concat_axis=0, tiled=True)


def on_device(tokens, expert_ids, gate_weights, w_gate, w_up, w_down):
    tok_dev, choose_k = expert_ids.shape
    width = tokens.shape[1]
    groups = lax.axis_size("expert")
    experts = w_gate.shape[0] * groups
    capacity = min(tok_dev, 3 * tok_dev * choose_k // (2 * experts))
    labels = jnp.arange(experts, dtype=jnp.int32)
    matched = expert_ids[:, :, None] == labels[None, None, :]
    weight = jnp.sum(
        jnp.where(matched, gate_weights.astype(jnp.float32)[:, :, None], jnp.float32(0.0)), axis=1
    )
    home_index, home_filled = slot_table(weight.T != 0.0, capacity)
    picked = tokens[home_index]
    returned_rows = send_back(
        expert_ffn(
            lax.all_to_all(picked, "expert", split_axis=0, concat_axis=0, tiled=True),
            w_gate,
            w_up,
            w_down,
        )
    )
    owners = jnp.arange(experts, dtype=jnp.int32)[:, None]
    factor = jnp.where(home_filled, weight.T[owners, home_index], jnp.float32(0.0))
    combined = jnp.zeros((tok_dev, width), jnp.float32)
    combined = combined.at[home_index.reshape(-1)].add(
        (factor[:, :, None] * returned_rows).reshape(-1, width)
    )
    return combined.astype(jnp.bfloat16)


def solution(mesh):
    return jax.shard_map(
        on_device,
        mesh=mesh,
        in_specs=(
            P(("dp", "expert"), None),
            P(("dp", "expert"), None),
            P(("dp", "expert"), None),
            P("expert", None, None),
            P("expert", None, None),
            P("expert", None, None),
        ),
        out_specs=P(("dp", "expert"), None),
        check_vma=False,
    )
```

profile of v0, /device:TPU:0, one launch (start us, length us, event | category | flops | bytes accessed | tf_op | source)
XLA Modules:
  0.0 163.9 jit_solution(7774825319647874410)
XLA Ops:
  0.0 0.0 copy-start
  0.0 0.8 convert_element_type.12
  0.8 0.8 select_reduce_fusion.1
  1.7 0.3 reduce_window_sum.11
  1.9 0.2 select_reduce_fusion
  2.2 0.1 reshape.80
  2.3 8.2 %gather_fusion.1 = bf16[768,2048]{1,0:T(8,128)(2,1)} fusion(bf16[128,2048]{1,0:T(8,128)(2,1)} %param.6, s32[1024]{0:T(1024)S(1)} %pad_clamp_fusion), kind=kCustom, calls=%fused_computation.1 | custom fusion | bytes 6294528 | tf_op jit(solution)/shard_map/gather | solution.py:44
  10.5 0.0 copy-start.1
  10.5 43.3 %all_to_all.10 = bf16[8,96,2048]{2,1,0:T(8,128)(2,1)S(1)} all-to-all(bf16[8,96,2048]{2,1,0:T(8,128)(2,1)} %bitcast.31), channel_id=1, replica_groups=mesh['expert'=8,'dp'=4] {'expert'}, dimensions={0} | all-to-all | bytes 6291456 | tf_op jit(solution)/shard_map/all_to_all | solution.py:47
  53.7 0.0 copy-done.1
  53.7 0.0 copy-start.2
  53.8 2.6 %fusion.2 = f32[768,768]{1,0:T(8,128)S(1)} fusion(bf16[768,2048]{1,0:T(8,128)(2,1)S(1)} %bitcast.33, bf16[1,2048,768]{2,1,0:T(8,128)(2,1)S(1)} %copy-done.1), kind=kOutput, calls=%fused_computation.5 | convolution fusion | flops 2415919104 | bytes 8650752 | tf_op jit(solution)/shard_map/dot_general | solution.py:22
  56.4 0.0 copy-done.2
  56.4 2.9 %multiply_convert_fusion = bf16[768,768]{1,0:T(8,128)(2,1)S(1)} fusion(f32[768,768]{1,0:T(8,128)S(1)} %fusion.2, bf16[768,2048]{1,0:T(8,128)(2,1)S(1)} %bitcast.34, bf16[1,2048,768]{2,1,0:T(8,128)(2,1)S(1)} %copy-done.2), kind=kOutput, calls=%fused_computation.10 | convolution fusion | flops 2419458048 | bytes 9830400 | tf_op jit(solution)/shard_map/dot_general | solution.py:21
  59.3 0.0 copy-done
  59.3 4.6 %fusion = f32[8,96,2048]{2,1,0:T(8,128)} fusion(bf16[8,96,768]{2,1,0:T(8,128)(2,1)S(1)} %bitcast.35, bf16[1,768,2048]{2,1,0:T(8,128)(2,1)S(1)} %copy-done), kind=kOutput, calls=%fused_computation.3 | convolution fusion | flops 2415919104 | bytes 10616832 | tf_op jit(solution)/shard_map/dot_general | solution.py:24
  63.9 4.9 %all-to-all-start.1 = ((f32[8,96,2048]{2,1,0:T(8,128)}), f32[8,96,2048]{2,1,0:T(8,128)}, u32[]{:S(2)}, u32[]{:S(2)}) async-start(f32[8,96,2048]{2,1,0:T(8,128)} %fusion), calls=%async_computation.1 | async-start | bytes 12582912 | tf_op jit(solution)/shard_map/all_to_all | solution.py:29
  68.8 0.1 reshape.69
  68.9 0.1 reshape.72
  69.0 3.2 %gather_fusion = f32[768]{0:T(1024)S(1)} fusion(f32[8,128]{1,0:T(8,128)S(1)} %bitcast.30, s32[768]{0:T(1024)S(1)} %reshape.72), kind=kCustom, calls=%fused_computation | custom fusion | bytes 12288 | tf_op jit(solution)/shard_map/gather | solution.py:54
  72.2 0.1 reshape.75
  72.3 0.2 fusion.11
  72.5 67.7 %all-to-all-done.1 = f32[8,96,2048]{2,1,0:T(8,128)} async-done(((f32[8,96,2048]{2,1,0:T(8,128)}), f32[8,96,2048]{2,1,0:T(8,128)}, u32[]{:S(2)}, u32[]{:S(2)}) %all-to-all-start.1) | async-done | bytes 6291488 | tf_op jit(solution)/shard_map/all_to_all | solution.py:29
  140.2 5.9 %broadcast_multiply_fusion = f32[8,96,2048]{2,1,0:T(8,128)} fusion(f32[8,96,2048]{2,1,0:T(8,128)} %all-to-all-done.1, f32[8,96]{1,0:T(8,128)S(1)} %broadcast_select_fusion), kind=kLoop, calls=%fused_computation.9 | loop fusion | flops 1572864 | bytes 12585984 | tf_op jit(solution)/shard_map/mul | solution.py:57
  146.1 15.7 %scatter_custom_fusion = f32[128,2048]{1,0:T(8,128)} fusion(s32[768]{0:T(1024)S(1)} %fusion.12, f32[768,2048]{1,0:T(8,128)} %bitcast.32, f32[]{:T(128)} %constant.6.clone.1), kind=kCustom, calls=%fused_computation.11 | custom fusion | flops 1572864 | bytes 1049088 | tf_op jit(solution)/shard_map/scatter-add | solution.py:56
  161.8 2.1 %convert_element_type.15 = bf16[128,2048]{1,0:T(8,128)(2,1)} convert(f32[128,2048]{1,0:T(8,128)} %scatter_custom_fusion) | non-fusion elementwise | flops 262144 | bytes 1572864 | tf_op jit(solution)/shard_map/convert_element_type | solution.py:59
  (6 shorter events, 0.1 us)
Async XLA Ops:
  0.0 59.3 %copy-start = (bf16[1,768,2048]{2,1,0:T(8,128)(2,1)S(1)}, bf16[1,768,2048]{2,1,0:T(8,128)(2,1)}, u32[]{:S(2)}) copy-start(bf16[1,768,2048]{2,1,0:T(8,128)(2,1)} %param.11) | copy-start | bytes 9437188
  10.5 43.3 %copy-start.1 = (bf16[1,2048,768]{2,1,0:T(8,128)(2,1)S(1)}, bf16[1,2048,768]{2,1,0:T(8,128)(2,1)}, u32[]{:S(2)}) copy-start(bf16[1,2048,768]{2,1,0:T(8,128)(2,1)} %param.10) | copy-start | bytes 9437188
  53.7 2.6 %copy-start.2 = (bf16[1,2048,768]{2,1,0:T(8,128)(2,1)S(1)}, bf16[1,2048,768]{2,1,0:T(8,128)(2,1)}, u32[]{:S(2)}) copy-start(bf16[1,2048,768]{2,1,0:T(8,128)(2,1)} %param.9) | copy-start | bytes 9437188
  63.9 76.3 %all-to-all-start.1 = ((f32[8,96,2048]{2,1,0:T(8,128)}), f32[8,96,2048]{2,1,0:T(8,128)}, u32[]{:S(2)}, u32[]{:S(2)}) async-start(f32[8,96,2048]{2,1,0:T(8,128)} %fusion), calls=%async_computation.1 | async-start | bytes 12582912 | tf_op jit(solution)/shard_map/all_to_all | solution.py:29
where the time goes:
time: 164 us
  waiting for transfers between devices  67.7 us (41%)
  blocking collectives  43.3 us (26%)
  other arithmetic  26.1 us (16%)
  local copies, waits for them, and re-layouts  11.7 us (7%)
  matrix products  10.1 us (6%)
  starting transfers between devices  4.92 us (3%)
    all_to_all x1, waiting for transfers between devices, send_back(): lax.all_to_all(expert_out, 'expert', split_axis=0, concat_axis=0, tiled=T...  67.7 us
    all_to_all x1, blocking collectives, on_device(): lax.all_to_all(picked, 'expert', split_axis=0, concat_axis=0, tiled=True)  43.3 us
    scatter-add x1, other arithmetic, on_device(): combined.at[home_index.reshape(-1)]  15.7 us
    gather x1, local copies, waits for them, and re-layouts, on_device(): picked = tokens[home_index]  8.22 us
    mul x1, other arithmetic, on_device(): factor[:, :, None] * returned_rows  5.91 us
    all_to_all x1, starting transfers between devices, send_back(): lax.all_to_all(expert_out, 'expert', split_axis=0, concat_axis=0, tiled=T...  4.92 us
    dot_general x1, matrix products, expert_ffn(): expert_out = jnp.dot(hidden, w_down[0], preferred_element_type=jnp.float32)  4.61 us
  transfers between devices with their start and end apart: 1, of which 1 were waited for; matrix products, arithmetic and copies ran while one was open for 2% of the time, Pallas kernels for 0%

commit v1 on v0

v1 whole, which is shorter than its diff:
```python
import functools

import jax
import jax.numpy as jnp
from jax import lax
from jax.experimental import pallas as pl
from jax.experimental.pallas import tpu as pltpu
from jax.sharding import PartitionSpec as P

AXIS = "expert"
CORE, XBIT, YBIT = 1, 2, 4


def slot_table(routed, capacity):
    counted = routed.astype(jnp.int32)
    position = jnp.cumsum(counted, axis=1) - 1
    slot_ids = jnp.arange(capacity, dtype=jnp.int32)
    chosen = routed[:, None, :] & (position[:, None, :] == slot_ids[None, :, None])
    row_ids = jnp.arange(routed.shape[1], dtype=jnp.int32)
    slot_index = jnp.sum(jnp.where(chosen, row_ids[None, None, :], 0), axis=2)
    filled = jnp.any(chosen, axis=2)
    return (slot_index, filled)


def expert_ffn(slot_block, w_gate, w_up, w_down):
    width = slot_block.shape[-1]
    flat_rows = slot_block.reshape(-1, width)
    gate_act = jnp.dot(flat_rows, w_gate[0], preferred_element_type=jnp.float32)
    up_act = jnp.dot(flat_rows, w_up[0], preferred_element_type=jnp.float32)
    hidden = (jax.nn.silu(gate_act) * up_act).astype(jnp.bfloat16)
    expert_out = jnp.dot(hidden, w_down[0], preferred_element_type=jnp.float32)
    return expert_out.reshape(slot_block.shape[:-1] + (w_down.shape[2],))


def swap_all(rows):
    return lax.all_to_all(rows, AXIS, split_axis=0, concat_axis=0, tiled=True)


def route_table(expert_ids, gate_weights, experts):
    labels = jnp.arange(experts, dtype=jnp.int32)
    matched = expert_ids[:, :, None] == labels[None, None, :]
    weights = gate_weights.astype(jnp.float32)[:, :, None]
    return jnp.sum(jnp.where(matched, weights, jnp.float32(0.0)), axis=1)


def any_slice(tokens, expert_ids, gate_weights, w_gate, w_up, w_down):
    tok_dev, choose_k = expert_ids.shape
    width = tokens.shape[1]
    experts = w_gate.shape[0] * lax.axis_size(AXIS)
    capacity = min(tok_dev, 3 * tok_dev * choose_k // (2 * experts))
    weight = route_table(expert_ids, gate_weights, experts)
    home_index, home_filled = slot_table(weight.T != 0.0, capacity)
    arrived = swap_all(tokens[home_index])
    returned_rows = swap_all(expert_ffn(arrived, w_gate, w_up, w_down))
    owners = jnp.arange(experts, dtype=jnp.int32)[:, None]
    factor = jnp.where(home_filled, weight.T[owners, home_index], jnp.float32(0.0))
    combined = jnp.zeros((tok_dev, width), jnp.float32)
    combined = combined.at[home_index.reshape(-1)].add(
        (factor[:, :, None] * returned_rows).reshape(-1, width)
    )
    return combined.astype(jnp.bfloat16)


def hop(block, bits):
    return lax.ppermute(block, AXIS, [(i, i ^ bits) for i in range(lax.axis_size(AXIS))])


def ffn_body(pieces, *refs):
    n = len(pieces)
    x_refs = refs[:n]
    route_ref = refs[n]
    weights = refs[n + 1 : n + 7]
    o_refs = refs[n + 7 : 2 * n + 7]
    x_buf, *bufs, x_sem, w_sem = refs[2 * n + 7 :]
    starts = [sum(pieces[:k]) for k in range(n)]
    x_copies = [
        pltpu.make_async_copy(x_refs[k], x_buf.at[pl.ds(starts[k], pieces[k])], x_sem.at[k])
        for k in range(n)
    ]
    w_copies = [pltpu.make_async_copy(weights[k], bufs[k], w_sem.at[k]) for k in range(6)]
    w_copies[0].start()
    for copy in x_copies:
        copy.start()
    for copy in w_copies[1:]:
        copy.start()
    for copy in x_copies:
        copy.wait()
    x = x_buf[...]
    total = None
    for e in range(2):
        w_copies[3 * e].wait()
        gate = jnp.dot(x, bufs[3 * e][...], preferred_element_type=jnp.float32)
        w_copies[3 * e + 1].wait()
        up = jnp.dot(x, bufs[3 * e + 1][...], preferred_element_type=jnp.float32)
        hidden = (gate / (1.0 + jnp.exp(-gate)) * up).astype(jnp.bfloat16)
        w_copies[3 * e + 2].wait()
        out = jnp.dot(hidden, bufs[3 * e + 2][...], preferred_element_type=jnp.float32)
        out = route_ref[:, e : e + 1] * out
        total = out if total is None else total + out
    total = total.astype(jnp.bfloat16)
    for k in range(n):
        o_refs[k][...] = total[starts[k] : starts[k] + pieces[k]]


def ffn(blocks, route, weights):
    pieces = tuple(block.shape[0] for block in blocks)
    rows, width = sum(pieces), blocks[0].shape[1]
    hidden = weights[0].shape[1]
    moved = sum(w.size * 2 for w in weights) + 4 * rows * width
    return pl.pallas_call(
        functools.partial(ffn_body, pieces),
        out_shape=[jax.ShapeDtypeStruct((p, width), jnp.bfloat16) for p in pieces],
        in_specs=[pl.BlockSpec(memory_space=pl.ANY)] * len(blocks)
        + [pl.BlockSpec(memory_space=pltpu.VMEM)]
        + [pl.BlockSpec(memory_space=pl.ANY)] * 6,
        out_specs=[pl.BlockSpec(memory_space=pltpu.VMEM)] * len(blocks),
        scratch_shapes=[pltpu.VMEM((rows, width), jnp.bfloat16)]
        + [pltpu.VMEM(w.shape, jnp.bfloat16) for w in weights]
        + [pltpu.SemaphoreType.DMA((len(blocks),)), pltpu.SemaphoreType.DMA((6,))],
        compiler_params=pltpu.CompilerParams(vmem_limit_bytes=40 * 1024 * 1024),
        cost_estimate=pl.CostEstimate(
            flops=12 * rows * width * hidden, bytes_accessed=moved, transcendentals=2 * rows * hidden
        ),
    )(*blocks, route, *weights)


def two_by_two(tokens, expert_ids, gate_weights, w_gate, w_up, w_down):
    tok_dev = tokens.shape[0]
    half = tok_dev // 2
    me = lax.axis_index(AXIS)
    route = route_table(expert_ids, gate_weights, lax.axis_size(AXIS)).astype(jnp.bfloat16)
    routes = lax.all_gather(route, AXIS, axis=0)
    top, low = tokens[:half], tokens[half:]

    x_top, y_low = hop(top, XBIT), hop(low, YBIT)
    own = (w_gate[0], w_up[0], w_down[0])
    weights = own + tuple(hop(w, CORE) for w in own)
    d_top, d_low = hop(x_top, YBIT), hop(y_low, XBIT)
    x_low, y_top = hop(low, XBIT), hop(top, YBIT)

    def columns(bits, rows):
        table = lax.dynamic_index_in_dim(routes, me ^ bits, 0, keepdims=False)[rows]
        pair = [lax.dynamic_index_in_dim(table, me ^ b, 1) for b in (0, CORE)]
        return jnp.concatenate(pair, axis=1).astype(jnp.float32)

    tops, lows, both = slice(0, half), slice(half, tok_dev), slice(0, tok_dev)
    first = [columns(XBIT, tops), columns(YBIT, lows), columns(XBIT | YBIT, both)]
    second = [columns(0, both), columns(XBIT, lows), columns(YBIT, tops)]
    ox_top, oy_low, od_top, od_low = ffn(
        [x_top, y_low, d_top, d_low], jnp.concatenate(first), weights
    )
    e_top, e_low = hop(od_top, XBIT), hop(od_low, YBIT)
    fx_top, fy_low = hop(ox_top, XBIT), hop(oy_low, YBIT)
    o_own, ox_low, oy_top = ffn([tokens, x_low, y_top], jnp.concatenate(second), weights)
    f32 = lambda a: a.astype(jnp.float32)
    my_top = hop((f32(oy_top) + f32(e_top)).astype(jnp.bfloat16), YBIT)
    mx_low = hop((f32(ox_low) + f32(e_low)).astype(jnp.bfloat16), XBIT)
    out_top = f32(o_own[:half]) + f32(fx_top) + f32(my_top)
    out_low = f32(o_own[half:]) + f32(fy_low) + f32(mx_low)
    return jnp.concatenate([out_top, out_low]).astype(jnp.bfloat16)


def solution(mesh):
    return jax.shard_map(
        two_by_two if mesh.shape[AXIS] == 8 else any_slice,
        mesh=mesh,
        in_specs=(
            P(("dp", AXIS), None),
            P(("dp", AXIS), None),
            P(("dp", AXIS), None),
            P(AXIS, None, None),
            P(AXIS, None, None),
            P(AXIS, None, None),
        ),
        out_specs=P(("dp", AXIS), None),
        check_vma=False,
    )
```

time: 164 us -> 63.5 us (0.39)
  waiting for transfers between devices: 67.7 us -> 11.2 us
  blocking collectives: 43.3 us -> 9.58 us
  other arithmetic: 26.1 us -> 1.88 us
  Pallas kernels: 0 us -> 15.6 us
  starting transfers between devices: 4.92 us -> 16.8 us
  matrix products: 10.1 us -> 0 us
  local copies, waits for them, and re-layouts: 11.7 us -> 7.94 us
    all_to_all x1 -> x0, waiting for transfers between devices: 67.7 us -> none  [send_back(): lax.all_to_all(expert_out, 'expert', split_axis=0, concat_axis=0, tiled=T...]
    all_to_all x1 -> x0, blocking collectives: 43.3 us -> none  [on_device(): lax.all_to_all(picked, 'expert', split_axis=0, concat_axis=0, tiled=True)]
    ppermute x0 -> x15, starting transfers between devices: none -> 16.8 us  [hop(): lax.ppermute(block, AXIS, [(i, i ^ bits) for i in range(lax.axis_size(AXI...]
    scatter-add x1 -> x0, other arithmetic: 15.7 us -> none  [on_device(): combined.at[home_index.reshape(-1)]]
    pallas_call x0 -> x2, Pallas kernels: none -> 15.6 us  [ffn(): pl.pallas_call(functools.partial(ffn_body, pieces), out_shape=[jax.ShapeD...]
    gather x3 -> x0, local copies, waits for them, and re-layouts: 11.5 us -> none  [the longest x1 8.22 us: on_device(): picked = tokens[home_index]]
    ppermute x0 -> x15, waiting for transfers between devices: none -> 11.2 us  [hop(): lax.ppermute(block, AXIS, [(i, i ^ bits) for i in range(lax.axis_size(AXI...]
    dot_general x3 -> x0, matrix products: 10.1 us -> none  [the longest x1 4.61 us: expert_ffn(): expert_out = jnp.dot(hidden, w_down[0], preferred_element_type=jnp.float32)]
  transfers between devices with their start and end apart: 1 -> 15, of which waited for: 1 -> 3; matrix products, arithmetic and copies ran while one was open for 2% -> 5% of each run, Pallas kernels for 0% -> 25%
where the time goes in v1:
time: 63.5 us; the launch traced here: 63.2 us
  starting transfers between devices  16.8 us (26%)
  Pallas kernels  15.6 us (25%)
  waiting for transfers between devices  11.2 us (18%)
  blocking collectives  9.58 us (15%)
  local copies, waits for them, and re-layouts  7.94 us (13%)
  other arithmetic  1.88 us (3%)
    ppermute x15, starting transfers between devices, hop(): lax.ppermute(block, AXIS, [(i, i ^ bits) for i in range(lax.axis_size(AXI...  16.8 us
    pallas_call x2, Pallas kernels, ffn(): pl.pallas_call(functools.partial(ffn_body, pieces), out_shape=[jax.ShapeD...  15.6 us
    ppermute x15, waiting for transfers between devices, hop(): lax.ppermute(block, AXIS, [(i, i ^ bits) for i in range(lax.axis_size(AXI...  11.2 us
    all_gather x1, blocking collectives, two_by_two(): routes = lax.all_gather(route, AXIS, axis=0)  9.58 us
    unnamed x16, local copies, waits for them, and re-layouts  6.47 us
  transfers between devices with their start and end apart: 15, of which 3 were waited for; matrix products, arithmetic and copies ran while one was open for 5% of the time, Pallas kernels for 25%

profile of v1, /device:TPU:0, one launch (start us, length us, event | category | flops | bytes accessed | tf_op | source)
XLA Modules:
  0.0 63.2 jit_solution(5292200462361238840)
XLA Ops:
  0.0 0.5 collective-permute-start.2
  0.5 0.1 collective-permute-start.3
  0.5 0.5 collective-permute-start.4
  1.0 1.1 %fusion.12 = (bf16[64,2048]{1,0:T(8,128)(2,1)S(1)}, bf16[64,2048]{1,0:T(8,128)(2,1)S(1)}) fusion(bf16[128,2048]{1,0:T(8,128)(2,1)} %refs_0_.1), kind=kLoop, calls=%fused_computation.35 | loop fusion | bytes 1048576 | tf_op jit(solution)/shard_map/slice | solution.py:133
  2.0 2.6 %collective-permute-start.5 = (bf16[64,2048]{1,0:T(8,128)(2,1)S(1)}, bf16[64,2048]{1,0:T(8,128)(2,1)S(1)}, u32[]{:S(2)}, u32[]{:S(2)}) collective-permute-start(bf16[64,2048]{1,0:T(8,128)(2,1)S(1)} %get-tuple-element.22), channel_id=1, source_target_pairs={{0,8},{4,12},{8,0},{12,4},{16,24},{20,28},{24,16},{28,20},{1,9},{5... | collective-permute-start | bytes 786440 | tf_op jit(solution)/shard_map/ppermute | solution.py:65
  4.6 1.5 %collective-permute-start.6 = (bf16[64,2048]{1,0:T(8,128)(2,1)S(1)}, bf16[64,2048]{1,0:T(8,128)(2,1)S(1)}, u32[]{:S(2)}, u32[]{:S(2)}) collective-permute-start(bf16[64,2048]{1,0:T(8,128)(2,1)S(1)} %get-tuple-element.21), channel_id=1, source_target_pairs={{0,16},{4,20},{8,24},{12,28},{16,0},{20,4},{24,8},{28,12},{1,17},{... | collective-permute-start | bytes 786440 | tf_op jit(solution)/shard_map/ppermute | solution.py:65
  6.1 0.7 %convert_element_type.59 = f32[128,4]{0,1:T(4,128)S(1)} convert(bf16[128,4]{0,1:T(4,128)(2,1)} %param.8) | non-fusion elementwise | flops 512 | bytes 3072 | tf_op jit(solution)/shard_map/convert_element_type | solution.py:42
  6.8 0.7 %select_reduce_fusion = bf16[128,8]{0,1:T(8,128)(2,1)S(1)} fusion(f32[128,4]{0,1:T(4,128)S(1)} %convert_element_type.59, s32[128,4]{0,1:T(4,128)} %param.7), kind=kLoop, calls=%fused_computation.5 | loop fusion | flops 11264 | bytes 6144 | tf_op jit(solution)/shard_map/reduce_sum | solution.py:43
  7.5 9.6 %all-gather = bf16[1024,8]{0,1:T(8,128)(2,1)S(1)} all-gather(bf16[128,8]{0,1:T(8,128)(2,1)S(1)} %select_reduce_fusion), channel_id=2, replica_groups=mesh['expert'=8,'dp'=4] {'expert'}, dimensions={0}, use_global_device_ids=true | all-gather | bytes 18432 | tf_op jit(solution)/shard_map/all_gather | solution.py:132
  17.1 0.1 fusion.13
  17.2 0.1 maximum_convert_fusion.1
  17.3 0.0 collective-permute-done.5.refs_0_
  17.3 1.4 %collective-permute-start.7 = (bf16[64,2048]{1,0:T(8,128)(2,1)S(1)}, bf16[64,2048]{1,0:T(8,128)(2,1)S(1)}, u32[]{:S(2)}, u32[]{:S(2)}) collective-permute-start(bf16[64,2048]{1,0:T(8,128)(2,1)S(1)} %collective-permute-done.5.refs_0_), channel_id=1, source_target_pairs={{0,16},{4,20},{8,24},{12,28},{16,0},{20,4},{24,8},{28,12},{1,17},{... | collective-permute-start | bytes 786440 | tf_op jit(solution)/shard_map/ppermute | solution.py:65
  18.7 0.0 collective-permute-done.6.refs_1_
  18.7 1.5 %collective-permute-start.8 = (bf16[64,2048]{1,0:T(8,128)(2,1)S(1)}, bf16[64,2048]{1,0:T(8,128)(2,1)S(1)}, u32[]{:S(2)}, u32[]{:S(2)}) collective-permute-start(bf16[64,2048]{1,0:T(8,128)(2,1)S(1)} %collective-permute-done.6.refs_1_), channel_id=1, source_target_pairs={{0,8},{4,12},{8,0},{12,4},{16,24},{20,28},{24,16},{28,20},{1,9},{5... | collective-permute-start | bytes 786440 | tf_op jit(solution)/shard_map/ppermute | solution.py:65
  20.2 0.1 copy.42.refs_4_
  20.4 0.1 maximum_convert_fusion
  20.4 0.1 copy.41.refs_3_
  20.6 5.3 %collective-permute-done.7.refs_2_ = bf16[64,2048]{1,0:T(8,128)(2,1)S(1)} collective-permute-done((bf16[64,2048]{1,0:T(8,128)(2,1)S(1)}, bf16[64,2048]{1,0:T(8,128)(2,1)S(1)}, u32[]{:S(2)}, u32[]{:S(2)}) %collective-permute-start.7) | collective-permute-done | bytes 262176 | tf_op jit(solution)/shard_map/ppermute | solution.py:65
  25.9 1.4 %collective-permute-start = (bf16[64,2048]{1,0:T(8,128)(2,1)S(1)}, bf16[64,2048]{1,0:T(8,128)(2,1)S(1)}, u32[]{:S(2)}, u32[]{:S(2)}) collective-permute-start(bf16[64,2048]{1,0:T(8,128)(2,1)S(1)} %get-tuple-element.21), channel_id=1, source_target_pairs={{0,8},{4,12},{8,0},{12,4},{16,24},{20,28},{24,16},{28,20},{1,9},{5... | collective-permute-start | bytes 786440 | tf_op jit(solution)/shard_map/ppermute | solution.py:65
  27.2 0.0 collective-permute-done.8.refs_3_
  27.2 1.5 %collective-permute-start.1 = (bf16[64,2048]{1,0:T(8,128)(2,1)S(1)}, bf16[64,2048]{1,0:T(8,128)(2,1)S(1)}, u32[]{:S(2)}, u32[]{:S(2)}) collective-permute-start(bf16[64,2048]{1,0:T(8,128)(2,1)S(1)} %get-tuple-element.22), channel_id=1, source_target_pairs={{0,16},{4,20},{8,24},{12,28},{16,0},{20,4},{24,8},{28,12},{1,17},{... | collective-permute-start | bytes 786440 | tf_op jit(solution)/shard_map/ppermute | solution.py:65
  28.7 0.0 collective-permute-done.2.refs_7_.refs_8_
  28.7 0.0 collective-permute-done.3.refs_8_.refs_9_
  28.7 0.0 collective-permute-done.4.refs_9_.refs_10_
  28.7 0.0 copy-start
  28.8 1.9 %copy-done = bf16[1,2048,768]{2,1,0:T(8,128)(2,1)S(1)} copy-done((bf16[1,2048,768]{2,1,0:T(8,128)(2,1)S(1)}, bf16[1,2048,768]{2,1,0:T(8,128)(2,1)}, u32[]{:S(2)}) %copy-start) | copy-done | bytes 3145752
  30.6 1.9 %copy-done.2 = bf16[1,2048,768]{2,1,0:T(8,128)(2,1)S(1)} copy-done((bf16[1,2048,768]{2,1,0:T(8,128)(2,1)S(1)}, bf16[1,2048,768]{2,1,0:T(8,128)(2,1)}, u32[]{:S(2)}) %copy-start.2) | copy-done | bytes 3145752
  32.5 1.9 %copy-done.4 = bf16[1,768,2048]{2,1,0:T(8,128)(2,1)S(1)} copy-done((bf16[1,768,2048]{2,1,0:T(8,128)(2,1)S(1)}, bf16[1,768,2048]{2,1,0:T(8,128)(2,1)}, u32[]{:S(2)}) %copy-start.4) | copy-done | bytes 3145752
  34.4 7.8 %shard_map.65 = (bf16[64,2048]{1,0:T(8,128)(2,1)S(1)}, bf16[64,2048]{1,0:T(8,128)(2,1)S(1)}, bf16[64,2048]{1,0:T(8,128)(2,1)S(1)}, bf16[64,2048]{1,0:T(8,128)(2,1)S(1)}) custom-call(bf16[64,2048]{1,0:T(8,128)(2,1)S(1)} %collective-permute-done.5.refs_0_, bf16[64,2048]{1,0:T(8,128)(2,1)S(1)} %collective-permute-done.6.refs_1_, ...), custom_call_target="tpu_custom_call" | custom-call | flops 4831838208 | bytes 20971520 | tf_op jit(solution)/shard_map/pallas_call | solution.py:110
  42.3 0.6 collective-permute-start.10
  42.9 1.5 %collective-permute-start.9 = (bf16[64,2048]{1,0:T(8,128)(2,1)S(1)}, bf16[64,2048]{1,0:T(8,128)(2,1)S(1)}, u32[]{:S(2)}, u32[]{:S(2)}) collective-permute-start(bf16[64,2048]{1,0:T(8,128)(2,1)S(1)} %get-tuple-element.13), channel_id=1, source_target_pairs={{0,8},{4,12},{8,0},{12,4},{16,24},{20,28},{24,16},{28,20},{1,9},{5... | collective-permute-start | bytes 786440 | tf_op jit(solution)/shard_map/ppermute | solution.py:65
  44.3 0.5 collective-permute-start.13
  44.8 0.0 collective-permute-done.refs_1_
  44.9 1.5 %collective-permute-start.12 = (bf16[64,2048]{1,0:T(8,128)(2,1)S(1)}, bf16[64,2048]{1,0:T(8,128)(2,1)S(1)}, u32[]{:S(2)}, u32[]{:S(2)}) collective-permute-start(bf16[64,2048]{1,0:T(8,128)(2,1)S(1)} %get-tuple-element.16), channel_id=1, source_target_pairs={{0,16},{4,20},{8,24},{12,28},{16,0},{20,4},{24,8},{28,12},{1,17},{... | collective-permute-start | bytes 786440 | tf_op jit(solution)/shard_map/ppermute | solution.py:65
  46.4 0.0 collective-permute-done.1.refs_2_
  46.4 7.8 %shard_map.64 = (bf16[128,2048]{1,0:T(8,128)(2,1)S(1)}, bf16[64,2048]{1,0:T(8,128)(2,1)S(1)}, bf16[64,2048]{1,0:T(8,128)(2,1)S(1)}) custom-call(bf16[128,2048]{1,0:T(8,128)(2,1)S(1)} %copy-done.6, bf16[64,2048]{1,0:T(8,128)(2,1)S(1)} %collective-permute-done.refs_1_, bf16[64,2048]{1,0:T(8,128)(2,1)S(1)} %collective-permute-done.1.refs_2_, ...), custom_call_target="tpu_custom_call" | custom-call | flops 4831838208 | bytes 20971520 | tf_op jit(solution)/shard_map/pallas_call | solution.py:110
  54.2 0.0 collective-permute-done.10
  54.2 0.1 add_convert_fusion.3
  54.3 0.6 collective-permute-start.11
  54.9 0.1 add_convert_fusion.1
  54.9 1.3 %collective-permute-start.14 = (bf16[64,2048]{1,0:T(8,128)(2,1)S(1)}, bf16[64,2048]{1,0:T(8,128)(2,1)S(1)}, u32[]{:S(2)}, u32[]{:S(2)}) collective-permute-start(bf16[64,2048]{1,0:T(8,128)(2,1)S(1)} %add_convert_fusion.1), channel_id=1, source_target_pairs={{0,8},{4,12},{8,0},{12,4},{16,24},{20,28},{24,16},{28,20},{1,9},{5... | collective-permute-start | bytes 786440 | tf_op jit(solution)/shard_map/ppermute | solution.py:65
  56.3 0.0 collective-permute-done.9
  56.3 2.0 %collective-permute-done.12 = bf16[64,2048]{1,0:T(8,128)(2,1)S(1)} collective-permute-done((bf16[64,2048]{1,0:T(8,128)(2,1)S(1)}, bf16[64,2048]{1,0:T(8,128)(2,1)S(1)}, u32[]{:S(2)}, u32[]{:S(2)}) %collective-permute-start.12) | collective-permute-done | bytes 262176 | tf_op jit(solution)/shard_map/ppermute | solution.py:65
  58.3 3.9 %collective-permute-done.11 = bf16[64,2048]{1,0:T(8,128)(2,1)S(1)} collective-permute-done((bf16[64,2048]{1,0:T(8,128)(2,1)S(1)}, bf16[64,2048]{1,0:T(8,128)(2,1)S(1)}, u32[]{:S(2)}, u32[]{:S(2)}) %collective-permute-start.11) | collective-permute-done | bytes 262176 | tf_op jit(solution)/shard_map/ppermute | solution.py:65
  62.2 0.2 add_convert_fusion.2
  62.4 0.0 copy-start.7
  62.4 0.8 %copy-done.7 = bf16[128,2048]{1,0:T(8,128)(2,1)} copy-done((bf16[128,2048]{1,0:T(8,128)(2,1)}, bf16[128,2048]{1,0:T(8,128)(2,1)S(1)}, u32[]{:S(2)}) %copy-start.7) | copy-done | bytes 524312
  (19 shorter events, 0.1 us)
Async XLA Ops:
  0.0 28.7 %collective-permute-start.2 = (bf16[2048,768]{1,0:T(8,128)(2,1)}, bf16[2048,768]{1,0:T(8,128)(2,1)}, u32[]{:S(2)}, u32[]{:S(2)}) collective-permute-start(bf16[2048,768]{1,0:T(8,128)(2,1)} %bitcast.28), channel_id=1, source_target_pairs={{0,4},{4,0},{8,12},{12,8},{16,20},{20,16},{24,28},{28,24},{1,5},{5... | collective-permute-start | bytes 9437192 | tf_op jit(solution)/shard_map/ppermute | solution.py:65
  0.5 28.3 %collective-permute-start.3 = (bf16[2048,768]{1,0:T(8,128)(2,1)}, bf16[2048,768]{1,0:T(8,128)(2,1)}, u32[]{:S(2)}, u32[]{:S(2)}) collective-permute-start(bf16[2048,768]{1,0:T(8,128)(2,1)} %bitcast.31), channel_id=1, source_target_pairs={{0,4},{4,0},{8,12},{12,8},{16,20},{20,16},{24,28},{28,24},{1,5},{5... | collective-permute-start | bytes 9437192 | tf_op jit(solution)/shard_map/ppermute | solution.py:65
  0.5 28.2 %collective-permute-start.4 = (bf16[768,2048]{1,0:T(8,128)(2,1)}, bf16[768,2048]{1,0:T(8,128)(2,1)}, u32[]{:S(2)}, u32[]{:S(2)}) collective-permute-start(bf16[768,2048]{1,0:T(8,128)(2,1)} %bitcast.34), channel_id=1, source_target_pairs={{0,4},{4,0},{8,12},{12,8},{16,20},{20,16},{24,28},{28,24},{1,5},{5... | collective-permute-start | bytes 9437192 | tf_op jit(solution)/shard_map/ppermute | solution.py:65
  2.0 15.3 %collective-permute-start.5 = (bf16[64,2048]{1,0:T(8,128)(2,1)S(1)}, bf16[64,2048]{1,0:T(8,128)(2,1)S(1)}, u32[]{:S(2)}, u32[]{:S(2)}) collective-permute-start(bf16[64,2048]{1,0:T(8,128)(2,1)S(1)} %get-tuple-element.22), channel_id=1, source_target_pairs={{0,8},{4,12},{8,0},{12,4},{16,24},{20,28},{24,16},{28,20},{1,9},{5... | collective-permute-start | bytes 786440 | tf_op jit(solution)/shard_map/ppermute | solution.py:65
  4.6 14.1 %collective-permute-start.6 = (bf16[64,2048]{1,0:T(8,128)(2,1)S(1)}, bf16[64,2048]{1,0:T(8,128)(2,1)S(1)}, u32[]{:S(2)}, u32[]{:S(2)}) collective-permute-start(bf16[64,2048]{1,0:T(8,128)(2,1)S(1)} %get-tuple-element.21), channel_id=1, source_target_pairs={{0,16},{4,20},{8,24},{12,28},{16,0},{20,4},{24,8},{28,12},{1,17},{... | collective-permute-start | bytes 786440 | tf_op jit(solution)/shard_map/ppermute | solution.py:65
  17.3 8.6 %collective-permute-start.7 = (bf16[64,2048]{1,0:T(8,128)(2,1)S(1)}, bf16[64,2048]{1,0:T(8,128)(2,1)S(1)}, u32[]{:S(2)}, u32[]{:S(2)}) collective-permute-start(bf16[64,2048]{1,0:T(8,128)(2,1)S(1)} %collective-permute-done.5.refs_0_), channel_id=1, source_target_pairs={{0,16},{4,20},{8,24},{12,28},{16,0},{20,4},{24,8},{28,12},{1,17},{... | collective-permute-start | bytes 786440 | tf_op jit(solution)/shard_map/ppermute | solution.py:65
  18.7 8.5 %collective-permute-start.8 = (bf16[64,2048]{1,0:T(8,128)(2,1)S(1)}, bf16[64,2048]{1,0:T(8,128)(2,1)S(1)}, u32[]{:S(2)}, u32[]{:S(2)}) collective-permute-start(bf16[64,2048]{1,0:T(8,128)(2,1)S(1)} %collective-permute-done.6.refs_1_), channel_id=1, source_target_pairs={{0,8},{4,12},{8,0},{12,4},{16,24},{20,28},{24,16},{28,20},{1,9},{5... | collective-permute-start | bytes 786440 | tf_op jit(solution)/shard_map/ppermute | solution.py:65
  25.9 19.0 %collective-permute-start = (bf16[64,2048]{1,0:T(8,128)(2,1)S(1)}, bf16[64,2048]{1,0:T(8,128)(2,1)S(1)}, u32[]{:S(2)}, u32[]{:S(2)}) collective-permute-start(bf16[64,2048]{1,0:T(8,128)(2,1)S(1)} %get-tuple-element.21), channel_id=1, source_target_pairs={{0,8},{4,12},{8,0},{12,4},{16,24},{20,28},{24,16},{28,20},{1,9},{5... | collective-permute-start | bytes 786440 | tf_op jit(solution)/shard_map/ppermute | solution.py:65
  27.2 19.2 %collective-permute-start.1 = (bf16[64,2048]{1,0:T(8,128)(2,1)S(1)}, bf16[64,2048]{1,0:T(8,128)(2,1)S(1)}, u32[]{:S(2)}, u32[]{:S(2)}) collective-permute-start(bf16[64,2048]{1,0:T(8,128)(2,1)S(1)} %get-tuple-element.22), channel_id=1, source_target_pairs={{0,16},{4,20},{8,24},{12,28},{16,0},{20,4},{24,8},{28,12},{1,17},{... | collective-permute-start | bytes 786440 | tf_op jit(solution)/shard_map/ppermute | solution.py:65
  28.7 1.9 %copy-start = (bf16[1,2048,768]{2,1,0:T(8,128)(2,1)S(1)}, bf16[1,2048,768]{2,1,0:T(8,128)(2,1)}, u32[]{:S(2)}) copy-start(bf16[1,2048,768]{2,1,0:T(8,128)(2,1)} %param.9) | copy-start | bytes 9437188
  30.6 1.9 %copy-start.2 = (bf16[1,2048,768]{2,1,0:T(8,128)(2,1)S(1)}, bf16[1,2048,768]{2,1,0:T(8,128)(2,1)}, u32[]{:S(2)}) copy-start(bf16[1,2048,768]{2,1,0:T(8,128)(2,1)} %param.10) | copy-start | bytes 9437188
  32.5 1.9 %copy-start.4 = (bf16[1,768,2048]{2,1,0:T(8,128)(2,1)S(1)}, bf16[1,768,2048]{2,1,0:T(8,128)(2,1)}, u32[]{:S(2)}) copy-start(bf16[1,768,2048]{2,1,0:T(8,128)(2,1)} %param.11) | copy-start | bytes 9437188
  34.4 12.0 %copy-start.1 = (bf16[1,2048,768]{2,1,0:T(8,128)(2,1)S(1)}, bf16[1,2048,768]{2,1,0:T(8,128)(2,1)}, u32[]{:S(2)}) copy-start(bf16[1,2048,768]{2,1,0:T(8,128)(2,1)} %param.9) | copy-start | bytes 9437188
  34.4 12.0 %copy-start.3 = (bf16[1,2048,768]{2,1,0:T(8,128)(2,1)S(1)}, bf16[1,2048,768]{2,1,0:T(8,128)(2,1)}, u32[]{:S(2)}) copy-start(bf16[1,2048,768]{2,1,0:T(8,128)(2,1)} %param.10) | copy-start | bytes 9437188
  34.4 12.0 %copy-start.5 = (bf16[1,768,2048]{2,1,0:T(8,128)(2,1)S(1)}, bf16[1,768,2048]{2,1,0:T(8,128)(2,1)}, u32[]{:S(2)}) copy-start(bf16[1,768,2048]{2,1,0:T(8,128)(2,1)} %param.11) | copy-start | bytes 9437188
  34.4 12.0 %copy-start.6 = (bf16[128,2048]{1,0:T(8,128)(2,1)S(1)}, bf16[128,2048]{1,0:T(8,128)(2,1)}, u32[]{:S(2)}) copy-start(bf16[128,2048]{1,0:T(8,128)(2,1)} %refs_0_.1) | copy-start | bytes 1572868
  42.3 12.0 %collective-permute-start.10 = (bf16[64,2048]{1,0:T(8,128)(2,1)S(1)}, bf16[64,2048]{1,0:T(8,128)(2,1)S(1)}, u32[]{:S(2)}, u32[]{:S(2)}) collective-permute-start(bf16[64,2048]{1,0:T(8,128)(2,1)S(1)} %get-tuple-element.15), channel_id=1, source_target_pairs={{0,8},{4,12},{8,0},{12,4},{16,24},{20,28},{24,16},{28,20},{1,9},{5... | collective-permute-start | bytes 786440 | tf_op jit(solution)/shard_map/ppermute | solution.py:65
  42.9 13.4 %collective-permute-start.9 = (bf16[64,2048]{1,0:T(8,128)(2,1)S(1)}, bf16[64,2048]{1,0:T(8,128)(2,1)S(1)}, u32[]{:S(2)}, u32[]{:S(2)}) collective-permute-start(bf16[64,2048]{1,0:T(8,128)(2,1)S(1)} %get-tuple-element.13), channel_id=1, source_target_pairs={{0,8},{4,12},{8,0},{12,4},{16,24},{20,28},{24,16},{28,20},{1,9},{5... | collective-permute-start | bytes 786440 | tf_op jit(solution)/shard_map/ppermute | solution.py:65
  44.3 10.5 %collective-permute-start.13 = (bf16[64,2048]{1,0:T(8,128)(2,1)S(1)}, bf16[64,2048]{1,0:T(8,128)(2,1)S(1)}, u32[]{:S(2)}, u32[]{:S(2)}) collective-permute-start(bf16[64,2048]{1,0:T(8,128)(2,1)S(1)} %get-tuple-element.18), channel_id=1, source_target_pairs={{0,16},{4,20},{8,24},{12,28},{16,0},{20,4},{24,8},{28,12},{1,17},{... | collective-permute-start | bytes 786440 | tf_op jit(solution)/shard_map/ppermute | solution.py:65
  44.9 13.4 %collective-permute-start.12 = (bf16[64,2048]{1,0:T(8,128)(2,1)S(1)}, bf16[64,2048]{1,0:T(8,128)(2,1)S(1)}, u32[]{:S(2)}, u32[]{:S(2)}) collective-permute-start(bf16[64,2048]{1,0:T(8,128)(2,1)S(1)} %get-tuple-element.16), channel_id=1, source_target_pairs={{0,16},{4,20},{8,24},{12,28},{16,0},{20,4},{24,8},{28,12},{1,17},{... | collective-permute-start | bytes 786440 | tf_op jit(solution)/shard_map/ppermute | solution.py:65
  54.3 7.9 %collective-permute-start.11 = (bf16[64,2048]{1,0:T(8,128)(2,1)S(1)}, bf16[64,2048]{1,0:T(8,128)(2,1)S(1)}, u32[]{:S(2)}, u32[]{:S(2)}) collective-permute-start(bf16[64,2048]{1,0:T(8,128)(2,1)S(1)} %add_convert_fusion.3), channel_id=1, source_target_pairs={{0,16},{4,20},{8,24},{12,28},{16,0},{20,4},{24,8},{28,12},{1,17},{... | collective-permute-start | bytes 786440 | tf_op jit(solution)/shard_map/ppermute | solution.py:65
  54.9 7.2 %collective-permute-start.14 = (bf16[64,2048]{1,0:T(8,128)(2,1)S(1)}, bf16[64,2048]{1,0:T(8,128)(2,1)S(1)}, u32[]{:S(2)}, u32[]{:S(2)}) collective-permute-start(bf16[64,2048]{1,0:T(8,128)(2,1)S(1)} %add_convert_fusion.1), channel_id=1, source_target_pairs={{0,8},{4,12},{8,0},{12,4},{16,24},{20,28},{24,16},{28,20},{1,9},{5... | collective-permute-start | bytes 786440 | tf_op jit(solution)/shard_map/ppermute | solution.py:65
  62.4 0.8 %copy-start.7 = (bf16[128,2048]{1,0:T(8,128)(2,1)}, bf16[128,2048]{1,0:T(8,128)(2,1)S(1)}, u32[]{:S(2)}) copy-start(bf16[128,2048]{1,0:T(8,128)(2,1)S(1)} %get-tuple-element.71) | copy-start | bytes 1572868

commit v2 on v1

v2 whole, which is shorter than its diff:
```python
import functools

import jax
import jax.numpy as jnp
from jax import lax
from jax.experimental import pallas as pl
from jax.experimental.pallas import tpu as pltpu
from jax.sharding import PartitionSpec as P

AXIS = "expert"
CORE, XBIT, YBIT = 1, 2, 4


def slot_table(routed, capacity):
    counted = routed.astype(jnp.int32)
    position = jnp.cumsum(counted, axis=1) - 1
    slot_ids = jnp.arange(capacity, dtype=jnp.int32)
    chosen = routed[:, None, :] & (position[:, None, :] == slot_ids[None, :, None])
    row_ids = jnp.arange(routed.shape[1], dtype=jnp.int32)
    slot_index = jnp.sum(jnp.where(chosen, row_ids[None, None, :], 0), axis=2)
    filled = jnp.any(chosen, axis=2)
    return (slot_index, filled)


def expert_ffn(slot_block, w_gate, w_up, w_down):
    width = slot_block.shape[-1]
    flat_rows = slot_block.reshape(-1, width)
    gate_act = jnp.dot(flat_rows, w_gate[0], preferred_element_type=jnp.float32)
    up_act = jnp.dot(flat_rows, w_up[0], preferred_element_type=jnp.float32)
    hidden = (jax.nn.silu(gate_act) * up_act).astype(jnp.bfloat16)
    expert_out = jnp.dot(hidden, w_down[0], preferred_element_type=jnp.float32)
    return expert_out.reshape(slot_block.shape[:-1] + (w_down.shape[2],))


def swap_all(rows):
    return lax.all_to_all(rows, AXIS, split_axis=0, concat_axis=0, tiled=True)


def route_table(expert_ids, gate_weights, experts):
    labels = jnp.arange(experts, dtype=jnp.int32)
    matched = expert_ids[:, :, None] == labels[None, None, :]
    weights = gate_weights.astype(jnp.float32)[:, :, None]
    return jnp.sum(jnp.where(matched, weights, jnp.float32(0.0)), axis=1)


def any_slice(tokens, expert_ids, gate_weights, w_gate, w_up, w_down):
    tok_dev, choose_k = expert_ids.shape
    width = tokens.shape[1]
    experts = w_gate.shape[0] * lax.axis_size(AXIS)
    capacity = min(tok_dev, 3 * tok_dev * choose_k // (2 * experts))
    weight = route_table(expert_ids, gate_weights, experts)
    home_index, home_filled = slot_table(weight.T != 0.0, capacity)
    arrived = swap_all(tokens[home_index])
    returned_rows = swap_all(expert_ffn(arrived, w_gate, w_up, w_down))
    owners = jnp.arange(experts, dtype=jnp.int32)[:, None]
    factor = jnp.where(home_filled, weight.T[owners, home_index], jnp.float32(0.0))
    combined = jnp.zeros((tok_dev, width), jnp.float32)
    combined = combined.at[home_index.reshape(-1)].add(
        (factor[:, :, None] * returned_rows).reshape(-1, width)
    )
    return combined.astype(jnp.bfloat16)


def hop(block, bits):
    return lax.ppermute(block, AXIS, [(i, i ^ bits) for i in range(lax.axis_size(AXIS))])


def in_vmem(array):
    return pltpu.with_memory_space_constraint(array, pltpu.VMEM)


def vmem_out(shape):
    return pltpu.VMEM(shape, jnp.bfloat16)


MIB = 1 << 20
VMEM_SPEC = pl.BlockSpec(memory_space=pltpu.VMEM)
ANY_SPEC = pl.BlockSpec(memory_space=pl.ANY)


def label_body(tokens_ref, ids_ref, gates_ref, *refs):
    *out_refs, ids_buf, gates_buf, sem = refs
    width = tokens_ref.shape[1]
    rows, tail = ids_ref.shape[1], out_refs[0].shape[1] - width
    pairs = [(ids_ref, ids_buf), (gates_ref, gates_buf)]
    at = 0
    for out_ref in out_refs:
        part = out_ref.shape[0]
        pairs.append((tokens_ref.at[pl.ds(at, part)], out_ref.at[:, pl.ds(0, width)]))
        at += part
    copies = [pltpu.make_async_copy(src, dst, sem.at[k]) for k, (src, dst) in enumerate(pairs)]
    for copy in copies:
        copy.start()
    for copy in copies[:2]:
        copy.wait()
    me = lax.axis_index(AXIS)
    column = lax.broadcasted_iota(jnp.int32, (tail, rows), 0)
    gates = gates_buf[...].astype(jnp.float32)
    route = jnp.zeros((tail, rows), jnp.float32)
    for k in range(ids_ref.shape[0]):
        route += jnp.where(column == ids_buf[k : k + 1, :] ^ me, gates[k : k + 1, :], 0.0)
    route = route.T.astype(jnp.bfloat16)
    at = 0
    for out_ref in out_refs:
        part = out_ref.shape[0]
        out_ref[:, width:] = route[at : at + part]
        at += part
    for copy in copies[2:]:
        copy.wait()


def label(tokens, expert_ids, gate_weights, tail, parts):
    rows, width = tokens.shape
    arrays = (tokens, expert_ids.T, gate_weights.T)
    return pl.pallas_call(
        label_body,
        out_shape=[vmem_out((rows // parts, width + tail))] * parts,
        in_specs=[ANY_SPEC] * 3,
        out_specs=[VMEM_SPEC] * parts,
        scratch_shapes=[pltpu.VMEM(a.shape, a.dtype) for a in arrays[1:]]
        + [pltpu.SemaphoreType.DMA((2 + parts,))],
        compiler_params=pltpu.CompilerParams(vmem_limit_bytes=8 * MIB),
    )(*[pltpu.with_memory_space_constraint(a, pltpu.HBM) for a in arrays])


def after_body(n, *refs):
    for src, dst in zip(refs[:n], refs[-n:]):
        dst[...] = src[...]


def after(blocks, arrived):
    n = len(blocks)
    return pl.pallas_call(
        functools.partial(after_body, n),
        out_shape=[vmem_out(b.shape) for b in blocks],
        in_specs=[VMEM_SPEC] * n + [ANY_SPEC] * len(arrived),
        out_specs=[VMEM_SPEC] * n,
        compiler_params=pltpu.CompilerParams(vmem_limit_bytes=8 * MIB),
    )(*[in_vmem(b) for b in blocks], *[in_vmem(a) for a in arrived])


def finish_body(n, *refs):
    terms, out_ref, (buf, sem) = refs[:-3], refs[-3], refs[-2:]
    at, copies = 0, []
    for k in range(len(terms) // n):
        total = sum(t[...].astype(jnp.float32) for t in terms[n * k : n * k + n])
        part = total.shape[0]
        buf[at : at + part] = total.astype(jnp.bfloat16)
        rows = pl.ds(at, part)
        copies.append(pltpu.make_async_copy(buf.at[rows], out_ref.at[rows], sem.at[k]))
        copies[-1].start()
        at += part
    for copy in copies:
        copy.wait()


def finish(sums):
    n, blocks = len(sums[0]), [in_vmem(block) for terms in sums for block in terms]
    rows, width = sum(terms[0].shape[0] for terms in sums), blocks[0].shape[1]
    return pl.pallas_call(
        functools.partial(finish_body, n),
        out_shape=jax.ShapeDtypeStruct((rows, width), jnp.bfloat16),
        in_specs=[VMEM_SPEC] * len(blocks),
        out_specs=ANY_SPEC,
        scratch_shapes=[
            pltpu.VMEM((rows, width), jnp.bfloat16),
            pltpu.SemaphoreType.DMA((len(sums),)),
        ],
        compiler_params=pltpu.CompilerParams(vmem_limit_bytes=8 * MIB),
    )(*blocks)


def fetch_body(*refs):
    n = len(refs) // 2
    sem = refs[-1]
    copies = [pltpu.make_async_copy(refs[k], refs[n + k], sem.at[k]) for k in range(n)]
    for copy in copies:
        copy.start()
    for copy in copies:
        copy.wait()


def fetch(arrays):
    n = len(arrays)
    return pl.pallas_call(
        fetch_body,
        out_shape=[vmem_out(a.shape) for a in arrays],
        in_specs=[ANY_SPEC] * n,
        out_specs=[VMEM_SPEC] * n,
        scratch_shapes=[pltpu.SemaphoreType.DMA((n,))],
        compiler_params=pltpu.CompilerParams(vmem_limit_bytes=8 * MIB),
        cost_estimate=pl.CostEstimate(
            flops=0, bytes_accessed=4 * sum(a.size for a in arrays), transcendentals=0
        ),
    )(*[pltpu.with_memory_space_constraint(a, pltpu.HBM) for a in arrays])


def ffn_body(hops, *refs):
    n = len(hops)
    x_refs, weights, o_refs, (x_buf, h_buf) = refs[:n], refs[n : n + 6], refs[n + 6 : -2], refs[-2:]
    width, hidden = x_buf.shape[1], h_buf.shape[1] // 2
    at = 0
    columns = ([], [])
    for x_ref, bits in zip(x_refs, hops):
        x_buf[at : at + x_ref.shape[0]] = x_ref[:, :width]
        at += x_ref.shape[0]
        for e in range(2):
            lane = width + (bits ^ (e * CORE))
            columns[e].append(x_ref[:, lane : lane + 1].astype(jnp.float32))
    columns = [jnp.concatenate(parts) for parts in columns]
    for e in range(2):
        w_gate, w_up = weights[3 * e], weights[3 * e + 1]
        for f in range(0, hidden, 256):
            gate = jnp.dot(x_buf[...], w_gate[:, f : f + 256], preferred_element_type=jnp.float32)
            up = jnp.dot(x_buf[...], w_up[:, f : f + 256], preferred_element_type=jnp.float32)
            act = (gate / (1.0 + jnp.exp(-gate)) * up).astype(jnp.bfloat16)
            h_buf[:, e * hidden + f : e * hidden + f + 256] = act
    for c in range(0, width, 512):
        out = None
        for e in range(2):
            act = h_buf[:, e * hidden : (e + 1) * hidden]
            part = jnp.dot(act, weights[3 * e + 2][:, c : c + 512], preferred_element_type=jnp.float32)
            part = columns[e] * part
            out = part if out is None else out + part
        out = out.astype(jnp.bfloat16)
        at = 0
        for o_ref in o_refs:
            o_ref[:, c : c + 512] = out[at : at + o_ref.shape[0]]
            at += o_ref.shape[0]


def ffn(blocks, hops, *, width, weights):
    pieces = [block.shape[0] for block in blocks]
    rows, n = sum(pieces), len(blocks)
    hidden = weights[0].shape[1]
    moved = sum(w.size * 2 for w in weights) + 4 * rows * width
    return pl.pallas_call(
        functools.partial(ffn_body, hops),
        out_shape=[vmem_out((p, width)) for p in pieces],
        in_specs=[VMEM_SPEC] * (n + 6),
        out_specs=[VMEM_SPEC] * n,
        scratch_shapes=[
            pltpu.VMEM((rows, width), jnp.bfloat16),
            pltpu.VMEM((rows, 2 * hidden), jnp.bfloat16),
        ],
        compiler_params=pltpu.CompilerParams(vmem_limit_bytes=16 * MIB),
        cost_estimate=pl.CostEstimate(
            flops=12 * rows * width * hidden, bytes_accessed=moved, transcendentals=2 * rows * hidden
        ),
    )(*[in_vmem(block) for block in blocks], *[in_vmem(w) for w in weights])


def two_by_two(tokens, expert_ids, gate_weights, w_gate, w_up, w_down):
    tok_dev, width = tokens.shape
    half = tok_dev // 2
    top, low = label(tokens, expert_ids, gate_weights, 128, 2)

    x_top, y_low = hop(top, XBIT), hop(low, YBIT)
    own = (w_gate[0], w_up[0], w_down[0])
    swapped = [hop(w, CORE) for w in own]
    fetched = fetch(own)
    weights = [*fetched, *swapped]
    (x_on,), (y_on,) = after([x_top], fetched[:1]), after([y_low], fetched[:1])
    d_top, d_low = hop(x_on, YBIT), hop(y_on, XBIT)
    low, top = after([low, top], [x_on, y_on, *swapped[:2]])
    x_low, y_top = hop(low, XBIT), hop(top, YBIT)

    run = functools.partial(ffn, width=width, weights=weights)
    ox_top, oy_low = run([x_on, y_on], [XBIT, YBIT])
    d_top, d_low = after([d_top, d_low], [ox_top])
    od_top, od_low = run([d_top, d_low], [XBIT | YBIT] * 2)
    e_top, e_low = hop(od_top, XBIT), hop(od_low, YBIT)
    x_low, y_top = after([x_low, y_top], [od_top])
    oy_top, ox_low = run([y_top, x_low], [YBIT, XBIT])
    ox_top, oy_low = after([ox_top, oy_low], [oy_top])
    fx_top, fy_low = hop(ox_top, XBIT), hop(oy_low, YBIT)
    o_top, o_low = run([top, low], [0, 0])
    f32 = lambda a: a.astype(jnp.float32)
    my_top = hop((f32(oy_top) + f32(e_top)).astype(jnp.bfloat16), YBIT)
    mx_low = hop((f32(ox_low) + f32(e_low)).astype(jnp.bfloat16), XBIT)
    return finish([[o_top, fx_top, my_top], [o_low, fy_low, mx_low]])


def solution(mesh):
    return jax.shard_map(
        two_by_two if mesh.shape[AXIS] == 8 else any_slice,
        mesh=mesh,
        in_specs=(
            P(("dp", AXIS), None),
            P(("dp", AXIS), None),
            P(("dp", AXIS), None),
            P(AXIS, None, None),
            P(AXIS, None, None),
            P(AXIS, None, None),
        ),
        out_specs=P(("dp", AXIS), None),
        check_vma=False,
    )
```

time: 63.5 us -> 46.6 us (0.73)
  blocking collectives: 9.58 us -> 0 us
  local copies, waits for them, and re-layouts: 7.94 us -> 0 us
  other arithmetic: 1.88 us -> 0.13 us
  Pallas kernels: 15.6 us -> 16.6 us
  waiting for transfers between devices: 11.2 us -> 12.2 us
    all_gather x1 -> x0, blocking collectives: 9.58 us -> none  [two_by_two(): routes = lax.all_gather(route, AXIS, axis=0)]
    unnamed x16 -> x0, local copies, waits for them, and re-layouts: 6.47 us -> none
    slice x2 -> x0, local copies, waits for them, and re-layouts: 1.15 us -> none  [the longest x1 1.07 us: two_by_two(): top, low = (tokens[:half], tokens[half:])]
    pallas_call x2 -> x13, Pallas kernels: 15.6 us -> 16.6 us  [the longest x4 10.6 us: ffn(): pl.pallas_call(functools.partial(ffn_body, hops), out_shape=[vmem_out((p,...]
    ppermute x15, waiting for transfers between devices: 11.2 us -> 12.2 us  [hop(): lax.ppermute(block, AXIS, [(i, i ^ bits) for i in range(lax.axis_size(AXI...]
    reduce_sum x1 -> x0, other arithmetic: 0.69 us -> none  [route_table(): return jnp.sum(jnp.where(matched, weights, jnp.float32(0.0)), axis=1)]
    convert_element_type x1 -> x0, other arithmetic: 0.68 us -> none  [route_table(): weights = gate_weights.astype(jnp.float32)[:, :, None]]
    ppermute x15, starting transfers between devices: 16.8 us -> 17.4 us  [hop(): lax.ppermute(block, AXIS, [(i, i ^ bits) for i in range(lax.axis_size(AXI...]
  transfers between devices with their start and end apart: 15 -> 15, of which waited for: 3 -> 7; matrix products, arithmetic and copies ran while one was open for 5% -> 0% of each run, Pallas kernels for 25% -> 34%
where the time goes in v2:
time: 46.6 us; the launch traced here: 46.5 us
  starting transfers between devices  17.4 us (37%)
  Pallas kernels  16.6 us (36%)
  waiting for transfers between devices  12.2 us (26%)
    ppermute x15, starting transfers between devices, hop(): lax.ppermute(block, AXIS, [(i, i ^ bits) for i in range(lax.axis_size(AXI...  17.4 us
    ppermute x15, waiting for transfers between devices, hop(): lax.ppermute(block, AXIS, [(i, i ^ bits) for i in range(lax.axis_size(AXI...  12.2 us
    pallas_call x4, Pallas kernels, ffn(): pl.pallas_call(functools.partial(ffn_body, hops), out_shape=[vmem_out((p,...  10.6 us
    pallas_call x1, Pallas kernels, fetch(): pl.pallas_call(fetch_body, out_shape=[vmem_out(a.shape) for a in arrays],...  3.78 us
    pallas_call x1, Pallas kernels, label(): pl.pallas_call(label_body, out_shape=[vmem_out((rows // parts, width + ta...  1.09 us
  transfers between devices with their start and end apart: 15, of which 7 were waited for; matrix products, arithmetic and copies ran while one was open for 0% of the time, Pallas kernels for 34%

profile of v2, /device:TPU:0, one launch (start us, length us, event | category | flops | bytes accessed | tf_op | source)
XLA Modules:
  0.0 46.5 jit_solution(13581632054226973891)
XLA Ops:
  0.0 0.5 collective-permute-start.2
  0.5 0.1 collective-permute-start.3
  0.5 0.5 collective-permute-start.4
  1.0 1.1 %shard_map.64 = (bf16[64,2176]{1,0:T(8,128)(2,1)S(1)}, bf16[64,2176]{1,0:T(8,128)(2,1)S(1)}) custom-call(bf16[128,2048]{1,0:T(8,128)(2,1)} %tokens_ref.1, s32[4,128]{1,0:T(4,128)} %bitcast.11, bf16[4,128]{1,0:T(4,128)(2,1)} %bitcast.12), custom_call_target="tpu_custom_call" | custom-call | tf_op jit(solution)/shard_map/pallas_call | solution.py:115
  2.1 2.6 %collective-permute-start = (bf16[64,2176]{1,0:T(8,128)(2,1)S(1)}, bf16[64,2176]{1,0:T(8,128)(2,1)S(1)}, u32[]{:S(2)}, u32[]{:S(2)}) collective-permute-start(bf16[64,2176]{1,0:T(8,128)(2,1)S(1)} %get-tuple-element.27.refs_1_), channel_id=1, source_target_pairs={{0,8},{4,12},{8,0},{12,4},{16,24},{20,28},{24,16},{28,20},{1,9},{5... | collective-permute-start | bytes 835592 | tf_op jit(solution)/shard_map/ppermute | solution.py:65
  4.6 1.5 %collective-permute-start.1 = (bf16[64,2176]{1,0:T(8,128)(2,1)S(1)}, bf16[64,2176]{1,0:T(8,128)(2,1)S(1)}, u32[]{:S(2)}, u32[]{:S(2)}) collective-permute-start(bf16[64,2176]{1,0:T(8,128)(2,1)S(1)} %get-tuple-element.26.refs_0_), channel_id=1, source_target_pairs={{0,16},{4,20},{8,24},{12,28},{16,0},{20,4},{24,8},{28,12},{1,17},{... | collective-permute-start | bytes 835592 | tf_op jit(solution)/shard_map/ppermute | solution.py:65
  6.1 3.8 %shard_map.65 = (bf16[2048,768]{1,0:T(8,128)(2,1)S(1)}, bf16[2048,768]{1,0:T(8,128)(2,1)S(1)}, bf16[768,2048]{1,0:T(8,128)(2,1)S(1)}) custom-call(bf16[2048,768]{1,0:T(8,128)(2,1)} %bitcast.6, bf16[2048,768]{1,0:T(8,128)(2,1)} %bitcast.8, bf16[768,2048]{1,0:T(8,128)(2,1)} %bitcast.10), custom_call_target="tpu_custom_call" | custom-call | bytes 18874368 | tf_op jit(solution)/shard_map/pallas_call | solution.py:185
  9.9 2.0 %collective-permute-done.refs_0_ = bf16[64,2176]{1,0:T(8,128)(2,1)S(1)} collective-permute-done((bf16[64,2176]{1,0:T(8,128)(2,1)S(1)}, bf16[64,2176]{1,0:T(8,128)(2,1)S(1)}, u32[]{:S(2)}, u32[]{:S(2)}) %collective-permute-start) | collective-permute-done | bytes 278560 | tf_op jit(solution)/shard_map/ppermute | solution.py:65
  12.0 1.8 %collective-permute-start.7 = (bf16[64,2176]{1,0:T(8,128)(2,1)S(1)}, bf16[64,2176]{1,0:T(8,128)(2,1)S(1)}, u32[]{:S(2)}, u32[]{:S(2)}) collective-permute-start(bf16[64,2176]{1,0:T(8,128)(2,1)S(1)} %shard_map.66.refs_2_.refs_0_), channel_id=1, source_target_pairs={{0,16},{4,20},{8,24},{12,28},{16,0},{20,4},{24,8},{28,12},{1,17},{... | collective-permute-start | bytes 835592 | tf_op jit(solution)/shard_map/ppermute | solution.py:65
  13.8 0.0 collective-permute-done.1.refs_0_
  13.8 1.6 %collective-permute-start.8 = (bf16[64,2176]{1,0:T(8,128)(2,1)S(1)}, bf16[64,2176]{1,0:T(8,128)(2,1)S(1)}, u32[]{:S(2)}, u32[]{:S(2)}) collective-permute-start(bf16[64,2176]{1,0:T(8,128)(2,1)S(1)} %shard_map.67.refs_3_.refs_1_), channel_id=1, source_target_pairs={{0,8},{4,12},{8,0},{12,4},{16,24},{20,28},{24,16},{28,20},{1,9},{5... | collective-permute-start | bytes 835592 | tf_op jit(solution)/shard_map/ppermute | solution.py:65
  15.4 0.0 collective-permute-done.2.refs_4_.refs_5_
  15.4 0.0 collective-permute-done.3.refs_5_.refs_6_
  15.4 0.6 %collective-permute-start.5 = (bf16[64,2176]{1,0:T(8,128)(2,1)S(1)}, bf16[64,2176]{1,0:T(8,128)(2,1)S(1)}, u32[]{:S(2)}, u32[]{:S(2)}) collective-permute-start(bf16[64,2176]{1,0:T(8,128)(2,1)S(1)} %get-tuple-element.30.refs_1_), channel_id=1, source_target_pairs={{0,8},{4,12},{8,0},{12,4},{16,24},{20,28},{24,16},{28,20},{1,9},{5... | collective-permute-start | bytes 835592 | tf_op jit(solution)/shard_map/ppermute | solution.py:65
  16.0 1.1 %collective-permute-start.6 = (bf16[64,2176]{1,0:T(8,128)(2,1)S(1)}, bf16[64,2176]{1,0:T(8,128)(2,1)S(1)}, u32[]{:S(2)}, u32[]{:S(2)}) collective-permute-start(bf16[64,2176]{1,0:T(8,128)(2,1)S(1)} %get-tuple-element.29.refs_0_), channel_id=1, source_target_pairs={{0,16},{4,20},{8,24},{12,28},{16,0},{20,4},{24,8},{28,12},{1,17},{... | collective-permute-start | bytes 835592 | tf_op jit(solution)/shard_map/ppermute | solution.py:65
  17.2 0.0 collective-permute-done.4.refs_7_
  17.2 2.7 %shard_map.70 = (bf16[64,2048]{1,0:T(8,128)(2,1)S(1)}, bf16[64,2048]{1,0:T(8,128)(2,1)S(1)}) custom-call(bf16[64,2176]{1,0:T(8,128)(2,1)S(1)} %shard_map.66.refs_2_.refs_0_, bf16[64,2176]{1,0:T(8,128)(2,1)S(1)} %shard_map.67.refs_3_.refs_1_, bf16[2048,768]{1,0:T(8,128)(2,1)S(1)} %get-tuple-element.28.refs_1_.refs_2_, ...), custom_call_target="tpu_custom_call" | custom-call | flops 2415919104 | bytes 19922944 | tf_op jit(solution)/shard_map/pallas_call | solution.py:237
  19.8 1.7 %collective-permute-done.7.refs_0_ = bf16[64,2176]{1,0:T(8,128)(2,1)S(1)} collective-permute-done((bf16[64,2176]{1,0:T(8,128)(2,1)S(1)}, bf16[64,2176]{1,0:T(8,128)(2,1)S(1)}, u32[]{:S(2)}, u32[]{:S(2)}) %collective-permute-start.7) | collective-permute-done | bytes 278560 | tf_op jit(solution)/shard_map/ppermute | solution.py:65
  21.6 1.9 %collective-permute-done.8.refs_1_ = bf16[64,2176]{1,0:T(8,128)(2,1)S(1)} collective-permute-done((bf16[64,2176]{1,0:T(8,128)(2,1)S(1)}, bf16[64,2176]{1,0:T(8,128)(2,1)S(1)}, u32[]{:S(2)}, u32[]{:S(2)}) %collective-permute-start.8) | collective-permute-done | bytes 278560 | tf_op jit(solution)/shard_map/ppermute | solution.py:65
  23.5 2.7 %shard_map.72 = (bf16[64,2048]{1,0:T(8,128)(2,1)S(1)}, bf16[64,2048]{1,0:T(8,128)(2,1)S(1)}) custom-call(bf16[64,2176]{1,0:T(8,128)(2,1)S(1)} %get-tuple-element.36.refs_0_, bf16[64,2176]{1,0:T(8,128)(2,1)S(1)} %get-tuple-element.37.refs_1_, bf16[2048,768]{1,0:T(8,128)(2,1)S(1)} %get-tuple-element.28.refs_1_.refs_2_, ...), custom_call_target="tpu_custom_call" | custom-call | flops 2415919104 | bytes 19922944 | tf_op jit(solution)/shard_map/pallas_call | solution.py:237
  26.2 1.6 %collective-permute-start.10 = (bf16[64,2048]{1,0:T(8,128)(2,1)S(1)}, bf16[64,2048]{1,0:T(8,128)(2,1)S(1)}, u32[]{:S(2)}, u32[]{:S(2)}) collective-permute-start(bf16[64,2048]{1,0:T(8,128)(2,1)S(1)} %get-tuple-element.38.refs_2_), channel_id=1, source_target_pairs={{0,8},{4,12},{8,0},{12,4},{16,24},{20,28},{24,16},{28,20},{1,9},{5... | collective-permute-start | bytes 786440 | tf_op jit(solution)/shard_map/ppermute | solution.py:65
  27.8 0.5 %collective-permute-start.13 = (bf16[64,2048]{1,0:T(8,128)(2,1)S(1)}, bf16[64,2048]{1,0:T(8,128)(2,1)S(1)}, u32[]{:S(2)}, u32[]{:S(2)}) collective-permute-start(bf16[64,2048]{1,0:T(8,128)(2,1)S(1)} %get-tuple-element.46), channel_id=1, source_target_pairs={{0,16},{4,20},{8,24},{12,28},{16,0},{20,4},{24,8},{28,12},{1,17},{... | collective-permute-start | bytes 786440 | tf_op jit(solution)/shard_map/ppermute | solution.py:65
  28.3 1.2 %collective-permute-done.5.refs_0_ = bf16[64,2176]{1,0:T(8,128)(2,1)S(1)} collective-permute-done((bf16[64,2176]{1,0:T(8,128)(2,1)S(1)}, bf16[64,2176]{1,0:T(8,128)(2,1)S(1)}, u32[]{:S(2)}, u32[]{:S(2)}) %collective-permute-start.5) | collective-permute-done | bytes 278560 | tf_op jit(solution)/shard_map/ppermute | solution.py:65
  29.5 0.0 collective-permute-done.6.refs_1_
  29.5 2.7 %shard_map.74 = (bf16[64,2048]{1,0:T(8,128)(2,1)S(1)}, bf16[64,2048]{1,0:T(8,128)(2,1)S(1)}) custom-call(bf16[64,2176]{1,0:T(8,128)(2,1)S(1)} %get-tuple-element.39.refs_0_, bf16[64,2176]{1,0:T(8,128)(2,1)S(1)} %get-tuple-element.40.refs_1_, bf16[2048,768]{1,0:T(8,128)(2,1)S(1)} %get-tuple-element.28.refs_1_.refs_2_, ...), custom_call_target="tpu_custom_call" | custom-call | flops 2415919104 | bytes 19922944 | tf_op jit(solution)/shard_map/pallas_call | solution.py:237
  32.2 1.6 %collective-permute-start.9 = (bf16[64,2048]{1,0:T(8,128)(2,1)S(1)}, bf16[64,2048]{1,0:T(8,128)(2,1)S(1)}, u32[]{:S(2)}, u32[]{:S(2)}) collective-permute-start(bf16[64,2048]{1,0:T(8,128)(2,1)S(1)} %get-tuple-element.42), channel_id=1, source_target_pairs={{0,8},{4,12},{8,0},{12,4},{16,24},{20,28},{24,16},{28,20},{1,9},{5... | collective-permute-start | bytes 786440 | tf_op jit(solution)/shard_map/ppermute | solution.py:65
  33.8 1.3 %collective-permute-done.10 = bf16[64,2048]{1,0:T(8,128)(2,1)S(1)} collective-permute-done((bf16[64,2048]{1,0:T(8,128)(2,1)S(1)}, bf16[64,2048]{1,0:T(8,128)(2,1)S(1)}, u32[]{:S(2)}, u32[]{:S(2)}) %collective-permute-start.10) | collective-permute-done | bytes 262176 | tf_op jit(solution)/shard_map/ppermute | solution.py:65
  35.1 0.1 add_convert_fusion.1
  35.2 1.2 %collective-permute-start.11 = (bf16[64,2048]{1,0:T(8,128)(2,1)S(1)}, bf16[64,2048]{1,0:T(8,128)(2,1)S(1)}, u32[]{:S(2)}, u32[]{:S(2)}) collective-permute-start(bf16[64,2048]{1,0:T(8,128)(2,1)S(1)} %add_convert_fusion.1), channel_id=1, source_target_pairs={{0,16},{4,20},{8,24},{12,28},{16,0},{20,4},{24,8},{28,12},{1,17},{... | collective-permute-start | bytes 786440 | tf_op jit(solution)/shard_map/ppermute | solution.py:65
  36.4 0.9 %collective-permute-start.12 = (bf16[64,2048]{1,0:T(8,128)(2,1)S(1)}, bf16[64,2048]{1,0:T(8,128)(2,1)S(1)}, u32[]{:S(2)}, u32[]{:S(2)}) collective-permute-start(bf16[64,2048]{1,0:T(8,128)(2,1)S(1)} %get-tuple-element.44), channel_id=1, source_target_pairs={{0,16},{4,20},{8,24},{12,28},{16,0},{20,4},{24,8},{28,12},{1,17},{... | collective-permute-start | bytes 786440 | tf_op jit(solution)/shard_map/ppermute | solution.py:65
  37.3 0.0 collective-permute-done.13
  37.3 0.1 add_convert_fusion
  37.3 1.6 %collective-permute-start.14 = (bf16[64,2048]{1,0:T(8,128)(2,1)S(1)}, bf16[64,2048]{1,0:T(8,128)(2,1)S(1)}, u32[]{:S(2)}, u32[]{:S(2)}) collective-permute-start(bf16[64,2048]{1,0:T(8,128)(2,1)S(1)} %add_convert_fusion), channel_id=1, source_target_pairs={{0,8},{4,12},{8,0},{12,4},{16,24},{20,28},{24,16},{28,20},{1,9},{5... | collective-permute-start | bytes 786440 | tf_op jit(solution)/shard_map/ppermute | solution.py:65
  38.9 2.7 %shard_map.69 = (bf16[64,2048]{1,0:T(8,128)(2,1)S(1)}, bf16[64,2048]{1,0:T(8,128)(2,1)S(1)}) custom-call(bf16[64,2176]{1,0:T(8,128)(2,1)S(1)} %get-tuple-element.29.refs_0_, bf16[64,2176]{1,0:T(8,128)(2,1)S(1)} %get-tuple-element.30.refs_1_, bf16[2048,768]{1,0:T(8,128)(2,1)S(1)} %get-tuple-element.28.refs_1_.refs_2_, ...), custom_call_target="tpu_custom_call" | custom-call | flops 2415919104 | bytes 19922944 | tf_op jit(solution)/shard_map/pallas_call | solution.py:237
  41.6 0.0 collective-permute-done.9.refs_1_
  41.6 1.2 %collective-permute-done.11.refs_2_ = bf16[64,2048]{1,0:T(8,128)(2,1)S(1)} collective-permute-done((bf16[64,2048]{1,0:T(8,128)(2,1)S(1)}, bf16[64,2048]{1,0:T(8,128)(2,1)S(1)}, u32[]{:S(2)}, u32[]{:S(2)}) %collective-permute-start.11) | collective-permute-done | bytes 262176 | tf_op jit(solution)/shard_map/ppermute | solution.py:65
  42.7 2.8 %collective-permute-done.12.refs_4_ = bf16[64,2048]{1,0:T(8,128)(2,1)S(1)} collective-permute-done((bf16[64,2048]{1,0:T(8,128)(2,1)S(1)}, bf16[64,2048]{1,0:T(8,128)(2,1)S(1)}, u32[]{:S(2)}, u32[]{:S(2)}) %collective-permute-start.12) | collective-permute-done | bytes 262176 | tf_op jit(solution)/shard_map/ppermute | solution.py:65
  45.6 0.0 collective-permute-done.14.refs_5_
  45.6 0.9 %shard_map.76 = bf16[128,2048]{1,0:T(8,128)(2,1)} custom-call(bf16[64,2048]{1,0:T(8,128)(2,1)S(1)} %get-tuple-element.33.refs_0_, bf16[64,2048]{1,0:T(8,128)(2,1)S(1)} %collective-permute-done.9.refs_1_, bf16[64,2048]{1,0:T(8,128)(2,1)S(1)} %collective-permute-done.11.refs_2_, bf16[64,2048]{1,0:T(8,128)(2,1)S(1)} %get-tuple-element.43.refs_3_, ...), custom_call_target="tpu_custom_call" | custom-call | tf_op jit(solution)/shard_map/pallas_call | solution.py:160
  (6 shorter events, 0.2 us)
Async XLA Ops:
  0.0 15.4 %collective-permute-start.2 = (bf16[2048,768]{1,0:T(8,128)(2,1)}, bf16[2048,768]{1,0:T(8,128)(2,1)S(1)}, u32[]{:S(2)}, u32[]{:S(2)}) collective-permute-start(bf16[2048,768]{1,0:T(8,128)(2,1)} %bitcast.5), channel_id=1, source_target_pairs={{0,4},{4,0},{8,12},{12,8},{16,20},{20,16},{24,28},{28,24},{1,5},{5... | collective-permute-start | bytes 9437192 | tf_op jit(solution)/shard_map/ppermute | solution.py:65
  0.5 14.9 %collective-permute-start.3 = (bf16[2048,768]{1,0:T(8,128)(2,1)}, bf16[2048,768]{1,0:T(8,128)(2,1)S(1)}, u32[]{:S(2)}, u32[]{:S(2)}) collective-permute-start(bf16[2048,768]{1,0:T(8,128)(2,1)} %bitcast.7), channel_id=1, source_target_pairs={{0,4},{4,0},{8,12},{12,8},{16,20},{20,16},{24,28},{28,24},{1,5},{5... | collective-permute-start | bytes 9437192 | tf_op jit(solution)/shard_map/ppermute | solution.py:65
  0.5 16.7 %collective-permute-start.4 = (bf16[768,2048]{1,0:T(8,128)(2,1)}, bf16[768,2048]{1,0:T(8,128)(2,1)S(1)}, u32[]{:S(2)}, u32[]{:S(2)}) collective-permute-start(bf16[768,2048]{1,0:T(8,128)(2,1)} %bitcast.9), channel_id=1, source_target_pairs={{0,4},{4,0},{8,12},{12,8},{16,20},{20,16},{24,28},{28,24},{1,5},{5... | collective-permute-start | bytes 9437192 | tf_op jit(solution)/shard_map/ppermute | solution.py:65
  2.1 9.9 %collective-permute-start = (bf16[64,2176]{1,0:T(8,128)(2,1)S(1)}, bf16[64,2176]{1,0:T(8,128)(2,1)S(1)}, u32[]{:S(2)}, u32[]{:S(2)}) collective-permute-start(bf16[64,2176]{1,0:T(8,128)(2,1)S(1)} %get-tuple-element.27.refs_1_), channel_id=1, source_target_pairs={{0,8},{4,12},{8,0},{12,4},{16,24},{20,28},{24,16},{28,20},{1,9},{5... | collective-permute-start | bytes 835592 | tf_op jit(solution)/shard_map/ppermute | solution.py:65
  4.6 9.2 %collective-permute-start.1 = (bf16[64,2176]{1,0:T(8,128)(2,1)S(1)}, bf16[64,2176]{1,0:T(8,128)(2,1)S(1)}, u32[]{:S(2)}, u32[]{:S(2)}) collective-permute-start(bf16[64,2176]{1,0:T(8,128)(2,1)S(1)} %get-tuple-element.26.refs_0_), channel_id=1, source_target_pairs={{0,16},{4,20},{8,24},{12,28},{16,0},{20,4},{24,8},{28,12},{1,17},{... | collective-permute-start | bytes 835592 | tf_op jit(solution)/shard_map/ppermute | solution.py:65
  12.0 9.6 %collective-permute-start.7 = (bf16[64,2176]{1,0:T(8,128)(2,1)S(1)}, bf16[64,2176]{1,0:T(8,128)(2,1)S(1)}, u32[]{:S(2)}, u32[]{:S(2)}) collective-permute-start(bf16[64,2176]{1,0:T(8,128)(2,1)S(1)} %shard_map.66.refs_2_.refs_0_), channel_id=1, source_target_pairs={{0,16},{4,20},{8,24},{12,28},{16,0},{20,4},{24,8},{28,12},{1,17},{... | collective-permute-start | bytes 835592 | tf_op jit(solution)/shard_map/ppermute | solution.py:65
  13.8 9.7 %collective-permute-start.8 = (bf16[64,2176]{1,0:T(8,128)(2,1)S(1)}, bf16[64,2176]{1,0:T(8,128)(2,1)S(1)}, u32[]{:S(2)}, u32[]{:S(2)}) collective-permute-start(bf16[64,2176]{1,0:T(8,128)(2,1)S(1)} %shard_map.67.refs_3_.refs_1_), channel_id=1, source_target_pairs={{0,8},{4,12},{8,0},{12,4},{16,24},{20,28},{24,16},{28,20},{1,9},{5... | collective-permute-start | bytes 835592 | tf_op jit(solution)/shard_map/ppermute | solution.py:65
  15.4 14.0 %collective-permute-start.5 = (bf16[64,2176]{1,0:T(8,128)(2,1)S(1)}, bf16[64,2176]{1,0:T(8,128)(2,1)S(1)}, u32[]{:S(2)}, u32[]{:S(2)}) collective-permute-start(bf16[64,2176]{1,0:T(8,128)(2,1)S(1)} %get-tuple-element.30.refs_1_), channel_id=1, source_target_pairs={{0,8},{4,12},{8,0},{12,4},{16,24},{20,28},{24,16},{28,20},{1,9},{5... | collective-permute-start | bytes 835592 | tf_op jit(solution)/shard_map/ppermute | solution.py:65
  16.0 13.4 %collective-permute-start.6 = (bf16[64,2176]{1,0:T(8,128)(2,1)S(1)}, bf16[64,2176]{1,0:T(8,128)(2,1)S(1)}, u32[]{:S(2)}, u32[]{:S(2)}) collective-permute-start(bf16[64,2176]{1,0:T(8,128)(2,1)S(1)} %get-tuple-element.29.refs_0_), channel_id=1, source_target_pairs={{0,16},{4,20},{8,24},{12,28},{16,0},{20,4},{24,8},{28,12},{1,17},{... | collective-permute-start | bytes 835592 | tf_op jit(solution)/shard_map/ppermute | solution.py:65
  26.2 8.9 %collective-permute-start.10 = (bf16[64,2048]{1,0:T(8,128)(2,1)S(1)}, bf16[64,2048]{1,0:T(8,128)(2,1)S(1)}, u32[]{:S(2)}, u32[]{:S(2)}) collective-permute-start(bf16[64,2048]{1,0:T(8,128)(2,1)S(1)} %get-tuple-element.38.refs_2_), channel_id=1, source_target_pairs={{0,8},{4,12},{8,0},{12,4},{16,24},{20,28},{24,16},{28,20},{1,9},{5... | collective-permute-start | bytes 786440 | tf_op jit(solution)/shard_map/ppermute | solution.py:65
  27.8 9.5 %collective-permute-start.13 = (bf16[64,2048]{1,0:T(8,128)(2,1)S(1)}, bf16[64,2048]{1,0:T(8,128)(2,1)S(1)}, u32[]{:S(2)}, u32[]{:S(2)}) collective-permute-start(bf16[64,2048]{1,0:T(8,128)(2,1)S(1)} %get-tuple-element.46), channel_id=1, source_target_pairs={{0,16},{4,20},{8,24},{12,28},{16,0},{20,4},{24,8},{28,12},{1,17},{... | collective-permute-start | bytes 786440 | tf_op jit(solution)/shard_map/ppermute | solution.py:65
  32.2 9.3 %collective-permute-start.9 = (bf16[64,2048]{1,0:T(8,128)(2,1)S(1)}, bf16[64,2048]{1,0:T(8,128)(2,1)S(1)}, u32[]{:S(2)}, u32[]{:S(2)}) collective-permute-start(bf16[64,2048]{1,0:T(8,128)(2,1)S(1)} %get-tuple-element.42), channel_id=1, source_target_pairs={{0,8},{4,12},{8,0},{12,4},{16,24},{20,28},{24,16},{28,20},{1,9},{5... | collective-permute-start | bytes 786440 | tf_op jit(solution)/shard_map/ppermute | solution.py:65
  35.2 7.6 %collective-permute-start.11 = (bf16[64,2048]{1,0:T(8,128)(2,1)S(1)}, bf16[64,2048]{1,0:T(8,128)(2,1)S(1)}, u32[]{:S(2)}, u32[]{:S(2)}) collective-permute-start(bf16[64,2048]{1,0:T(8,128)(2,1)S(1)} %add_convert_fusion.1), channel_id=1, source_target_pairs={{0,16},{4,20},{8,24},{12,28},{16,0},{20,4},{24,8},{28,12},{1,17},{... | collective-permute-start | bytes 786440 | tf_op jit(solution)/shard_map/ppermute | solution.py:65
  36.4 9.2 %collective-permute-start.12 = (bf16[64,2048]{1,0:T(8,128)(2,1)S(1)}, bf16[64,2048]{1,0:T(8,128)(2,1)S(1)}, u32[]{:S(2)}, u32[]{:S(2)}) collective-permute-start(bf16[64,2048]{1,0:T(8,128)(2,1)S(1)} %get-tuple-element.44), channel_id=1, source_target_pairs={{0,16},{4,20},{8,24},{12,28},{16,0},{20,4},{24,8},{28,12},{1,17},{... | collective-permute-start | bytes 786440 | tf_op jit(solution)/shard_map/ppermute | solution.py:65
  37.3 8.2 %collective-permute-start.14 = (bf16[64,2048]{1,0:T(8,128)(2,1)S(1)}, bf16[64,2048]{1,0:T(8,128)(2,1)S(1)}, u32[]{:S(2)}, u32[]{:S(2)}) collective-permute-start(bf16[64,2048]{1,0:T(8,128)(2,1)S(1)} %add_convert_fusion), channel_id=1, source_target_pairs={{0,8},{4,12},{8,0},{12,4},{16,24},{20,28},{24,16},{28,20},{1,9},{5... | collective-permute-start | bytes 786440 | tf_op jit(solution)/shard_map/ppermute | solution.py:65

commit v3 on v2

v3 whole, which is shorter than its diff:
```python
import functools

import jax
import jax.numpy as jnp
from jax import lax
from jax.experimental import pallas as pl
from jax.experimental.pallas import tpu as pltpu
from jax.sharding import PartitionSpec as P

AXIS = "expert"
CORE, XBIT, YBIT = 1, 2, 4
FIRST, SECOND = 2, 4


def slot_table(routed, capacity):
    counted = routed.astype(jnp.int32)
    position = jnp.cumsum(counted, axis=1) - 1
    slot_ids = jnp.arange(capacity, dtype=jnp.int32)
    chosen = routed[:, None, :] & (position[:, None, :] == slot_ids[None, :, None])
    row_ids = jnp.arange(routed.shape[1], dtype=jnp.int32)
    slot_index = jnp.sum(jnp.where(chosen, row_ids[None, None, :], 0), axis=2)
    filled = jnp.any(chosen, axis=2)
    return (slot_index, filled)


def expert_ffn(slot_block, w_gate, w_up, w_down):
    width = slot_block.shape[-1]
    flat_rows = slot_block.reshape(-1, width)
    gate_act = jnp.dot(flat_rows, w_gate[0], preferred_element_type=jnp.float32)
    up_act = jnp.dot(flat_rows, w_up[0], preferred_element_type=jnp.float32)
    hidden = (jax.nn.silu(gate_act) * up_act).astype(jnp.bfloat16)
    expert_out = jnp.dot(hidden, w_down[0], preferred_element_type=jnp.float32)
    return expert_out.reshape(slot_block.shape[:-1] + (w_down.shape[2],))


def swap_all(rows):
    return lax.all_to_all(rows, AXIS, split_axis=0, concat_axis=0, tiled=True)


def route_table(expert_ids, gate_weights, experts):
    labels = jnp.arange(experts, dtype=jnp.int32)
    matched = expert_ids[:, :, None] == labels[None, None, :]
    weights = gate_weights.astype(jnp.float32)[:, :, None]
    return jnp.sum(jnp.where(matched, weights, jnp.float32(0.0)), axis=1)


def any_slice(tokens, expert_ids, gate_weights, w_gate, w_up, w_down):
    tok_dev, choose_k = expert_ids.shape
    width = tokens.shape[1]
    experts = w_gate.shape[0] * lax.axis_size(AXIS)
    capacity = min(tok_dev, 3 * tok_dev * choose_k // (2 * experts))
    weight = route_table(expert_ids, gate_weights, experts)
    home_index, home_filled = slot_table(weight.T != 0.0, capacity)
    arrived = swap_all(tokens[home_index])
    returned_rows = swap_all(expert_ffn(arrived, w_gate, w_up, w_down))
    owners = jnp.arange(experts, dtype=jnp.int32)[:, None]
    factor = jnp.where(home_filled, weight.T[owners, home_index], jnp.float32(0.0))
    combined = jnp.zeros((tok_dev, width), jnp.float32)
    combined = combined.at[home_index.reshape(-1)].add(
        (factor[:, :, None] * returned_rows).reshape(-1, width)
    )
    return combined.astype(jnp.bfloat16)


def hop(block, way):
    bits = {CORE: (CORE, CORE), FIRST: (XBIT, YBIT), SECOND: (YBIT, XBIT)}[way]
    pairs = [(i, i ^ bits[i & CORE]) for i in range(lax.axis_size(AXIS))]
    return lax.ppermute(block, AXIS, pairs)


def in_vmem(array):
    return pltpu.with_memory_space_constraint(array, pltpu.VMEM)


def vmem_out(shape):
    return pltpu.VMEM(shape, jnp.bfloat16)


MIB = 1 << 20
PARTS = 4
VMEM_SPEC = pl.BlockSpec(memory_space=pltpu.VMEM)
ANY_SPEC = pl.BlockSpec(memory_space=pl.ANY)


def parts_of(rows):
    return slice(0, rows // 2), slice(rows // 2, rows), slice(0, rows)


def label_body(tokens_ref, ids_ref, gates_ref, *refs):
    *out_refs, ids_buf, gates_buf, sem = refs
    width = tokens_ref.shape[1]
    rows, tail = ids_ref.shape[1], out_refs[0].shape[1] - width
    pairs = [(ids_ref, ids_buf), (gates_ref, gates_buf)]
    for out_ref, part in zip(out_refs, parts_of(rows)):
        pairs.append((tokens_ref.at[pl.ds(part.start, out_ref.shape[0])], out_ref.at[:, pl.ds(0, width)]))
    copies = [pltpu.make_async_copy(src, dst, sem.at[k]) for k, (src, dst) in enumerate(pairs)]
    for copy in copies:
        copy.start()
    for copy in copies[:2]:
        copy.wait()
    me = lax.axis_index(AXIS)
    column = lax.broadcasted_iota(jnp.int32, (tail, rows), 0)
    gates = gates_buf[...].astype(jnp.float32)
    route = jnp.zeros((tail, rows), jnp.float32)
    for k in range(ids_ref.shape[0]):
        away = ids_buf[k : k + 1, :] ^ me
        turned = (away & CORE) | ((away & XBIT) << 1) | ((away & YBIT) >> 1)
        away = jnp.where(me & CORE == 0, away, turned)
        route += jnp.where(column == away, gates[k : k + 1, :], 0.0)
    route = route.T.astype(jnp.bfloat16)
    for out_ref, part in zip(out_refs, parts_of(rows)):
        out_ref[:, width:] = route[part]
    for copy in copies[2:]:
        copy.wait()


def label(tokens, expert_ids, gate_weights, tail):
    rows, width = tokens.shape
    parts = parts_of(rows)
    arrays = (tokens, expert_ids.T, gate_weights.T)
    return pl.pallas_call(
        label_body,
        out_shape=[vmem_out((p.stop - p.start, width + tail)) for p in parts],
        in_specs=[ANY_SPEC] * 3,
        out_specs=[VMEM_SPEC] * len(parts),
        scratch_shapes=[pltpu.VMEM(a.shape, a.dtype) for a in arrays[1:]]
        + [pltpu.SemaphoreType.DMA((2 + len(parts),))],
        compiler_params=pltpu.CompilerParams(vmem_limit_bytes=8 * MIB),
    )(*[pltpu.with_memory_space_constraint(a, pltpu.HBM) for a in arrays])


def after(value, *arrived):
    return lax.optimization_barrier((value, *arrived))[0]


def finish_body(*refs):
    terms, out_ref, (buf, sem) = refs[:-3], refs[-3], refs[-2:]
    rows = out_ref.shape[0] // PARTS
    copies = []
    for k in range(PARTS):
        part = slice(k * rows, (k + 1) * rows)
        buf[part] = sum(t[part].astype(jnp.float32) for t in terms).astype(jnp.bfloat16)
        at = pl.ds(k * rows, rows)
        copies.append(pltpu.make_async_copy(buf.at[at], out_ref.at[at], sem.at[k]))
        copies[-1].start()
    for copy in copies:
        copy.wait()


def finish(terms):
    shape = terms[0].shape
    return pl.pallas_call(
        finish_body,
        out_shape=jax.ShapeDtypeStruct(shape, jnp.bfloat16),
        in_specs=[VMEM_SPEC] * len(terms),
        out_specs=ANY_SPEC,
        scratch_shapes=[pltpu.VMEM(shape, jnp.bfloat16), pltpu.SemaphoreType.DMA((PARTS,))],
        compiler_params=pltpu.CompilerParams(vmem_limit_bytes=8 * MIB),
    )(*[in_vmem(a) for a in terms])


def fetch_body(n, *refs):
    outs, sem = refs[-n - 1 : -1], refs[-1]
    copies = [pltpu.make_async_copy(refs[k], outs[k], sem.at[k]) for k in range(n)]
    for copy in copies:
        copy.start()
    for copy in copies:
        copy.wait()


def fetch(arrays):
    n = len(arrays)
    return pl.pallas_call(
        functools.partial(fetch_body, n),
        out_shape=[vmem_out(a.shape) for a in arrays],
        in_specs=[ANY_SPEC] * n,
        out_specs=[VMEM_SPEC] * n,
        scratch_shapes=[pltpu.SemaphoreType.DMA((n,))],
        compiler_params=pltpu.CompilerParams(vmem_limit_bytes=8 * MIB),
        cost_estimate=pl.CostEstimate(
            flops=0, bytes_accessed=4 * sum(a.size for a in arrays), transcendentals=0
        ),
    )(*[pltpu.with_memory_space_constraint(a, pltpu.HBM) for a in arrays])


def ffn_body(steps, n, *refs):
    x_refs, weights, (o_ref, x_buf, h_buf) = refs[:n], refs[n : n + 6], refs[n + 6 :]
    width, hidden = o_ref.shape[1], h_buf.shape[1] // 2
    columns, at = ([], []), 0
    for x_ref in x_refs:
        x_buf[at : at + x_ref.shape[0]] = x_ref[:, :width]
        at += x_ref.shape[0]
        for e in range(2):
            lane = width + (steps ^ (e * CORE))
            columns[e].append(x_ref[:, lane : lane + 1].astype(jnp.float32))
    columns = [jnp.concatenate(parts) for parts in columns]
    for e in range(2):
        w_gate, w_up = weights[3 * e], weights[3 * e + 1]
        for f in range(0, hidden, 256):
            x = x_buf[...]
            gate = jnp.dot(x, w_gate[:, f : f + 256], preferred_element_type=jnp.float32)
            up = jnp.dot(x, w_up[:, f : f + 256], preferred_element_type=jnp.float32)
            act = (gate / (1.0 + jnp.exp(-gate)) * up).astype(jnp.bfloat16)
            h_buf[:, e * hidden + f : e * hidden + f + 256] = act
    for c in range(0, width, 512):
        out = None
        for e in range(2):
            act = h_buf[:, e * hidden : (e + 1) * hidden]
            part = jnp.dot(act, weights[3 * e + 2][:, c : c + 512], preferred_element_type=jnp.float32)
            part = columns[e] * part
            out = part if out is None else out + part
        o_ref[:, c : c + 512] = out.astype(jnp.bfloat16)


def ffn(blocks, steps, *, width, weights):
    rows, hidden = sum(block.shape[0] for block in blocks), weights[0].shape[1]
    return pl.pallas_call(
        functools.partial(ffn_body, steps, len(blocks)),
        out_shape=vmem_out((rows, width)),
        in_specs=[VMEM_SPEC] * (len(blocks) + 6),
        out_specs=VMEM_SPEC,
        scratch_shapes=[
            pltpu.VMEM((rows, width), jnp.bfloat16),
            pltpu.VMEM((rows, 2 * hidden), jnp.bfloat16),
        ],
        compiler_params=pltpu.CompilerParams(vmem_limit_bytes=16 * MIB),
        cost_estimate=pl.CostEstimate(
            flops=12 * rows * width * hidden,
            bytes_accessed=2 * sum(w.size for w in weights) + 4 * rows * width,
            transcendentals=2 * rows * hidden,
        ),
    )(*[in_vmem(a) for a in (*blocks, *weights)])


def two_by_two(tokens, expert_ids, gate_weights, w_gate, w_up, w_down):
    width = tokens.shape[1]
    *halves, home = label(tokens, expert_ids, gate_weights, 128)

    near = [hop(half, FIRST) for half in halves]
    own = (w_gate[0], w_up[0], w_down[0])
    swapped = [hop(w, CORE) for w in own]
    fetched = fetch(own)
    near = [after(half, fetched[0]) for half in near]
    far = [hop(half, SECOND) for half in near]
    side = hop(after(home, *near), SECOND)

    run = functools.partial(ffn, width=width, weights=[*fetched, *swapped])
    far_out = run(far, FIRST | SECOND)
    passed = hop(far_out, FIRST)
    near_out = run([after(near[0], far_out), near[1]], FIRST)
    from_near = hop(near_out, FIRST)
    side_out = run([after(side, near_out)], SECOND)
    joined = side_out.astype(jnp.float32) + passed.astype(jnp.float32)
    from_side = hop(joined.astype(jnp.bfloat16), SECOND)
    home_out = run([after(home, from_near)], 0)
    return finish([home_out, from_near, from_side])


def solution(mesh):
    return jax.shard_map(
        two_by_two if mesh.shape[AXIS] == 8 else any_slice,
        mesh=mesh,
        in_specs=(
            P(("dp", AXIS), None),
            P(("dp", AXIS), None),
            P(("dp", AXIS), None),
            P(AXIS, None, None),
            P(AXIS, None, None),
            P(AXIS, None, None),
        ),
        out_specs=P(("dp", AXIS), None),
        check_vma=False,
    )
```

time: 46.6 us -> 43.6 us (0.936)
  starting transfers between devices: 17.4 us -> 14.3 us
    ppermute x15 -> x11, starting transfers between devices: 17.4 us -> 14.3 us  [hop(): return lax.ppermute(block, AXIS, pairs)]
    ppermute x15 -> x11, waiting for transfers between devices: 12.2 us -> 12.4 us  [hop(): return lax.ppermute(block, AXIS, pairs)]
    pallas_call x13 -> x7, Pallas kernels: 16.6 us -> 16.6 us  [the longest x4 10.6 us: ffn(): pl.pallas_call(functools.partial(ffn_body, steps, len(blocks)), out_shape...]
  transfers between devices with their start and end apart: 15 -> 11, of which waited for: 7 -> 6; matrix products, arithmetic and copies ran while one was open for 0% -> 0% of each run, Pallas kernels for 34% -> 36%
where the time goes in v3:
time: 43.6 us; the launch traced here: 43.5 us
  Pallas kernels  16.6 us (38%)
  starting transfers between devices  14.3 us (33%)
  waiting for transfers between devices  12.4 us (28%)
    ppermute x11, starting transfers between devices, hop(): return lax.ppermute(block, AXIS, pairs)  14.3 us
    ppermute x11, waiting for transfers between devices, hop(): return lax.ppermute(block, AXIS, pairs)  12.4 us
    pallas_call x4, Pallas kernels, ffn(): pl.pallas_call(functools.partial(ffn_body, steps, len(blocks)), out_shape...  10.6 us
    pallas_call x1, Pallas kernels, fetch(): pl.pallas_call(functools.partial(fetch_body, n), out_shape=[vmem_out(a.sh...  3.78 us
    pallas_call x1, Pallas kernels, label(): pl.pallas_call(label_body, out_shape=[vmem_out((p.stop - p.start, width +...  1.36 us
    pallas_call x1, Pallas kernels, finish(): pl.pallas_call(finish_body, out_shape=jax.ShapeDtypeStruct(shape, jnp.bfl...  0.88 us
  transfers between devices with their start and end apart: 11, of which 6 were waited for; matrix products, arithmetic and copies ran while one was open for 0% of the time, Pallas kernels for 36%

profile of v3, /device:TPU:0, one launch (start us, length us, event | category | flops | bytes accessed | tf_op | source)
XLA Modules:
  0.0 43.5 jit_solution(16477451959779550248)
XLA Ops:
  0.0 0.5 %collective-permute-start.4 = (bf16[2048,768]{1,0:T(8,128)(2,1)}, bf16[2048,768]{1,0:T(8,128)(2,1)S(1)}, u32[]{:S(2)}, u32[]{:S(2)}) collective-permute-start(bf16[2048,768]{1,0:T(8,128)(2,1)} %bitcast.5), channel_id=1, source_target_pairs={{0,4},{4,0},{8,12},{12,8},{16,20},{20,16},{24,28},{28,24},{1,5},{5... | collective-permute-start | bytes 9437192 | tf_op jit(solution)/shard_map/ppermute | solution.py:68
  0.5 0.1 collective-permute-start.5
  0.5 0.5 %collective-permute-start.6 = (bf16[768,2048]{1,0:T(8,128)(2,1)}, bf16[768,2048]{1,0:T(8,128)(2,1)S(1)}, u32[]{:S(2)}, u32[]{:S(2)}) collective-permute-start(bf16[768,2048]{1,0:T(8,128)(2,1)} %bitcast.9), channel_id=1, source_target_pairs={{0,4},{4,0},{8,12},{12,8},{16,20},{20,16},{24,28},{28,24},{1,5},{5... | collective-permute-start | bytes 9437192 | tf_op jit(solution)/shard_map/ppermute | solution.py:68
  1.0 1.4 %shard_map.64 = (bf16[64,2176]{1,0:T(8,128)(2,1)S(1)}, bf16[64,2176]{1,0:T(8,128)(2,1)S(1)}, bf16[128,2176]{1,0:T(8,128)(2,1)S(1)}) custom-call(bf16[128,2048]{1,0:T(8,128)(2,1)} %tokens_ref.1, s32[4,128]{1,0:T(4,128)} %bitcast.11, bf16[4,128]{1,0:T(4,128)(2,1)} %bitcast.12), custom_call_target="tpu_custom_call" | custom-call | tf_op jit(solution)/shard_map/pallas_call | solution.py:121
  2.3 2.6 %collective-permute-start = (bf16[64,2176]{1,0:T(8,128)(2,1)S(1)}, bf16[64,2176]{1,0:T(8,128)(2,1)S(1)}, u32[]{:S(2)}, u32[]{:S(2)}) collective-permute-start(bf16[64,2176]{1,0:T(8,128)(2,1)S(1)} %get-tuple-element.18), channel_id=1, source_target_pairs={{0,8},{4,20},{8,0},{12,28},{16,24},{20,4},{24,16},{28,12},{1,9},{5... | collective-permute-start | bytes 835592 | tf_op jit(solution)/shard_map/ppermute | solution.py:68
  4.9 0.1 collective-permute-start.2
  5.0 3.8 %shard_map.65 = (bf16[2048,768]{1,0:T(8,128)(2,1)S(1)}, bf16[2048,768]{1,0:T(8,128)(2,1)S(1)}, bf16[768,2048]{1,0:T(8,128)(2,1)S(1)}) custom-call(bf16[2048,768]{1,0:T(8,128)(2,1)} %bitcast.6, bf16[2048,768]{1,0:T(8,128)(2,1)} %bitcast.8, bf16[768,2048]{1,0:T(8,128)(2,1)} %bitcast.10), custom_call_target="tpu_custom_call" | custom-call | bytes 18874368 | tf_op jit(solution)/shard_map/pallas_call | solution.py:173
  8.8 0.7 %collective-permute-done.refs_0_ = bf16[64,2176]{1,0:T(8,128)(2,1)S(1)} collective-permute-done((bf16[64,2176]{1,0:T(8,128)(2,1)S(1)}, bf16[64,2176]{1,0:T(8,128)(2,1)S(1)}, u32[]{:S(2)}, u32[]{:S(2)}) %collective-permute-start) | collective-permute-done | bytes 278560 | tf_op jit(solution)/shard_map/ppermute | solution.py:68
  9.4 2.0 %collective-permute-start.1 = (bf16[64,2176]{1,0:T(8,128)(2,1)S(1)}, bf16[64,2176]{1,0:T(8,128)(2,1)S(1)}, u32[]{:S(2)}, u32[]{:S(2)}) collective-permute-start(bf16[64,2176]{1,0:T(8,128)(2,1)S(1)} %collective-permute-done.refs_0_), channel_id=1, source_target_pairs={{0,16},{4,12},{8,24},{12,4},{16,0},{20,28},{24,8},{28,20},{1,17},{... | collective-permute-start | bytes 835592 | tf_op jit(solution)/shard_map/ppermute | solution.py:68
  11.5 1.3 %collective-permute-done.2.refs_1_ = bf16[64,2176]{1,0:T(8,128)(2,1)S(1)} collective-permute-done((bf16[64,2176]{1,0:T(8,128)(2,1)S(1)}, bf16[64,2176]{1,0:T(8,128)(2,1)S(1)}, u32[]{:S(2)}, u32[]{:S(2)}) %collective-permute-start.2) | collective-permute-done | bytes 278560 | tf_op jit(solution)/shard_map/ppermute | solution.py:68
  12.8 2.4 %collective-permute-start.3 = (bf16[64,2176]{1,0:T(8,128)(2,1)S(1)}, bf16[64,2176]{1,0:T(8,128)(2,1)S(1)}, u32[]{:S(2)}, u32[]{:S(2)}) collective-permute-start(bf16[64,2176]{1,0:T(8,128)(2,1)S(1)} %collective-permute-done.2.refs_1_), channel_id=1, source_target_pairs={{0,16},{4,12},{8,24},{12,4},{16,0},{20,28},{24,8},{28,20},{1,17},{... | collective-permute-start | bytes 835592 | tf_op jit(solution)/shard_map/ppermute | solution.py:68
  15.1 0.9 %collective-permute-done.1.refs_0_ = bf16[64,2176]{1,0:T(8,128)(2,1)S(1)} collective-permute-done((bf16[64,2176]{1,0:T(8,128)(2,1)S(1)}, bf16[64,2176]{1,0:T(8,128)(2,1)S(1)}, u32[]{:S(2)}, u32[]{:S(2)}) %collective-permute-start.1) | collective-permute-done | bytes 278560 | tf_op jit(solution)/shard_map/ppermute | solution.py:68
  16.0 2.0 %collective-permute-start.8 = (bf16[128,2176]{1,0:T(8,128)(2,1)S(1)}, bf16[128,2176]{1,0:T(8,128)(2,1)S(1)}, u32[]{:S(2)}, u32[]{:S(2)}) collective-permute-start(bf16[128,2176]{1,0:T(8,128)(2,1)S(1)} %get-tuple-element.27.refs_0_), channel_id=1, source_target_pairs={{0,16},{4,12},{8,24},{12,4},{16,0},{20,28},{24,8},{28,20},{1,17},{... | collective-permute-start | bytes 1671176 | tf_op jit(solution)/shard_map/ppermute | solution.py:68
  18.0 1.6 %collective-permute-done.3.refs_1_ = bf16[64,2176]{1,0:T(8,128)(2,1)S(1)} collective-permute-done((bf16[64,2176]{1,0:T(8,128)(2,1)S(1)}, bf16[64,2176]{1,0:T(8,128)(2,1)S(1)}, u32[]{:S(2)}, u32[]{:S(2)}) %collective-permute-start.3) | collective-permute-done | bytes 278560 | tf_op jit(solution)/shard_map/ppermute | solution.py:68
  19.6 0.0 collective-permute-done.4.refs_5_.refs_4_
  19.6 0.0 collective-permute-done.5.refs_6_.refs_5_
  19.7 0.0 collective-permute-done.6.refs_7_.refs_6_
  19.7 2.7 %shard_map.66 = bf16[128,2048]{1,0:T(8,128)(2,1)S(1)} custom-call(bf16[64,2176]{1,0:T(8,128)(2,1)S(1)} %collective-permute-done.1.refs_0_, bf16[64,2176]{1,0:T(8,128)(2,1)S(1)} %collective-permute-done.3.refs_1_, bf16[2048,768]{1,0:T(8,128)(2,1)S(1)} %get-tuple-element.19.refs_2_.refs_1_, bf16[2048,768]{1,0:T(8,128)(2,1)S(1)} %get-tuple-element.23.refs_3_.refs_2_, ...), custom_call_target="tpu_custom_call" | custom-call | flops 2415919104 | bytes 19922944 | tf_op jit(solution)/shard_map/pallas_call | solution.py:217
  22.3 2.1 %collective-permute-start.9 = (bf16[128,2048]{1,0:T(8,128)(2,1)S(1)}, bf16[128,2048]{1,0:T(8,128)(2,1)S(1)}, u32[]{:S(2)}, u32[]{:S(2)}) collective-permute-start(bf16[128,2048]{1,0:T(8,128)(2,1)S(1)} %shard_map.66), channel_id=1, source_target_pairs={{0,8},{4,20},{8,0},{12,28},{16,24},{20,4},{24,16},{28,12},{1,9},{5... | collective-permute-start | bytes 1572872 | tf_op jit(solution)/shard_map/ppermute | solution.py:68
  24.4 2.7 %shard_map.67 = bf16[128,2048]{1,0:T(8,128)(2,1)S(1)} custom-call(bf16[64,2176]{1,0:T(8,128)(2,1)S(1)} %collective-permute-done.refs_0_, bf16[64,2176]{1,0:T(8,128)(2,1)S(1)} %collective-permute-done.2.refs_1_, bf16[2048,768]{1,0:T(8,128)(2,1)S(1)} %get-tuple-element.19.refs_2_.refs_1_, bf16[2048,768]{1,0:T(8,128)(2,1)S(1)} %get-tuple-element.23.refs_3_.refs_2_, ...), custom_call_target="tpu_custom_call" | custom-call | flops 2415919104 | bytes 19922944 | tf_op jit(solution)/shard_map/pallas_call | solution.py:217
  27.0 0.1 collective-permute-start.7
  27.1 0.0 collective-permute-done.8.refs_0_
  27.1 2.7 %shard_map.69 = bf16[128,2048]{1,0:T(8,128)(2,1)S(1)} custom-call(bf16[128,2176]{1,0:T(8,128)(2,1)S(1)} %collective-permute-done.8.refs_0_, bf16[2048,768]{1,0:T(8,128)(2,1)S(1)} %get-tuple-element.19.refs_2_.refs_1_, bf16[2048,768]{1,0:T(8,128)(2,1)S(1)} %get-tuple-element.23.refs_3_.refs_2_, bf16[768,2048]{1,0:T(8,128)(2,1)S(1)} %get-tuple-element.24.refs_4_.refs_3_, ...), custom_call_target="tpu_custom_call" | custom-call | flops 2415919104 | bytes 19922944 | tf_op jit(solution)/shard_map/pallas_call | solution.py:217
  29.8 1.8 %collective-permute-done.9 = bf16[128,2048]{1,0:T(8,128)(2,1)S(1)} collective-permute-done((bf16[128,2048]{1,0:T(8,128)(2,1)S(1)}, bf16[128,2048]{1,0:T(8,128)(2,1)S(1)}, u32[]{:S(2)}, u32[]{:S(2)}) %collective-permute-start.9) | collective-permute-done | bytes 524320 | tf_op jit(solution)/shard_map/ppermute | solution.py:68
  31.6 0.1 add_convert_fusion
  31.7 2.1 %collective-permute-start.10 = (bf16[128,2048]{1,0:T(8,128)(2,1)S(1)}, bf16[128,2048]{1,0:T(8,128)(2,1)S(1)}, u32[]{:S(2)}, u32[]{:S(2)}) collective-permute-start(bf16[128,2048]{1,0:T(8,128)(2,1)S(1)} %add_convert_fusion), channel_id=1, source_target_pairs={{0,16},{4,12},{8,24},{12,4},{16,0},{20,28},{24,8},{28,20},{1,17},{... | collective-permute-start | bytes 1572872 | tf_op jit(solution)/shard_map/ppermute | solution.py:68
  33.8 6.1 %collective-permute-done.7.refs_1_ = bf16[128,2048]{1,0:T(8,128)(2,1)S(1)} collective-permute-done((bf16[128,2048]{1,0:T(8,128)(2,1)S(1)}, bf16[128,2048]{1,0:T(8,128)(2,1)S(1)}, u32[]{:S(2)}, u32[]{:S(2)}) %collective-permute-start.7) | collective-permute-done | bytes 524320 | tf_op jit(solution)/shard_map/ppermute | solution.py:68
  39.9 2.7 %shard_map.68.refs_0_ = bf16[128,2048]{1,0:T(8,128)(2,1)S(1)} custom-call(bf16[128,2176]{1,0:T(8,128)(2,1)S(1)} %get-tuple-element.27.refs_0_, bf16[2048,768]{1,0:T(8,128)(2,1)S(1)} %get-tuple-element.19.refs_2_.refs_1_, bf16[2048,768]{1,0:T(8,128)(2,1)S(1)} %get-tuple-element.23.refs_3_.refs_2_, bf16[768,2048]{1,0:T(8,128)(2,1)S(1)} %get-tuple-element.24.refs_4_.refs_3_, ...), custom_call_target="tpu_custom_call" | custom-call | flops 2415919104 | bytes 19922944 | tf_op jit(solution)/shard_map/pallas_call | solution.py:217
  42.6 0.0 collective-permute-done.10.refs_2_
  42.6 0.9 %shard_map.70 = bf16[128,2048]{1,0:T(8,128)(2,1)} custom-call(bf16[128,2048]{1,0:T(8,128)(2,1)S(1)} %shard_map.68.refs_0_, bf16[128,2048]{1,0:T(8,128)(2,1)S(1)} %collective-permute-done.7.refs_1_, bf16[128,2048]{1,0:T(8,128)(2,1)S(1)} %collective-permute-done.10.refs_2_), custom_call_target="tpu_custom_call" | custom-call | tf_op jit(solution)/shard_map/pallas_call | solution.py:152
Async XLA Ops:
  0.0 19.6 %collective-permute-start.4 = (bf16[2048,768]{1,0:T(8,128)(2,1)}, bf16[2048,768]{1,0:T(8,128)(2,1)S(1)}, u32[]{:S(2)}, u32[]{:S(2)}) collective-permute-start(bf16[2048,768]{1,0:T(8,128)(2,1)} %bitcast.5), channel_id=1, source_target_pairs={{0,4},{4,0},{8,12},{12,8},{16,20},{20,16},{24,28},{28,24},{1,5},{5... | collective-permute-start | bytes 9437192 | tf_op jit(solution)/shard_map/ppermute | solution.py:68
  0.5 19.2 %collective-permute-start.5 = (bf16[2048,768]{1,0:T(8,128)(2,1)}, bf16[2048,768]{1,0:T(8,128)(2,1)S(1)}, u32[]{:S(2)}, u32[]{:S(2)}) collective-permute-start(bf16[2048,768]{1,0:T(8,128)(2,1)} %bitcast.7), channel_id=1, source_target_pairs={{0,4},{4,0},{8,12},{12,8},{16,20},{20,16},{24,28},{28,24},{1,5},{5... | collective-permute-start | bytes 9437192 | tf_op jit(solution)/shard_map/ppermute | solution.py:68
  0.5 19.1 %collective-permute-start.6 = (bf16[768,2048]{1,0:T(8,128)(2,1)}, bf16[768,2048]{1,0:T(8,128)(2,1)S(1)}, u32[]{:S(2)}, u32[]{:S(2)}) collective-permute-start(bf16[768,2048]{1,0:T(8,128)(2,1)} %bitcast.9), channel_id=1, source_target_pairs={{0,4},{4,0},{8,12},{12,8},{16,20},{20,16},{24,28},{28,24},{1,5},{5... | collective-permute-start | bytes 9437192 | tf_op jit(solution)/shard_map/ppermute | solution.py:68
  2.3 7.1 %collective-permute-start = (bf16[64,2176]{1,0:T(8,128)(2,1)S(1)}, bf16[64,2176]{1,0:T(8,128)(2,1)S(1)}, u32[]{:S(2)}, u32[]{:S(2)}) collective-permute-start(bf16[64,2176]{1,0:T(8,128)(2,1)S(1)} %get-tuple-element.18), channel_id=1, source_target_pairs={{0,8},{4,20},{8,0},{12,28},{16,24},{20,4},{24,16},{28,12},{1,9},{5... | collective-permute-start | bytes 835592 | tf_op jit(solution)/shard_map/ppermute | solution.py:68
  4.9 7.9 %collective-permute-start.2 = (bf16[64,2176]{1,0:T(8,128)(2,1)S(1)}, bf16[64,2176]{1,0:T(8,128)(2,1)S(1)}, u32[]{:S(2)}, u32[]{:S(2)}) collective-permute-start(bf16[64,2176]{1,0:T(8,128)(2,1)S(1)} %get-tuple-element.21), channel_id=1, source_target_pairs={{0,8},{4,20},{8,0},{12,28},{16,24},{20,4},{24,16},{28,12},{1,9},{5... | collective-permute-start | bytes 835592 | tf_op jit(solution)/shard_map/ppermute | solution.py:68
  9.4 6.6 %collective-permute-start.1 = (bf16[64,2176]{1,0:T(8,128)(2,1)S(1)}, bf16[64,2176]{1,0:T(8,128)(2,1)S(1)}, u32[]{:S(2)}, u32[]{:S(2)}) collective-permute-start(bf16[64,2176]{1,0:T(8,128)(2,1)S(1)} %collective-permute-done.refs_0_), channel_id=1, source_target_pairs={{0,16},{4,12},{8,24},{12,4},{16,0},{20,28},{24,8},{28,20},{1,17},{... | collective-permute-start | bytes 835592 | tf_op jit(solution)/shard_map/ppermute | solution.py:68
  12.8 6.9 %collective-permute-start.3 = (bf16[64,2176]{1,0:T(8,128)(2,1)S(1)}, bf16[64,2176]{1,0:T(8,128)(2,1)S(1)}, u32[]{:S(2)}, u32[]{:S(2)}) collective-permute-start(bf16[64,2176]{1,0:T(8,128)(2,1)S(1)} %collective-permute-done.2.refs_1_), channel_id=1, source_target_pairs={{0,16},{4,12},{8,24},{12,4},{16,0},{20,28},{24,8},{28,20},{1,17},{... | collective-permute-start | bytes 835592 | tf_op jit(solution)/shard_map/ppermute | solution.py:68
  16.0 11.2 %collective-permute-start.8 = (bf16[128,2176]{1,0:T(8,128)(2,1)S(1)}, bf16[128,2176]{1,0:T(8,128)(2,1)S(1)}, u32[]{:S(2)}, u32[]{:S(2)}) collective-permute-start(bf16[128,2176]{1,0:T(8,128)(2,1)S(1)} %get-tuple-element.27.refs_0_), channel_id=1, source_target_pairs={{0,16},{4,12},{8,24},{12,4},{16,0},{20,28},{24,8},{28,20},{1,17},{... | collective-permute-start | bytes 1671176 | tf_op jit(solution)/shard_map/ppermute | solution.py:68
  22.3 9.2 %collective-permute-start.9 = (bf16[128,2048]{1,0:T(8,128)(2,1)S(1)}, bf16[128,2048]{1,0:T(8,128)(2,1)S(1)}, u32[]{:S(2)}, u32[]{:S(2)}) collective-permute-start(bf16[128,2048]{1,0:T(8,128)(2,1)S(1)} %shard_map.66), channel_id=1, source_target_pairs={{0,8},{4,20},{8,0},{12,28},{16,24},{20,4},{24,16},{28,12},{1,9},{5... | collective-permute-start | bytes 1572872 | tf_op jit(solution)/shard_map/ppermute | solution.py:68
  27.0 12.9 %collective-permute-start.7 = (bf16[128,2048]{1,0:T(8,128)(2,1)S(1)}, bf16[128,2048]{1,0:T(8,128)(2,1)S(1)}, u32[]{:S(2)}, u32[]{:S(2)}) collective-permute-start(bf16[128,2048]{1,0:T(8,128)(2,1)S(1)} %shard_map.67), channel_id=1, source_target_pairs={{0,8},{4,20},{8,0},{12,28},{16,24},{20,4},{24,16},{28,12},{1,9},{5... | collective-permute-start | bytes 1572872 | tf_op jit(solution)/shard_map/ppermute | solution.py:68
  31.7 10.9 %collective-permute-start.10 = (bf16[128,2048]{1,0:T(8,128)(2,1)S(1)}, bf16[128,2048]{1,0:T(8,128)(2,1)S(1)}, u32[]{:S(2)}, u32[]{:S(2)}) collective-permute-start(bf16[128,2048]{1,0:T(8,128)(2,1)S(1)} %add_convert_fusion), channel_id=1, source_target_pairs={{0,16},{4,12},{8,24},{12,4},{16,0},{20,28},{24,8},{28,20},{1,17},{... | collective-permute-start | bytes 1572872 | tf_op jit(solution)/shard_map/ppermute | solution.py:68

commit v4 on v3

--- a/solution.py
+++ b/solution.py
@@ -78,6 +78,8 @@
 
 MIB = 1 << 20
 PARTS = 4
+LANES = 128
+WEIGHT_ROWS = 16
 VMEM_SPEC = pl.BlockSpec(memory_space=pltpu.VMEM)
 ANY_SPEC = pl.BlockSpec(memory_space=pl.ANY)
 
@@ -87,44 +89,45 @@
 
 
 def label_body(tokens_ref, ids_ref, gates_ref, *refs):
-    *out_refs, ids_buf, gates_buf, sem = refs
-    width = tokens_ref.shape[1]
-    rows, tail = ids_ref.shape[1], out_refs[0].shape[1] - width
-    pairs = [(ids_ref, ids_buf), (gates_ref, gates_buf)]
-    for out_ref, part in zip(out_refs, parts_of(rows)):
-        pairs.append((tokens_ref.at[pl.ds(part.start, out_ref.shape[0])], out_ref.at[:, pl.ds(0, width)]))
+    *out_refs, buf, ids_buf, gates_buf, sem = refs
+    rows, width = buf.shape
+    pairs = [(ids_ref, ids_buf), (gates_ref, gates_buf), (tokens_ref, buf)]
     copies = [pltpu.make_async_copy(src, dst, sem.at[k]) for k, (src, dst) in enumerate(pairs)]
     for copy in copies:
         copy.start()
     for copy in copies[:2]:
         copy.wait()
     me = lax.axis_index(AXIS)
-    column = lax.broadcasted_iota(jnp.int32, (tail, rows), 0)
+    row = lax.broadcasted_iota(jnp.int32, (WEIGHT_ROWS, rows), 0)
     gates = gates_buf[...].astype(jnp.float32)
-    route = jnp.zeros((tail, rows), jnp.float32)
+    route = jnp.zeros((WEIGHT_ROWS, rows), jnp.float32)
     for k in range(ids_ref.shape[0]):
         away = ids_buf[k : k + 1, :] ^ me
         turned = (away & CORE) | ((away & XBIT) << 1) | ((away & YBIT) >> 1)
         away = jnp.where(me & CORE == 0, away, turned)
-        route += jnp.where(column == away, gates[k : k + 1, :], 0.0)
-    route = route.T.astype(jnp.bfloat16)
+        route += jnp.where(row == away, gates[k : k + 1, :], 0.0)
+    route = route.astype(jnp.bfloat16)
+    for out_ref in out_refs:
+        out_ref[out_ref.shape[0] - WEIGHT_ROWS :] = route
+    copies[2].wait()
     for out_ref, part in zip(out_refs, parts_of(rows)):
-        out_ref[:, width:] = route[part]
-    for copy in copies[2:]:
-        copy.wait()
-
-
-def label(tokens, expert_ids, gate_weights, tail):
+        size = part.stop - part.start
+        for k in range(width // LANES):
+            out_ref[k * size : (k + 1) * size] = buf[part, k * LANES : (k + 1) * LANES]
+
+
+def label(tokens, expert_ids, gate_weights):
     rows, width = tokens.shape
     parts = parts_of(rows)
     arrays = (tokens, expert_ids.T, gate_weights.T)
+    lengths = [(p.stop - p.start) * width // LANES + WEIGHT_ROWS for p in parts]
     return pl.pallas_call(
         label_body,
-        out_shape=[vmem_out((p.stop - p.start, width + tail)) for p in parts],
+        out_shape=[vmem_out((length, LANES)) for length in lengths],
         in_specs=[ANY_SPEC] * 3,
         out_specs=[VMEM_SPEC] * len(parts),
-        scratch_shapes=[pltpu.VMEM(a.shape, a.dtype) for a in arrays[1:]]
-        + [pltpu.SemaphoreType.DMA((2 + len(parts),))],
+        scratch_shapes=[pltpu.VMEM(a.shape, a.dtype) for a in arrays]
+        + [pltpu.SemaphoreType.DMA((3,))],
         compiler_params=pltpu.CompilerParams(vmem_limit_bytes=8 * MIB),
     )(*[pltpu.with_memory_space_constraint(a, pltpu.HBM) for a in arrays])
 
@@ -159,6 +162,41 @@
     )(*[in_vmem(a) for a in terms])
 
 
+def stage_body(*refs):
+    n = len(refs) // 2
+    for src, dst in zip(refs[:n], refs[n:]):
+        dst[...] = src[...]
+
+
+def stage(parts, hint):
+    n = len(parts)
+    return pl.pallas_call(
+        stage_body,
+        out_shape=[vmem_out(p.shape) for p in parts],
+        in_specs=[VMEM_SPEC] * n,
+        out_specs=[VMEM_SPEC] * n,
+        compiler_params=pltpu.CompilerParams(vmem_limit_bytes=8 * MIB),
+        cost_estimate=pl.CostEstimate(
+            flops=hint, bytes_accessed=4 * sum(p.size for p in parts), transcendentals=0
+        ),
+    )(*[in_vmem(p) for p in parts])
+
+
+def add_body(a_ref, b_ref, out_ref):
+    out_ref[...] = a_ref[...].astype(jnp.float32) + b_ref[...].astype(jnp.float32)
+
+
+def add(a, b):
+    return pl.pallas_call(
+        add_body,
+        out_shape=pltpu.VMEM(a.shape, jnp.float32),
+        in_specs=[VMEM_SPEC] * 2,
+        out_specs=VMEM_SPEC,
+        compiler_params=pltpu.CompilerParams(vmem_limit_bytes=8 * MIB),
+        cost_estimate=pl.CostEstimate(flops=10000000000, bytes_accessed=8 * a.size, transcendentals=0),
+    )(in_vmem(a), in_vmem(b))
+
+
 def fetch_body(n, *refs):
     outs, sem = refs[-n - 1 : -1], refs[-1]
     copies = [pltpu.make_async_copy(refs[k], outs[k], sem.at[k]) for k in range(n)]
@@ -186,14 +224,17 @@
 def ffn_body(steps, n, *refs):
     x_refs, weights, (o_ref, x_buf, h_buf) = refs[:n], refs[n : n + 6], refs[n + 6 :]
     width, hidden = o_ref.shape[1], h_buf.shape[1] // 2
-    columns, at = ([], []), 0
+    at = 0
     for x_ref in x_refs:
-        x_buf[at : at + x_ref.shape[0]] = x_ref[:, :width]
-        at += x_ref.shape[0]
-        for e in range(2):
-            lane = width + (steps ^ (e * CORE))
-            columns[e].append(x_ref[:, lane : lane + 1].astype(jnp.float32))
-    columns = [jnp.concatenate(parts) for parts in columns]
+        rows = (x_ref.shape[0] - WEIGHT_ROWS) * LANES // width
+        for k in range(width // LANES):
+            x_buf[at : at + rows, k * LANES : (k + 1) * LANES] = x_ref[k * rows : (k + 1) * rows]
+        at += rows
+    route = x_refs[0][x_refs[0].shape[0] - WEIGHT_ROWS :].astype(jnp.float32)
+    columns = []
+    for row in (steps, steps ^ CORE):
+        spread = jnp.broadcast_to(route[row : row + 1], (route.shape[1], route.shape[1]))
+        columns.append(spread.T[:, :1])
     for e in range(2):
         w_gate, w_up = weights[3 * e], weights[3 * e + 1]
         for f in range(0, hidden, 256):
@@ -213,7 +254,8 @@
 
 
 def ffn(blocks, steps, *, width, weights):
-    rows, hidden = sum(block.shape[0] for block in blocks), weights[0].shape[1]
+    hidden = weights[0].shape[1]
+    rows = sum(block.shape[0] - WEIGHT_ROWS for block in blocks) * LANES // width
     return pl.pallas_call(
         functools.partial(ffn_body, steps, len(blocks)),
         out_shape=vmem_out((rows, width)),
@@ -234,31 +276,38 @@
 
 def two_by_two(tokens, expert_ids, gate_weights, w_gate, w_up, w_down):
     width = tokens.shape[1]
-    *halves, home = label(tokens, expert_ids, gate_weights, 128)
+    *halves, home = label(tokens, expert_ids, gate_weights)
 
     near = [hop(half, FIRST) for half in halves]
     own = (w_gate[0], w_up[0], w_down[0])
+    fetched = fetch(own)
     swapped = [hop(w, CORE) for w in own]
-    fetched = fetch(own)
     near = [after(half, fetched[0]) for half in near]
-    far = [hop(half, SECOND) for half in near]
-    side = hop(after(home, *near), SECOND)
+    far = stage([hop(half, SECOND) for half in near], 28000000000)
+    side = [hop(after(home, *near, swapped[0]), SECOND)]
 
     run = functools.partial(ffn, width=width, weights=[*fetched, *swapped])
     far_out = run(far, FIRST | SECOND)
     passed = hop(far_out, FIRST)
     near_out = run([after(near[0], far_out), near[1]], FIRST)
     from_near = hop(near_out, FIRST)
-    side_out = run([after(side, near_out)], SECOND)
+    side_out = run([after(side[0], near_out), *side[1:]], SECOND)
     joined = side_out.astype(jnp.float32) + passed.astype(jnp.float32)
-    from_side = hop(joined.astype(jnp.bfloat16), SECOND)
-    home_out = run([after(home, from_near)], 0)
-    return finish([home_out, from_near, from_side])
+    joined = joined.astype(jnp.bfloat16)
+    from_side = hop(joined, SECOND)
+    home_out = run([after(home, joined)], 0)
+    total = add(home_out, from_near)
+    return finish([total, from_side])
+
+
+def on_device(tokens, *rest):
+    fits = lax.axis_size(AXIS) == 8 and tokens.shape[0] == LANES
+    return (two_by_two if fits else any_slice)(tokens, *rest)
 
 
 def solution(mesh):
     return jax.shard_map(
-        two_by_two if mesh.shape[AXIS] == 8 else any_slice,
+        on_device,
         mesh=mesh,
         in_specs=(
             P(("dp", AXIS), None),

time: 43.6 us -> 42 us (0.963)
  starting transfers between devices: 14.3 us -> 12.2 us
  Pallas kernels: 16.6 us -> 17.6 us
  waiting for transfers between devices: 12.4 us -> 11.6 us
    ppermute x11, starting transfers between devices: 14.3 us -> 12.2 us  [hop(): return lax.ppermute(block, AXIS, pairs)]
    pallas_call x4, Pallas kernels: 10.6 us -> 11.6 us  [ffn(): pl.pallas_call(functools.partial(ffn_body, steps, len(blocks)), out_shape...]
    ppermute x11, waiting for transfers between devices: 12.4 us -> 11.6 us  [hop(): return lax.ppermute(block, AXIS, pairs)]
    pallas_call x1 -> x3, Pallas kernels: 1.36 us -> 1.39 us  [the longest x1 1.25 us: label(): pl.pallas_call(label_body, out_shape=[vmem_out((length, LANES)) for lengt...]
  transfers between devices with their start and end apart: 11 -> 11, of which waited for: 6 -> 6; matrix products, arithmetic and copies ran while one was open for 0% -> 0% of each run, Pallas kernels for 36% -> 40%
where the time goes in v4:
time: 42 us; the launch traced here: 41.5 us
  Pallas kernels  17.6 us (42%)
  starting transfers between devices  12.2 us (29%)
  waiting for transfers between devices  11.6 us (28%)
    ppermute x11, starting transfers between devices, hop(): return lax.ppermute(block, AXIS, pairs)  12.2 us
    ppermute x11, waiting for transfers between devices, hop(): return lax.ppermute(block, AXIS, pairs)  11.6 us
    pallas_call x4, Pallas kernels, ffn(): pl.pallas_call(functools.partial(ffn_body, steps, len(blocks)), out_shape...  11.6 us
    pallas_call x1, Pallas kernels, fetch(): pl.pallas_call(functools.partial(fetch_body, n), out_shape=[vmem_out(a.sh...  3.78 us
    pallas_call x1, Pallas kernels, label(): pl.pallas_call(label_body, out_shape=[vmem_out((length, LANES)) for lengt...  1.25 us
    pallas_call x1, Pallas kernels, finish(): pl.pallas_call(finish_body, out_shape=jax.ShapeDtypeStruct(shape, jnp.bfl...  0.85 us
  transfers between devices with their start and end apart: 11, of which 6 were waited for; matrix products, arithmetic and copies ran while one was open for 0% of the time, Pallas kernels for 40%

profile of v4, /device:TPU:0, one launch (start us, length us, event | category | flops | bytes accessed | tf_op | source)
XLA Modules:
  0.0 41.5 jit_solution(17505914981165025850)
XLA Ops:
  0.0 0.5 %collective-permute-start.2 = (bf16[2048,768]{1,0:T(8,128)(2,1)}, bf16[2048,768]{1,0:T(8,128)(2,1)S(1)}, u32[]{:S(2)}, u32[]{:S(2)}) collective-permute-start(bf16[2048,768]{1,0:T(8,128)(2,1)} %bitcast.5), channel_id=1, source_target_pairs={{0,4},{4,0},{8,12},{12,8},{16,20},{20,16},{24,28},{28,24},{1,5},{5... | collective-permute-start | bytes 9437192 | tf_op jit(solution)/shard_map/ppermute | solution.py:68
  0.5 1.3 %shard_map.64 = (bf16[1040,128]{1,0:T(8,128)(2,1)S(1)}, bf16[1040,128]{1,0:T(8,128)(2,1)S(1)}, bf16[2064,128]{1,0:T(8,128)(2,1)S(1)}) custom-call(bf16[128,2048]{1,0:T(8,128)(2,1)} %tokens_ref.1, s32[4,128]{1,0:T(4,128)} %bitcast.11, bf16[4,128]{1,0:T(4,128)(2,1)} %bitcast.12), custom_call_target="tpu_custom_call" | custom-call | tf_op jit(solution)/shard_map/pallas_call | solution.py:124
  1.7 2.6 %collective-permute-start = (bf16[1040,128]{1,0:T(8,128)(2,1)S(1)}, bf16[1040,128]{1,0:T(8,128)(2,1)S(1)}, u32[]{:S(2)}, u32[]{:S(2)}) collective-permute-start(bf16[1040,128]{1,0:T(8,128)(2,1)S(1)} %get-tuple-element.20), channel_id=1, source_target_pairs={{0,8},{4,20},{8,0},{12,28},{16,24},{20,4},{24,16},{28,12},{1,9},{5... | collective-permute-start | bytes 798728 | tf_op jit(solution)/shard_map/ppermute | solution.py:68
  4.3 0.1 collective-permute-start.1
  4.3 0.3 collective-permute-start.6
  4.6 0.3 collective-permute-start.7
  4.9 3.8 %shard_map.65 = (bf16[2048,768]{1,0:T(8,128)(2,1)S(1)}, bf16[2048,768]{1,0:T(8,128)(2,1)S(1)}, bf16[768,2048]{1,0:T(8,128)(2,1)S(1)}) custom-call(bf16[2048,768]{1,0:T(8,128)(2,1)} %bitcast.6, bf16[2048,768]{1,0:T(8,128)(2,1)} %bitcast.8, bf16[768,2048]{1,0:T(8,128)(2,1)} %bitcast.10), custom_call_target="tpu_custom_call" | custom-call | bytes 18874368 | tf_op jit(solution)/shard_map/pallas_call | solution.py:211
  8.6 0.0 collective-permute-done.refs_0_
  8.7 2.0 %collective-permute-start.4 = (bf16[1040,128]{1,0:T(8,128)(2,1)S(1)}, bf16[1040,128]{1,0:T(8,128)(2,1)S(1)}, u32[]{:S(2)}, u32[]{:S(2)}) collective-permute-start(bf16[1040,128]{1,0:T(8,128)(2,1)S(1)} %collective-permute-done.refs_0_), channel_id=1, source_target_pairs={{0,16},{4,12},{8,24},{12,4},{16,0},{20,28},{24,8},{28,20},{1,17},{... | collective-permute-start | bytes 798728 | tf_op jit(solution)/shard_map/ppermute | solution.py:68
  10.7 0.8 %collective-permute-done.1.refs_1_ = bf16[1040,128]{1,0:T(8,128)(2,1)S(1)} collective-permute-done((bf16[1040,128]{1,0:T(8,128)(2,1)S(1)}, bf16[1040,128]{1,0:T(8,128)(2,1)S(1)}, u32[]{:S(2)}, u32[]{:S(2)}) %collective-permute-start.1) | collective-permute-done | bytes 266272 | tf_op jit(solution)/shard_map/ppermute | solution.py:68
  11.5 2.3 %collective-permute-start.5 = (bf16[1040,128]{1,0:T(8,128)(2,1)S(1)}, bf16[1040,128]{1,0:T(8,128)(2,1)S(1)}, u32[]{:S(2)}, u32[]{:S(2)}) collective-permute-start(bf16[1040,128]{1,0:T(8,128)(2,1)S(1)} %collective-permute-done.1.refs_1_), channel_id=1, source_target_pairs={{0,16},{4,12},{8,24},{12,4},{16,0},{20,28},{24,8},{28,20},{1,17},{... | collective-permute-start | bytes 798728 | tf_op jit(solution)/shard_map/ppermute | solution.py:68
  13.8 0.0 collective-permute-done.2.refs_5_.refs_4_
  13.8 0.0 collective-permute-start.3
  13.8 1.3 %collective-permute-done.4.refs_0_ = bf16[1040,128]{1,0:T(8,128)(2,1)S(1)} collective-permute-done((bf16[1040,128]{1,0:T(8,128)(2,1)S(1)}, bf16[1040,128]{1,0:T(8,128)(2,1)S(1)}, u32[]{:S(2)}, u32[]{:S(2)}) %collective-permute-start.4) | collective-permute-done | bytes 266272 | tf_op jit(solution)/shard_map/ppermute | solution.py:68
  15.1 3.0 %collective-permute-done.5.refs_1_ = bf16[1040,128]{1,0:T(8,128)(2,1)S(1)} collective-permute-done((bf16[1040,128]{1,0:T(8,128)(2,1)S(1)}, bf16[1040,128]{1,0:T(8,128)(2,1)S(1)}, u32[]{:S(2)}, u32[]{:S(2)}) %collective-permute-start.5) | collective-permute-done | bytes 266272 | tf_op jit(solution)/shard_map/ppermute | solution.py:68
  18.2 0.0 collective-permute-done.6.refs_6_.refs_5_
  18.2 0.0 collective-permute-done.7.refs_7_.refs_6_
  18.2 2.9 %shard_map.67 = bf16[128,2048]{1,0:T(8,128)(2,1)S(1)} custom-call(bf16[1040,128]{1,0:T(8,128)(2,1)S(1)} %get-tuple-element.26.refs_0_, bf16[1040,128]{1,0:T(8,128)(2,1)S(1)} %get-tuple-element.27.refs_1_, bf16[2048,768]{1,0:T(8,128)(2,1)S(1)} %get-tuple-element.21.refs_2_.refs_1_, bf16[2048,768]{1,0:T(8,128)(2,1)S(1)} %get-tuple-element.28.refs_3_.refs_2_, ...), custom_call_target="tpu_custom_call" | custom-call | flops 2415919104 | bytes 19922944 | tf_op jit(solution)/shard_map/pallas_call | solution.py:259
  21.1 2.1 %collective-permute-start.8 = (bf16[128,2048]{1,0:T(8,128)(2,1)S(1)}, bf16[128,2048]{1,0:T(8,128)(2,1)S(1)}, u32[]{:S(2)}, u32[]{:S(2)}) collective-permute-start(bf16[128,2048]{1,0:T(8,128)(2,1)S(1)} %shard_map.67), channel_id=1, source_target_pairs={{0,8},{4,20},{8,0},{12,28},{16,24},{20,4},{24,16},{28,12},{1,9},{5... | collective-permute-start | bytes 1572872 | tf_op jit(solution)/shard_map/ppermute | solution.py:68
  23.2 2.9 %shard_map.68 = bf16[128,2048]{1,0:T(8,128)(2,1)S(1)} custom-call(bf16[1040,128]{1,0:T(8,128)(2,1)S(1)} %collective-permute-done.refs_0_, bf16[1040,128]{1,0:T(8,128)(2,1)S(1)} %collective-permute-done.1.refs_1_, bf16[2048,768]{1,0:T(8,128)(2,1)S(1)} %get-tuple-element.21.refs_2_.refs_1_, bf16[2048,768]{1,0:T(8,128)(2,1)S(1)} %get-tuple-element.28.refs_3_.refs_2_, ...), custom_call_target="tpu_custom_call" | custom-call | flops 2415919104 | bytes 19922944 | tf_op jit(solution)/shard_map/pallas_call | solution.py:259
  26.1 0.1 collective-permute-start.9
  26.2 0.0 collective-permute-done.3.refs_0_
  26.2 2.9 %shard_map.69 = bf16[128,2048]{1,0:T(8,128)(2,1)S(1)} custom-call(bf16[2064,128]{1,0:T(8,128)(2,1)S(1)} %collective-permute-done.3.refs_0_, bf16[2048,768]{1,0:T(8,128)(2,1)S(1)} %get-tuple-element.21.refs_2_.refs_1_, bf16[2048,768]{1,0:T(8,128)(2,1)S(1)} %get-tuple-element.28.refs_3_.refs_2_, bf16[768,2048]{1,0:T(8,128)(2,1)S(1)} %get-tuple-element.29.refs_4_.refs_3_, ...), custom_call_target="tpu_custom_call" | custom-call | flops 2415919104 | bytes 19922944 | tf_op jit(solution)/shard_map/pallas_call | solution.py:259
  29.1 1.3 %collective-permute-done.8 = bf16[128,2048]{1,0:T(8,128)(2,1)S(1)} collective-permute-done((bf16[128,2048]{1,0:T(8,128)(2,1)S(1)}, bf16[128,2048]{1,0:T(8,128)(2,1)S(1)}, u32[]{:S(2)}, u32[]{:S(2)}) %collective-permute-start.8) | collective-permute-done | bytes 524320 | tf_op jit(solution)/shard_map/ppermute | solution.py:68
  30.4 0.1 add_convert_fusion
  30.5 2.1 %collective-permute-start.10 = (bf16[128,2048]{1,0:T(8,128)(2,1)S(1)}, bf16[128,2048]{1,0:T(8,128)(2,1)S(1)}, u32[]{:S(2)}, u32[]{:S(2)}) collective-permute-start(bf16[128,2048]{1,0:T(8,128)(2,1)S(1)} %add_convert_fusion), channel_id=1, source_target_pairs={{0,16},{4,12},{8,24},{12,4},{16,0},{20,28},{24,8},{28,20},{1,17},{... | collective-permute-start | bytes 1572872 | tf_op jit(solution)/shard_map/ppermute | solution.py:68
  32.6 2.9 %shard_map.70.a_ref = bf16[128,2048]{1,0:T(8,128)(2,1)S(1)} custom-call(bf16[2064,128]{1,0:T(8,128)(2,1)S(1)} %get-tuple-element.32.refs_0_, bf16[2048,768]{1,0:T(8,128)(2,1)S(1)} %get-tuple-element.21.refs_2_.refs_1_, bf16[2048,768]{1,0:T(8,128)(2,1)S(1)} %get-tuple-element.28.refs_3_.refs_2_, bf16[768,2048]{1,0:T(8,128)(2,1)S(1)} %get-tuple-element.29.refs_4_.refs_3_, ...), custom_call_target="tpu_custom_call" | custom-call | flops 2415919104 | bytes 19922944 | tf_op jit(solution)/shard_map/pallas_call | solution.py:259
  35.5 3.8 %collective-permute-done.9.b_ref = bf16[128,2048]{1,0:T(8,128)(2,1)S(1)} collective-permute-done((bf16[128,2048]{1,0:T(8,128)(2,1)S(1)}, bf16[128,2048]{1,0:T(8,128)(2,1)S(1)}, u32[]{:S(2)}, u32[]{:S(2)}) %collective-permute-start.9) | collective-permute-done | bytes 524320 | tf_op jit(solution)/shard_map/ppermute | solution.py:68
  39.3 0.1 shard_map.71.refs_0_
  39.4 1.3 %collective-permute-done.10.refs_1_ = bf16[128,2048]{1,0:T(8,128)(2,1)S(1)} collective-permute-done((bf16[128,2048]{1,0:T(8,128)(2,1)S(1)}, bf16[128,2048]{1,0:T(8,128)(2,1)S(1)}, u32[]{:S(2)}, u32[]{:S(2)}) %collective-permute-start.10) | collective-permute-done | bytes 524320 | tf_op jit(solution)/shard_map/ppermute | solution.py:68
  40.7 0.9 %shard_map.72 = bf16[128,2048]{1,0:T(8,128)(2,1)} custom-call(f32[128,2048]{1,0:T(8,128)S(1)} %shard_map.71.refs_0_, bf16[128,2048]{1,0:T(8,128)(2,1)S(1)} %collective-permute-done.10.refs_1_), custom_call_target="tpu_custom_call" | custom-call | tf_op jit(solution)/shard_map/pallas_call | solution.py:155
  (1 shorter events, 0.0 us)
Async XLA Ops:
  0.0 13.8 %collective-permute-start.2 = (bf16[2048,768]{1,0:T(8,128)(2,1)}, bf16[2048,768]{1,0:T(8,128)(2,1)S(1)}, u32[]{:S(2)}, u32[]{:S(2)}) collective-permute-start(bf16[2048,768]{1,0:T(8,128)(2,1)} %bitcast.5), channel_id=1, source_target_pairs={{0,4},{4,0},{8,12},{12,8},{16,20},{20,16},{24,28},{28,24},{1,5},{5... | collective-permute-start | bytes 9437192 | tf_op jit(solution)/shard_map/ppermute | solution.py:68
  1.7 7.0 %collective-permute-start = (bf16[1040,128]{1,0:T(8,128)(2,1)S(1)}, bf16[1040,128]{1,0:T(8,128)(2,1)S(1)}, u32[]{:S(2)}, u32[]{:S(2)}) collective-permute-start(bf16[1040,128]{1,0:T(8,128)(2,1)S(1)} %get-tuple-element.20), channel_id=1, source_target_pairs={{0,8},{4,20},{8,0},{12,28},{16,24},{20,4},{24,16},{28,12},{1,9},{5... | collective-permute-start | bytes 798728 | tf_op jit(solution)/shard_map/ppermute | solution.py:68
  4.3 7.2 %collective-permute-start.1 = (bf16[1040,128]{1,0:T(8,128)(2,1)S(1)}, bf16[1040,128]{1,0:T(8,128)(2,1)S(1)}, u32[]{:S(2)}, u32[]{:S(2)}) collective-permute-start(bf16[1040,128]{1,0:T(8,128)(2,1)S(1)} %get-tuple-element.23), channel_id=1, source_target_pairs={{0,8},{4,20},{8,0},{12,28},{16,24},{20,4},{24,16},{28,12},{1,9},{5... | collective-permute-start | bytes 798728 | tf_op jit(solution)/shard_map/ppermute | solution.py:68
  4.3 13.9 %collective-permute-start.6 = (bf16[2048,768]{1,0:T(8,128)(2,1)}, bf16[2048,768]{1,0:T(8,128)(2,1)S(1)}, u32[]{:S(2)}, u32[]{:S(2)}) collective-permute-start(bf16[2048,768]{1,0:T(8,128)(2,1)} %bitcast.7), channel_id=1, source_target_pairs={{0,4},{4,0},{8,12},{12,8},{16,20},{20,16},{24,28},{28,24},{1,5},{5... | collective-permute-start | bytes 9437192 | tf_op jit(solution)/shard_map/ppermute | solution.py:68
  4.6 13.6 %collective-permute-start.7 = (bf16[768,2048]{1,0:T(8,128)(2,1)}, bf16[768,2048]{1,0:T(8,128)(2,1)S(1)}, u32[]{:S(2)}, u32[]{:S(2)}) collective-permute-start(bf16[768,2048]{1,0:T(8,128)(2,1)} %bitcast.9), channel_id=1, source_target_pairs={{0,4},{4,0},{8,12},{12,8},{16,20},{20,16},{24,28},{28,24},{1,5},{5... | collective-permute-start | bytes 9437192 | tf_op jit(solution)/shard_map/ppermute | solution.py:68
  8.7 6.5 %collective-permute-start.4 = (bf16[1040,128]{1,0:T(8,128)(2,1)S(1)}, bf16[1040,128]{1,0:T(8,128)(2,1)S(1)}, u32[]{:S(2)}, u32[]{:S(2)}) collective-permute-start(bf16[1040,128]{1,0:T(8,128)(2,1)S(1)} %collective-permute-done.refs_0_), channel_id=1, source_target_pairs={{0,16},{4,12},{8,24},{12,4},{16,0},{20,28},{24,8},{28,20},{1,17},{... | collective-permute-start | bytes 798728 | tf_op jit(solution)/shard_map/ppermute | solution.py:68
  11.5 6.6 %collective-permute-start.5 = (bf16[1040,128]{1,0:T(8,128)(2,1)S(1)}, bf16[1040,128]{1,0:T(8,128)(2,1)S(1)}, u32[]{:S(2)}, u32[]{:S(2)}) collective-permute-start(bf16[1040,128]{1,0:T(8,128)(2,1)S(1)} %collective-permute-done.1.refs_1_), channel_id=1, source_target_pairs={{0,16},{4,12},{8,24},{12,4},{16,0},{20,28},{24,8},{28,20},{1,17},{... | collective-permute-start | bytes 798728 | tf_op jit(solution)/shard_map/ppermute | solution.py:68
  13.8 12.4 %collective-permute-start.3 = (bf16[2064,128]{1,0:T(8,128)(2,1)S(1)}, bf16[2064,128]{1,0:T(8,128)(2,1)S(1)}, u32[]{:S(2)}, u32[]{:S(2)}) collective-permute-start(bf16[2064,128]{1,0:T(8,128)(2,1)S(1)} %get-tuple-element.32.refs_0_), channel_id=1, source_target_pairs={{0,16},{4,12},{8,24},{12,4},{16,0},{20,28},{24,8},{28,20},{1,17},{... | collective-permute-start | bytes 1585160 | tf_op jit(solution)/shard_map/ppermute | solution.py:68
  21.1 9.2 %collective-permute-start.8 = (bf16[128,2048]{1,0:T(8,128)(2,1)S(1)}, bf16[128,2048]{1,0:T(8,128)(2,1)S(1)}, u32[]{:S(2)}, u32[]{:S(2)}) collective-permute-start(bf16[128,2048]{1,0:T(8,128)(2,1)S(1)} %shard_map.67), channel_id=1, source_target_pairs={{0,8},{4,20},{8,0},{12,28},{16,24},{20,4},{24,16},{28,12},{1,9},{5... | collective-permute-start | bytes 1572872 | tf_op jit(solution)/shard_map/ppermute | solution.py:68
  26.1 13.2 %collective-permute-start.9 = (bf16[128,2048]{1,0:T(8,128)(2,1)S(1)}, bf16[128,2048]{1,0:T(8,128)(2,1)S(1)}, u32[]{:S(2)}, u32[]{:S(2)}) collective-permute-start(bf16[128,2048]{1,0:T(8,128)(2,1)S(1)} %shard_map.68), channel_id=1, source_target_pairs={{0,8},{4,20},{8,0},{12,28},{16,24},{20,4},{24,16},{28,12},{1,9},{5... | collective-permute-start | bytes 1572872 | tf_op jit(solution)/shard_map/ppermute | solution.py:68
  30.5 10.2 %collective-permute-start.10 = (bf16[128,2048]{1,0:T(8,128)(2,1)S(1)}, bf16[128,2048]{1,0:T(8,128)(2,1)S(1)}, u32[]{:S(2)}, u32[]{:S(2)}) collective-permute-start(bf16[128,2048]{1,0:T(8,128)(2,1)S(1)} %add_convert_fusion), channel_id=1, source_target_pairs={{0,16},{4,12},{8,24},{12,4},{16,0},{20,28},{24,8},{28,20},{1,17},{... | collective-permute-start | bytes 1572872 | tf_op jit(solution)/shard_map/ppermute | solution.py:68

commit v5 on v4

--- a/solution.py
+++ b/solution.py
@@ -224,12 +224,12 @@
 def ffn_body(steps, n, *refs):
     x_refs, weights, (o_ref, x_buf, h_buf) = refs[:n], refs[n : n + 6], refs[n + 6 :]
     width, hidden = o_ref.shape[1], h_buf.shape[1] // 2
-    at = 0
+    parts = []
     for x_ref in x_refs:
         rows = (x_ref.shape[0] - WEIGHT_ROWS) * LANES // width
-        for k in range(width // LANES):
-            x_buf[at : at + rows, k * LANES : (k + 1) * LANES] = x_ref[k * rows : (k + 1) * rows]
-        at += rows
+        blocks = [x_ref[k * rows : (k + 1) * rows] for k in range(width // LANES)]
+        parts.append(jnp.concatenate(blocks, axis=1))
+    x_buf[...] = jnp.concatenate(parts)
     route = x_refs[0][x_refs[0].shape[0] - WEIGHT_ROWS :].astype(jnp.float32)
     columns = []
     for row in (steps, steps ^ CORE):
@@ -243,14 +243,14 @@
             up = jnp.dot(x, w_up[:, f : f + 256], preferred_element_type=jnp.float32)
             act = (gate / (1.0 + jnp.exp(-gate)) * up).astype(jnp.bfloat16)
             h_buf[:, e * hidden + f : e * hidden + f + 256] = act
-    for c in range(0, width, 512):
+    for c in range(0, width, 1024):
         out = None
         for e in range(2):
             act = h_buf[:, e * hidden : (e + 1) * hidden]
-            part = jnp.dot(act, weights[3 * e + 2][:, c : c + 512], preferred_element_type=jnp.float32)
+            part = jnp.dot(act, weights[3 * e + 2][:, c : c + 1024], preferred_element_type=jnp.float32)
             part = columns[e] * part
             out = part if out is None else out + part
-        o_ref[:, c : c + 512] = out.astype(jnp.bfloat16)
+        o_ref[:, c : c + 1024] = out.astype(jnp.bfloat16)
 
 
 def ffn(blocks, steps, *, width, weights):

time: 42 us -> 41.9 us (level)
  Pallas kernels: 17.6 us -> 17.1 us
  waiting for transfers between devices: 11.6 us -> 12.1 us
    ppermute x11, waiting for transfers between devices: 11.6 us -> 12.1 us  [hop(): return lax.ppermute(block, AXIS, pairs)]
    pallas_call x4, Pallas kernels: 11.6 us -> 11.1 us  [ffn(): pl.pallas_call(functools.partial(ffn_body, steps, len(blocks)), out_shape...]
  transfers between devices with their start and end apart: 11 -> 11, of which waited for: 6 -> 6; matrix products, arithmetic and copies ran while one was open for 0% -> 0% of each run, Pallas kernels for 40% -> 39%
where the time goes in v5:
time: 41.9 us; the launch traced here: 41.5 us
  Pallas kernels  17.1 us (41%)
  starting transfers between devices  12.2 us (29%)
  waiting for transfers between devices  12.1 us (29%)
    ppermute x11, starting transfers between devices, hop(): return lax.ppermute(block, AXIS, pairs)  12.2 us
    ppermute x11, waiting for transfers between devices, hop(): return lax.ppermute(block, AXIS, pairs)  12.1 us
    pallas_call x4, Pallas kernels, ffn(): pl.pallas_call(functools.partial(ffn_body, steps, len(blocks)), out_shape...  11.1 us
    pallas_call x1, Pallas kernels, fetch(): pl.pallas_call(functools.partial(fetch_body, n), out_shape=[vmem_out(a.sh...  3.78 us
    pallas_call x1, Pallas kernels, label(): pl.pallas_call(label_body, out_shape=[vmem_out((length, LANES)) for lengt...  1.25 us
    pallas_call x1, Pallas kernels, finish(): pl.pallas_call(finish_body, out_shape=jax.ShapeDtypeStruct(shape, jnp.bfl...  0.85 us
  transfers between devices with their start and end apart: 11, of which 6 were waited for; matrix products, arithmetic and copies ran while one was open for 0% of the time, Pallas kernels for 39%

profile of v5, /device:TPU:0, one launch (start us, length us, event | category | flops | bytes accessed | tf_op | source)
XLA Modules:
  0.0 41.5 jit_solution(15283146891807949296)
XLA Ops:
  0.0 0.5 %collective-permute-start.2 = (bf16[2048,768]{1,0:T(8,128)(2,1)}, bf16[2048,768]{1,0:T(8,128)(2,1)S(1)}, u32[]{:S(2)}, u32[]{:S(2)}) collective-permute-start(bf16[2048,768]{1,0:T(8,128)(2,1)} %bitcast.5), channel_id=1, source_target_pairs={{0,4},{4,0},{8,12},{12,8},{16,20},{20,16},{24,28},{28,24},{1,5},{5... | collective-permute-start | bytes 9437192 | tf_op jit(solution)/shard_map/ppermute | solution.py:68
  0.5 1.3 %shard_map.64 = (bf16[1040,128]{1,0:T(8,128)(2,1)S(1)}, bf16[1040,128]{1,0:T(8,128)(2,1)S(1)}, bf16[2064,128]{1,0:T(8,128)(2,1)S(1)}) custom-call(bf16[128,2048]{1,0:T(8,128)(2,1)} %tokens_ref.1, s32[4,128]{1,0:T(4,128)} %bitcast.11, bf16[4,128]{1,0:T(4,128)(2,1)} %bitcast.12), custom_call_target="tpu_custom_call" | custom-call | tf_op jit(solution)/shard_map/pallas_call | solution.py:124
  1.7 2.6 %collective-permute-start = (bf16[1040,128]{1,0:T(8,128)(2,1)S(1)}, bf16[1040,128]{1,0:T(8,128)(2,1)S(1)}, u32[]{:S(2)}, u32[]{:S(2)}) collective-permute-start(bf16[1040,128]{1,0:T(8,128)(2,1)S(1)} %get-tuple-element.20), channel_id=1, source_target_pairs={{0,8},{4,20},{8,0},{12,28},{16,24},{20,4},{24,16},{28,12},{1,9},{5... | collective-permute-start | bytes 798728 | tf_op jit(solution)/shard_map/ppermute | solution.py:68
  4.3 0.1 collective-permute-start.1
  4.3 0.3 collective-permute-start.6
  4.6 0.3 collective-permute-start.7
  4.9 3.8 %shard_map.65 = (bf16[2048,768]{1,0:T(8,128)(2,1)S(1)}, bf16[2048,768]{1,0:T(8,128)(2,1)S(1)}, bf16[768,2048]{1,0:T(8,128)(2,1)S(1)}) custom-call(bf16[2048,768]{1,0:T(8,128)(2,1)} %bitcast.6, bf16[2048,768]{1,0:T(8,128)(2,1)} %bitcast.8, bf16[768,2048]{1,0:T(8,128)(2,1)} %bitcast.10), custom_call_target="tpu_custom_call" | custom-call | bytes 18874368 | tf_op jit(solution)/shard_map/pallas_call | solution.py:211
  8.6 0.0 collective-permute-done.refs_0_
  8.7 2.0 %collective-permute-start.4 = (bf16[1040,128]{1,0:T(8,128)(2,1)S(1)}, bf16[1040,128]{1,0:T(8,128)(2,1)S(1)}, u32[]{:S(2)}, u32[]{:S(2)}) collective-permute-start(bf16[1040,128]{1,0:T(8,128)(2,1)S(1)} %collective-permute-done.refs_0_), channel_id=1, source_target_pairs={{0,16},{4,12},{8,24},{12,4},{16,0},{20,28},{24,8},{28,20},{1,17},{... | collective-permute-start | bytes 798728 | tf_op jit(solution)/shard_map/ppermute | solution.py:68
  10.7 0.8 %collective-permute-done.1.refs_1_ = bf16[1040,128]{1,0:T(8,128)(2,1)S(1)} collective-permute-done((bf16[1040,128]{1,0:T(8,128)(2,1)S(1)}, bf16[1040,128]{1,0:T(8,128)(2,1)S(1)}, u32[]{:S(2)}, u32[]{:S(2)}) %collective-permute-start.1) | collective-permute-done | bytes 266272 | tf_op jit(solution)/shard_map/ppermute | solution.py:68
  11.5 2.3 %collective-permute-start.5 = (bf16[1040,128]{1,0:T(8,128)(2,1)S(1)}, bf16[1040,128]{1,0:T(8,128)(2,1)S(1)}, u32[]{:S(2)}, u32[]{:S(2)}) collective-permute-start(bf16[1040,128]{1,0:T(8,128)(2,1)S(1)} %collective-permute-done.1.refs_1_), channel_id=1, source_target_pairs={{0,16},{4,12},{8,24},{12,4},{16,0},{20,28},{24,8},{28,20},{1,17},{... | collective-permute-start | bytes 798728 | tf_op jit(solution)/shard_map/ppermute | solution.py:68
  13.8 0.0 collective-permute-done.2.refs_5_.refs_4_
  13.8 0.0 collective-permute-start.3
  13.8 1.3 %collective-permute-done.4.refs_0_ = bf16[1040,128]{1,0:T(8,128)(2,1)S(1)} collective-permute-done((bf16[1040,128]{1,0:T(8,128)(2,1)S(1)}, bf16[1040,128]{1,0:T(8,128)(2,1)S(1)}, u32[]{:S(2)}, u32[]{:S(2)}) %collective-permute-start.4) | collective-permute-done | bytes 266272 | tf_op jit(solution)/shard_map/ppermute | solution.py:68
  15.1 3.0 %collective-permute-done.5.refs_1_ = bf16[1040,128]{1,0:T(8,128)(2,1)S(1)} collective-permute-done((bf16[1040,128]{1,0:T(8,128)(2,1)S(1)}, bf16[1040,128]{1,0:T(8,128)(2,1)S(1)}, u32[]{:S(2)}, u32[]{:S(2)}) %collective-permute-start.5) | collective-permute-done | bytes 266272 | tf_op jit(solution)/shard_map/ppermute | solution.py:68
  18.2 0.0 collective-permute-done.6.refs_6_.refs_5_
  18.2 0.0 collective-permute-done.7.refs_7_.refs_6_
  18.2 2.8 %shard_map.67 = bf16[128,2048]{1,0:T(8,128)(2,1)S(1)} custom-call(bf16[1040,128]{1,0:T(8,128)(2,1)S(1)} %get-tuple-element.26.refs_0_, bf16[1040,128]{1,0:T(8,128)(2,1)S(1)} %get-tuple-element.27.refs_1_, bf16[2048,768]{1,0:T(8,128)(2,1)S(1)} %get-tuple-element.21.refs_2_.refs_1_, bf16[2048,768]{1,0:T(8,128)(2,1)S(1)} %get-tuple-element.28.refs_3_.refs_2_, ...), custom_call_target="tpu_custom_call" | custom-call | flops 2415919104 | bytes 19922944 | tf_op jit(solution)/shard_map/pallas_call | solution.py:259
  21.0 2.1 %collective-permute-start.8 = (bf16[128,2048]{1,0:T(8,128)(2,1)S(1)}, bf16[128,2048]{1,0:T(8,128)(2,1)S(1)}, u32[]{:S(2)}, u32[]{:S(2)}) collective-permute-start(bf16[128,2048]{1,0:T(8,128)(2,1)S(1)} %shard_map.67), channel_id=1, source_target_pairs={{0,8},{4,20},{8,0},{12,28},{16,24},{20,4},{24,16},{28,12},{1,9},{5... | collective-permute-start | bytes 1572872 | tf_op jit(solution)/shard_map/ppermute | solution.py:68
  23.1 2.8 %shard_map.68 = bf16[128,2048]{1,0:T(8,128)(2,1)S(1)} custom-call(bf16[1040,128]{1,0:T(8,128)(2,1)S(1)} %collective-permute-done.refs_0_, bf16[1040,128]{1,0:T(8,128)(2,1)S(1)} %collective-permute-done.1.refs_1_, bf16[2048,768]{1,0:T(8,128)(2,1)S(1)} %get-tuple-element.21.refs_2_.refs_1_, bf16[2048,768]{1,0:T(8,128)(2,1)S(1)} %get-tuple-element.28.refs_3_.refs_2_, ...), custom_call_target="tpu_custom_call" | custom-call | flops 2415919104 | bytes 19922944 | tf_op jit(solution)/shard_map/pallas_call | solution.py:259
  25.9 0.1 collective-permute-start.9
  26.0 0.0 collective-permute-done.3.refs_0_
  26.0 2.7 %shard_map.69 = bf16[128,2048]{1,0:T(8,128)(2,1)S(1)} custom-call(bf16[2064,128]{1,0:T(8,128)(2,1)S(1)} %collective-permute-done.3.refs_0_, bf16[2048,768]{1,0:T(8,128)(2,1)S(1)} %get-tuple-element.21.refs_2_.refs_1_, bf16[2048,768]{1,0:T(8,128)(2,1)S(1)} %get-tuple-element.28.refs_3_.refs_2_, bf16[768,2048]{1,0:T(8,128)(2,1)S(1)} %get-tuple-element.29.refs_4_.refs_3_, ...), custom_call_target="tpu_custom_call" | custom-call | flops 2415919104 | bytes 19922944 | tf_op jit(solution)/shard_map/pallas_call | solution.py:259
  28.7 1.6 %collective-permute-done.8 = bf16[128,2048]{1,0:T(8,128)(2,1)S(1)} collective-permute-done((bf16[128,2048]{1,0:T(8,128)(2,1)S(1)}, bf16[128,2048]{1,0:T(8,128)(2,1)S(1)}, u32[]{:S(2)}, u32[]{:S(2)}) %collective-permute-start.8) | collective-permute-done | bytes 524320 | tf_op jit(solution)/shard_map/ppermute | solution.py:68
  30.3 0.1 add_convert_fusion
  30.4 2.1 %collective-permute-start.10 = (bf16[128,2048]{1,0:T(8,128)(2,1)S(1)}, bf16[128,2048]{1,0:T(8,128)(2,1)S(1)}, u32[]{:S(2)}, u32[]{:S(2)}) collective-permute-start(bf16[128,2048]{1,0:T(8,128)(2,1)S(1)} %add_convert_fusion), channel_id=1, source_target_pairs={{0,16},{4,12},{8,24},{12,4},{16,0},{20,28},{24,8},{28,20},{1,17},{... | collective-permute-start | bytes 1572872 | tf_op jit(solution)/shard_map/ppermute | solution.py:68
  32.5 2.7 %shard_map.70.a_ref = bf16[128,2048]{1,0:T(8,128)(2,1)S(1)} custom-call(bf16[2064,128]{1,0:T(8,128)(2,1)S(1)} %get-tuple-element.32.refs_0_, bf16[2048,768]{1,0:T(8,128)(2,1)S(1)} %get-tuple-element.21.refs_2_.refs_1_, bf16[2048,768]{1,0:T(8,128)(2,1)S(1)} %get-tuple-element.28.refs_3_.refs_2_, bf16[768,2048]{1,0:T(8,128)(2,1)S(1)} %get-tuple-element.29.refs_4_.refs_3_, ...), custom_call_target="tpu_custom_call" | custom-call | flops 2415919104 | bytes 19922944 | tf_op jit(solution)/shard_map/pallas_call | solution.py:259
  35.3 3.9 %collective-permute-done.9.b_ref = bf16[128,2048]{1,0:T(8,128)(2,1)S(1)} collective-permute-done((bf16[128,2048]{1,0:T(8,128)(2,1)S(1)}, bf16[128,2048]{1,0:T(8,128)(2,1)S(1)}, u32[]{:S(2)}, u32[]{:S(2)}) %collective-permute-start.9) | collective-permute-done | bytes 524320 | tf_op jit(solution)/shard_map/ppermute | solution.py:68
  39.1 0.1 shard_map.71.refs_0_
  39.2 1.5 %collective-permute-done.10.refs_1_ = bf16[128,2048]{1,0:T(8,128)(2,1)S(1)} collective-permute-done((bf16[128,2048]{1,0:T(8,128)(2,1)S(1)}, bf16[128,2048]{1,0:T(8,128)(2,1)S(1)}, u32[]{:S(2)}, u32[]{:S(2)}) %collective-permute-start.10) | collective-permute-done | bytes 524320 | tf_op jit(solution)/shard_map/ppermute | solution.py:68
  40.7 0.9 %shard_map.72 = bf16[128,2048]{1,0:T(8,128)(2,1)} custom-call(f32[128,2048]{1,0:T(8,128)S(1)} %shard_map.71.refs_0_, bf16[128,2048]{1,0:T(8,128)(2,1)S(1)} %collective-permute-done.10.refs_1_), custom_call_target="tpu_custom_call" | custom-call | tf_op jit(solution)/shard_map/pallas_call | solution.py:155
  (1 shorter events, 0.0 us)
Async XLA Ops:
  0.0 13.8 %collective-permute-start.2 = (bf16[2048,768]{1,0:T(8,128)(2,1)}, bf16[2048,768]{1,0:T(8,128)(2,1)S(1)}, u32[]{:S(2)}, u32[]{:S(2)}) collective-permute-start(bf16[2048,768]{1,0:T(8,128)(2,1)} %bitcast.5), channel_id=1, source_target_pairs={{0,4},{4,0},{8,12},{12,8},{16,20},{20,16},{24,28},{28,24},{1,5},{5... | collective-permute-start | bytes 9437192 | tf_op jit(solution)/shard_map/ppermute | solution.py:68
  1.7 7.0 %collective-permute-start = (bf16[1040,128]{1,0:T(8,128)(2,1)S(1)}, bf16[1040,128]{1,0:T(8,128)(2,1)S(1)}, u32[]{:S(2)}, u32[]{:S(2)}) collective-permute-start(bf16[1040,128]{1,0:T(8,128)(2,1)S(1)} %get-tuple-element.20), channel_id=1, source_target_pairs={{0,8},{4,20},{8,0},{12,28},{16,24},{20,4},{24,16},{28,12},{1,9},{5... | collective-permute-start | bytes 798728 | tf_op jit(solution)/shard_map/ppermute | solution.py:68
  4.3 7.2 %collective-permute-start.1 = (bf16[1040,128]{1,0:T(8,128)(2,1)S(1)}, bf16[1040,128]{1,0:T(8,128)(2,1)S(1)}, u32[]{:S(2)}, u32[]{:S(2)}) collective-permute-start(bf16[1040,128]{1,0:T(8,128)(2,1)S(1)} %get-tuple-element.23), channel_id=1, source_target_pairs={{0,8},{4,20},{8,0},{12,28},{16,24},{20,4},{24,16},{28,12},{1,9},{5... | collective-permute-start | bytes 798728 | tf_op jit(solution)/shard_map/ppermute | solution.py:68
  4.3 13.9 %collective-permute-start.6 = (bf16[2048,768]{1,0:T(8,128)(2,1)}, bf16[2048,768]{1,0:T(8,128)(2,1)S(1)}, u32[]{:S(2)}, u32[]{:S(2)}) collective-permute-start(bf16[2048,768]{1,0:T(8,128)(2,1)} %bitcast.7), channel_id=1, source_target_pairs={{0,4},{4,0},{8,12},{12,8},{16,20},{20,16},{24,28},{28,24},{1,5},{5... | collective-permute-start | bytes 9437192 | tf_op jit(solution)/shard_map/ppermute | solution.py:68
  4.6 13.6 %collective-permute-start.7 = (bf16[768,2048]{1,0:T(8,128)(2,1)}, bf16[768,2048]{1,0:T(8,128)(2,1)S(1)}, u32[]{:S(2)}, u32[]{:S(2)}) collective-permute-start(bf16[768,2048]{1,0:T(8,128)(2,1)} %bitcast.9), channel_id=1, source_target_pairs={{0,4},{4,0},{8,12},{12,8},{16,20},{20,16},{24,28},{28,24},{1,5},{5... | collective-permute-start | bytes 9437192 | tf_op jit(solution)/shard_map/ppermute | solution.py:68
  8.7 6.5 %collective-permute-start.4 = (bf16[1040,128]{1,0:T(8,128)(2,1)S(1)}, bf16[1040,128]{1,0:T(8,128)(2,1)S(1)}, u32[]{:S(2)}, u32[]{:S(2)}) collective-permute-start(bf16[1040,128]{1,0:T(8,128)(2,1)S(1)} %collective-permute-done.refs_0_), channel_id=1, source_target_pairs={{0,16},{4,12},{8,24},{12,4},{16,0},{20,28},{24,8},{28,20},{1,17},{... | collective-permute-start | bytes 798728 | tf_op jit(solution)/shard_map/ppermute | solution.py:68
  11.5 6.6 %collective-permute-start.5 = (bf16[1040,128]{1,0:T(8,128)(2,1)S(1)}, bf16[1040,128]{1,0:T(8,128)(2,1)S(1)}, u32[]{:S(2)}, u32[]{:S(2)}) collective-permute-start(bf16[1040,128]{1,0:T(8,128)(2,1)S(1)} %collective-permute-done.1.refs_1_), channel_id=1, source_target_pairs={{0,16},{4,12},{8,24},{12,4},{16,0},{20,28},{24,8},{28,20},{1,17},{... | collective-permute-start | bytes 798728 | tf_op jit(solution)/shard_map/ppermute | solution.py:68
  13.8 12.2 %collective-permute-start.3 = (bf16[2064,128]{1,0:T(8,128)(2,1)S(1)}, bf16[2064,128]{1,0:T(8,128)(2,1)S(1)}, u32[]{:S(2)}, u32[]{:S(2)}) collective-permute-start(bf16[2064,128]{1,0:T(8,128)(2,1)S(1)} %get-tuple-element.32.refs_0_), channel_id=1, source_target_pairs={{0,16},{4,12},{8,24},{12,4},{16,0},{20,28},{24,8},{28,20},{1,17},{... | collective-permute-start | bytes 1585160 | tf_op jit(solution)/shard_map/ppermute | solution.py:68
  21.0 9.2 %collective-permute-start.8 = (bf16[128,2048]{1,0:T(8,128)(2,1)S(1)}, bf16[128,2048]{1,0:T(8,128)(2,1)S(1)}, u32[]{:S(2)}, u32[]{:S(2)}) collective-permute-start(bf16[128,2048]{1,0:T(8,128)(2,1)S(1)} %shard_map.67), channel_id=1, source_target_pairs={{0,8},{4,20},{8,0},{12,28},{16,24},{20,4},{24,16},{28,12},{1,9},{5... | collective-permute-start | bytes 1572872 | tf_op jit(solution)/shard_map/ppermute | solution.py:68
  25.9 13.2 %collective-permute-start.9 = (bf16[128,2048]{1,0:T(8,128)(2,1)S(1)}, bf16[128,2048]{1,0:T(8,128)(2,1)S(1)}, u32[]{:S(2)}, u32[]{:S(2)}) collective-permute-start(bf16[128,2048]{1,0:T(8,128)(2,1)S(1)} %shard_map.68), channel_id=1, source_target_pairs={{0,8},{4,20},{8,0},{12,28},{16,24},{20,4},{24,16},{28,12},{1,9},{5... | collective-permute-start | bytes 1572872 | tf_op jit(solution)/shard_map/ppermute | solution.py:68
  30.4 10.3 %collective-permute-start.10 = (bf16[128,2048]{1,0:T(8,128)(2,1)S(1)}, bf16[128,2048]{1,0:T(8,128)(2,1)S(1)}, u32[]{:S(2)}, u32[]{:S(2)}) collective-permute-start(bf16[128,2048]{1,0:T(8,128)(2,1)S(1)} %add_convert_fusion), channel_id=1, source_target_pairs={{0,16},{4,12},{8,24},{12,4},{16,0},{20,28},{24,8},{28,20},{1,17},{... | collective-permute-start | bytes 1572872 | tf_op jit(solution)/shard_map/ppermute | solution.py:68

commit v6 on v5

--- a/solution.py
+++ b/solution.py
@@ -85,13 +85,17 @@
 
 
 def parts_of(rows):
-    return slice(0, rows // 2), slice(rows // 2, rows), slice(0, rows)
+    return slice(0, rows // 2), slice(rows // 2, rows)
 
 
 def label_body(tokens_ref, ids_ref, gates_ref, *refs):
     *out_refs, buf, ids_buf, gates_buf, sem = refs
     rows, width = buf.shape
-    pairs = [(ids_ref, ids_buf), (gates_ref, gates_buf), (tokens_ref, buf)]
+    parts = parts_of(rows)
+    pairs = [(ids_ref, ids_buf), (gates_ref, gates_buf)]
+    for part in parts:
+        at = pl.ds(part.start, part.stop - part.start)
+        pairs.append((tokens_ref.at[at], buf.at[at]))
     copies = [pltpu.make_async_copy(src, dst, sem.at[k]) for k, (src, dst) in enumerate(pairs)]
     for copy in copies:
         copy.start()
@@ -109,9 +113,9 @@
     route = route.astype(jnp.bfloat16)
     for out_ref in out_refs:
         out_ref[out_ref.shape[0] - WEIGHT_ROWS :] = route
-    copies[2].wait()
-    for out_ref, part in zip(out_refs, parts_of(rows)):
+    for out_ref, part, copy in zip(out_refs, parts, copies[2:]):
         size = part.stop - part.start
+        copy.wait()
         for k in range(width // LANES):
             out_ref[k * size : (k + 1) * size] = buf[part, k * LANES : (k + 1) * LANES]
 
@@ -127,7 +131,7 @@
         in_specs=[ANY_SPEC] * 3,
         out_specs=[VMEM_SPEC] * len(parts),
         scratch_shapes=[pltpu.VMEM(a.shape, a.dtype) for a in arrays]
-        + [pltpu.SemaphoreType.DMA((3,))],
+        + [pltpu.SemaphoreType.DMA((2 + len(parts),))],
         compiler_params=pltpu.CompilerParams(vmem_limit_bytes=8 * MIB),
     )(*[pltpu.with_memory_space_constraint(a, pltpu.HBM) for a in arrays])
 
@@ -197,28 +201,39 @@
     )(in_vmem(a), in_vmem(b))
 
 
-def fetch_body(n, *refs):
-    outs, sem = refs[-n - 1 : -1], refs[-1]
-    copies = [pltpu.make_async_copy(refs[k], outs[k], sem.at[k]) for k in range(n)]
+def fetch_body(n, blocks, *refs):
+    arrays, parts, outs, whole, sem = refs[:n], refs[n:-n - 2], refs[-n - 2 : -2], refs[-2], refs[-1]
+    copies = [pltpu.make_async_copy(arrays[k], outs[k], sem.at[k]) for k in range(n)]
     for copy in copies:
         copy.start()
+    sizes = [(part.shape[0] - WEIGHT_ROWS) // blocks for part in parts]
+    for k in range(blocks):
+        at = k * sum(sizes)
+        for part, size in zip(parts, sizes):
+            whole[at : at + size] = part[k * size : (k + 1) * size]
+            at += size
+    whole[blocks * sum(sizes) :] = parts[0][blocks * sizes[0] :]
     for copy in copies:
         copy.wait()
 
 
-def fetch(arrays):
+def fetch(arrays, parts, width):
     n = len(arrays)
-    return pl.pallas_call(
-        functools.partial(fetch_body, n),
-        out_shape=[vmem_out(a.shape) for a in arrays],
-        in_specs=[ANY_SPEC] * n,
-        out_specs=[VMEM_SPEC] * n,
+    length = sum(part.shape[0] - WEIGHT_ROWS for part in parts) + WEIGHT_ROWS
+    return pl.pallas_call(
+        functools.partial(fetch_body, n, width // LANES),
+        out_shape=[vmem_out(a.shape) for a in arrays] + [vmem_out((length, LANES))],
+        in_specs=[ANY_SPEC] * n + [VMEM_SPEC] * len(parts),
+        out_specs=[VMEM_SPEC] * (n + 1),
         scratch_shapes=[pltpu.SemaphoreType.DMA((n,))],
         compiler_params=pltpu.CompilerParams(vmem_limit_bytes=8 * MIB),
         cost_estimate=pl.CostEstimate(
             flops=0, bytes_accessed=4 * sum(a.size for a in arrays), transcendentals=0
         ),
-    )(*[pltpu.with_memory_space_constraint(a, pltpu.HBM) for a in arrays])
+    )(
+        *[pltpu.with_memory_space_constraint(a, pltpu.HBM) for a in arrays],
+        *[in_vmem(part) for part in parts],
+    )
 
 
 def ffn_body(steps, n, *refs):
@@ -276,11 +291,11 @@
 
 def two_by_two(tokens, expert_ids, gate_weights, w_gate, w_up, w_down):
     width = tokens.shape[1]
-    *halves, home = label(tokens, expert_ids, gate_weights)
+    halves = label(tokens, expert_ids, gate_weights)
 
     near = [hop(half, FIRST) for half in halves]
     own = (w_gate[0], w_up[0], w_down[0])
-    fetched = fetch(own)
+    *fetched, home = fetch(own, halves, width)
     swapped = [hop(w, CORE) for w in own]
     near = [after(half, fetched[0]) for half in near]
     far = stage([hop(half, SECOND) for half in near], 28000000000)

time: 41.9 us -> 41.7 us (level)
  no operation moved by 1% of the time
where the time goes in v6:
time: 41.7 us; the launch traced here: 41.4 us
  Pallas kernels  17 us (41%)
  starting transfers between devices  12.2 us (29%)
  waiting for transfers between devices  12.1 us (29%)
    ppermute x11, starting transfers between devices, hop(): return lax.ppermute(block, AXIS, pairs)  12.2 us
    ppermute x11, waiting for transfers between devices, hop(): return lax.ppermute(block, AXIS, pairs)  12.1 us
    pallas_call x4, Pallas kernels, ffn(): pl.pallas_call(functools.partial(ffn_body, steps, len(blocks)), out_shape...  11.1 us
    pallas_call x1, Pallas kernels, fetch(): pl.pallas_call(functools.partial(fetch_body, n, width // LANES), out_shap...  3.78 us
    pallas_call x1, Pallas kernels, label(): pl.pallas_call(label_body, out_shape=[vmem_out((length, LANES)) for lengt...  1.14 us
    pallas_call x1, Pallas kernels, finish(): pl.pallas_call(finish_body, out_shape=jax.ShapeDtypeStruct(shape, jnp.bfl...  0.85 us
  transfers between devices with their start and end apart: 11, of which 6 were waited for; matrix products, arithmetic and copies ran while one was open for 0% of the time, Pallas kernels for 39%

profile of v6, /device:TPU:0, one launch (start us, length us, event | category | flops | bytes accessed | tf_op | source)
XLA Modules:
  0.0 41.4 jit_solution(8440205767974735245)
XLA Ops:
  0.0 0.5 %collective-permute-start.2 = (bf16[2048,768]{1,0:T(8,128)(2,1)}, bf16[2048,768]{1,0:T(8,128)(2,1)S(1)}, u32[]{:S(2)}, u32[]{:S(2)}) collective-permute-start(bf16[2048,768]{1,0:T(8,128)(2,1)} %bitcast.5), channel_id=1, source_target_pairs={{0,4},{4,0},{8,12},{12,8},{16,20},{20,16},{24,28},{28,24},{1,5},{5... | collective-permute-start | bytes 9437192 | tf_op jit(solution)/shard_map/ppermute | solution.py:68
  0.5 1.1 %shard_map.64 = (bf16[1040,128]{1,0:T(8,128)(2,1)S(1)}, bf16[1040,128]{1,0:T(8,128)(2,1)S(1)}) custom-call(bf16[128,2048]{1,0:T(8,128)(2,1)} %tokens_ref.1, s32[4,128]{1,0:T(4,128)} %bitcast.11, bf16[4,128]{1,0:T(4,128)(2,1)} %bitcast.12), custom_call_target="tpu_custom_call" | custom-call | tf_op jit(solution)/shard_map/pallas_call | solution.py:128
  1.6 2.6 %collective-permute-start.1 = (bf16[1040,128]{1,0:T(8,128)(2,1)S(1)}, bf16[1040,128]{1,0:T(8,128)(2,1)S(1)}, u32[]{:S(2)}, u32[]{:S(2)}) collective-permute-start(bf16[1040,128]{1,0:T(8,128)(2,1)S(1)} %get-tuple-element.20.refs_4_), channel_id=1, source_target_pairs={{0,8},{4,20},{8,0},{12,28},{16,24},{20,4},{24,16},{28,12},{1,9},{5... | collective-permute-start | bytes 798728 | tf_op jit(solution)/shard_map/ppermute | solution.py:68
  4.2 0.1 collective-permute-start
  4.2 0.3 collective-permute-start.6
  4.5 0.3 collective-permute-start.7
  4.7 3.8 %shard_map.65 = (bf16[2048,768]{1,0:T(8,128)(2,1)S(1)}, bf16[2048,768]{1,0:T(8,128)(2,1)S(1)}, bf16[768,2048]{1,0:T(8,128)(2,1)S(1)}, bf16[2064,128]{1,0:T(8,128)(2,1)S(1)}) custom-call(bf16[2048,768]{1,0:T(8,128)(2,1)} %bitcast.6, bf16[2048,768]{1,0:T(8,128)(2,1)} %bitcast.8, bf16[768,2048]{1,0:T(8,128)(2,1)} %bitcast.10, ...), custom_call_target="tpu_custom_call" | custom-call | bytes 18874368 | tf_op jit(solution)/shard_map/pallas_call | solution.py:223
  8.5 0.0 collective-permute-done.1.refs_1_
  8.6 2.0 %collective-permute-start.5 = (bf16[1040,128]{1,0:T(8,128)(2,1)S(1)}, bf16[1040,128]{1,0:T(8,128)(2,1)S(1)}, u32[]{:S(2)}, u32[]{:S(2)}) collective-permute-start(bf16[1040,128]{1,0:T(8,128)(2,1)S(1)} %collective-permute-done.1.refs_1_), channel_id=1, source_target_pairs={{0,16},{4,12},{8,24},{12,4},{16,0},{20,28},{24,8},{28,20},{1,17},{... | collective-permute-start | bytes 798728 | tf_op jit(solution)/shard_map/ppermute | solution.py:68
  10.6 0.8 %collective-permute-done.refs_0_ = bf16[1040,128]{1,0:T(8,128)(2,1)S(1)} collective-permute-done((bf16[1040,128]{1,0:T(8,128)(2,1)S(1)}, bf16[1040,128]{1,0:T(8,128)(2,1)S(1)}, u32[]{:S(2)}, u32[]{:S(2)}) %collective-permute-start) | collective-permute-done | bytes 266272 | tf_op jit(solution)/shard_map/ppermute | solution.py:68
  11.4 2.3 %collective-permute-start.4 = (bf16[1040,128]{1,0:T(8,128)(2,1)S(1)}, bf16[1040,128]{1,0:T(8,128)(2,1)S(1)}, u32[]{:S(2)}, u32[]{:S(2)}) collective-permute-start(bf16[1040,128]{1,0:T(8,128)(2,1)S(1)} %collective-permute-done.refs_0_), channel_id=1, source_target_pairs={{0,16},{4,12},{8,24},{12,4},{16,0},{20,28},{24,8},{28,20},{1,17},{... | collective-permute-start | bytes 798728 | tf_op jit(solution)/shard_map/ppermute | solution.py:68
  13.7 0.0 collective-permute-done.2.refs_5_.refs_4_
  13.7 0.0 collective-permute-start.3
  13.7 1.3 %collective-permute-done.5.refs_1_ = bf16[1040,128]{1,0:T(8,128)(2,1)S(1)} collective-permute-done((bf16[1040,128]{1,0:T(8,128)(2,1)S(1)}, bf16[1040,128]{1,0:T(8,128)(2,1)S(1)}, u32[]{:S(2)}, u32[]{:S(2)}) %collective-permute-start.5) | collective-permute-done | bytes 266272 | tf_op jit(solution)/shard_map/ppermute | solution.py:68
  15.0 3.0 %collective-permute-done.4.refs_0_ = bf16[1040,128]{1,0:T(8,128)(2,1)S(1)} collective-permute-done((bf16[1040,128]{1,0:T(8,128)(2,1)S(1)}, bf16[1040,128]{1,0:T(8,128)(2,1)S(1)}, u32[]{:S(2)}, u32[]{:S(2)}) %collective-permute-start.4) | collective-permute-done | bytes 266272 | tf_op jit(solution)/shard_map/ppermute | solution.py:68
  18.1 0.0 collective-permute-done.6.refs_6_.refs_5_
  18.1 0.0 collective-permute-done.7.refs_7_.refs_6_
  18.1 2.7 %shard_map.67 = bf16[128,2048]{1,0:T(8,128)(2,1)S(1)} custom-call(bf16[1040,128]{1,0:T(8,128)(2,1)S(1)} %get-tuple-element.26.refs_0_, bf16[1040,128]{1,0:T(8,128)(2,1)S(1)} %get-tuple-element.27.refs_1_, bf16[2048,768]{1,0:T(8,128)(2,1)S(1)} %get-tuple-element.22.refs_2_.refs_1_, bf16[2048,768]{1,0:T(8,128)(2,1)S(1)} %get-tuple-element.28.refs_3_.refs_2_, ...), custom_call_target="tpu_custom_call" | custom-call | flops 2415919104 | bytes 19922944 | tf_op jit(solution)/shard_map/pallas_call | solution.py:274
  20.8 2.1 %collective-permute-start.8 = (bf16[128,2048]{1,0:T(8,128)(2,1)S(1)}, bf16[128,2048]{1,0:T(8,128)(2,1)S(1)}, u32[]{:S(2)}, u32[]{:S(2)}) collective-permute-start(bf16[128,2048]{1,0:T(8,128)(2,1)S(1)} %shard_map.67), channel_id=1, source_target_pairs={{0,8},{4,20},{8,0},{12,28},{16,24},{20,4},{24,16},{28,12},{1,9},{5... | collective-permute-start | bytes 1572872 | tf_op jit(solution)/shard_map/ppermute | solution.py:68
  22.9 2.7 %shard_map.68 = bf16[128,2048]{1,0:T(8,128)(2,1)S(1)} custom-call(bf16[1040,128]{1,0:T(8,128)(2,1)S(1)} %collective-permute-done.refs_0_, bf16[1040,128]{1,0:T(8,128)(2,1)S(1)} %collective-permute-done.1.refs_1_, bf16[2048,768]{1,0:T(8,128)(2,1)S(1)} %get-tuple-element.22.refs_2_.refs_1_, bf16[2048,768]{1,0:T(8,128)(2,1)S(1)} %get-tuple-element.28.refs_3_.refs_2_, ...), custom_call_target="tpu_custom_call" | custom-call | flops 2415919104 | bytes 19922944 | tf_op jit(solution)/shard_map/pallas_call | solution.py:274
  25.7 0.1 collective-permute-start.9
  25.8 0.0 collective-permute-done.3.refs_0_
  25.8 2.8 %shard_map.69 = bf16[128,2048]{1,0:T(8,128)(2,1)S(1)} custom-call(bf16[2064,128]{1,0:T(8,128)(2,1)S(1)} %collective-permute-done.3.refs_0_, bf16[2048,768]{1,0:T(8,128)(2,1)S(1)} %get-tuple-element.22.refs_2_.refs_1_, bf16[2048,768]{1,0:T(8,128)(2,1)S(1)} %get-tuple-element.28.refs_3_.refs_2_, bf16[768,2048]{1,0:T(8,128)(2,1)S(1)} %get-tuple-element.29.refs_4_.refs_3_, ...), custom_call_target="tpu_custom_call" | custom-call | flops 2415919104 | bytes 19922944 | tf_op jit(solution)/shard_map/pallas_call | solution.py:274
  28.5 1.6 %collective-permute-done.8 = bf16[128,2048]{1,0:T(8,128)(2,1)S(1)} collective-permute-done((bf16[128,2048]{1,0:T(8,128)(2,1)S(1)}, bf16[128,2048]{1,0:T(8,128)(2,1)S(1)}, u32[]{:S(2)}, u32[]{:S(2)}) %collective-permute-start.8) | collective-permute-done | bytes 524320 | tf_op jit(solution)/shard_map/ppermute | solution.py:68
  30.1 0.1 add_convert_fusion
  30.2 2.1 %collective-permute-start.10 = (bf16[128,2048]{1,0:T(8,128)(2,1)S(1)}, bf16[128,2048]{1,0:T(8,128)(2,1)S(1)}, u32[]{:S(2)}, u32[]{:S(2)}) collective-permute-start(bf16[128,2048]{1,0:T(8,128)(2,1)S(1)} %add_convert_fusion), channel_id=1, source_target_pairs={{0,16},{4,12},{8,24},{12,4},{16,0},{20,28},{24,8},{28,20},{1,17},{... | collective-permute-start | bytes 1572872 | tf_op jit(solution)/shard_map/ppermute | solution.py:68
  32.3 2.8 %shard_map.70.a_ref = bf16[128,2048]{1,0:T(8,128)(2,1)S(1)} custom-call(bf16[2064,128]{1,0:T(8,128)(2,1)S(1)} %get-tuple-element.32.refs_0_, bf16[2048,768]{1,0:T(8,128)(2,1)S(1)} %get-tuple-element.22.refs_2_.refs_1_, bf16[2048,768]{1,0:T(8,128)(2,1)S(1)} %get-tuple-element.28.refs_3_.refs_2_, bf16[768,2048]{1,0:T(8,128)(2,1)S(1)} %get-tuple-element.29.refs_4_.refs_3_, ...), custom_call_target="tpu_custom_call" | custom-call | flops 2415919104 | bytes 19922944 | tf_op jit(solution)/shard_map/pallas_call | solution.py:274
  35.1 3.7 %collective-permute-done.9.b_ref = bf16[128,2048]{1,0:T(8,128)(2,1)S(1)} collective-permute-done((bf16[128,2048]{1,0:T(8,128)(2,1)S(1)}, bf16[128,2048]{1,0:T(8,128)(2,1)S(1)}, u32[]{:S(2)}, u32[]{:S(2)}) %collective-permute-start.9) | collective-permute-done | bytes 524320 | tf_op jit(solution)/shard_map/ppermute | solution.py:68
  38.9 0.1 shard_map.71.refs_0_
  39.0 1.6 %collective-permute-done.10.refs_1_ = bf16[128,2048]{1,0:T(8,128)(2,1)S(1)} collective-permute-done((bf16[128,2048]{1,0:T(8,128)(2,1)S(1)}, bf16[128,2048]{1,0:T(8,128)(2,1)S(1)}, u32[]{:S(2)}, u32[]{:S(2)}) %collective-permute-start.10) | collective-permute-done | bytes 524320 | tf_op jit(solution)/shard_map/ppermute | solution.py:68
  40.6 0.9 %shard_map.72 = bf16[128,2048]{1,0:T(8,128)(2,1)} custom-call(f32[128,2048]{1,0:T(8,128)S(1)} %shard_map.71.refs_0_, bf16[128,2048]{1,0:T(8,128)(2,1)S(1)} %collective-permute-done.10.refs_1_), custom_call_target="tpu_custom_call" | custom-call | tf_op jit(solution)/shard_map/pallas_call | solution.py:159
  (1 shorter events, 0.0 us)
Async XLA Ops:
  0.0 13.7 %collective-permute-start.2 = (bf16[2048,768]{1,0:T(8,128)(2,1)}, bf16[2048,768]{1,0:T(8,128)(2,1)S(1)}, u32[]{:S(2)}, u32[]{:S(2)}) collective-permute-start(bf16[2048,768]{1,0:T(8,128)(2,1)} %bitcast.5), channel_id=1, source_target_pairs={{0,4},{4,0},{8,12},{12,8},{16,20},{20,16},{24,28},{28,24},{1,5},{5... | collective-permute-start | bytes 9437192 | tf_op jit(solution)/shard_map/ppermute | solution.py:68
  1.6 7.0 %collective-permute-start.1 = (bf16[1040,128]{1,0:T(8,128)(2,1)S(1)}, bf16[1040,128]{1,0:T(8,128)(2,1)S(1)}, u32[]{:S(2)}, u32[]{:S(2)}) collective-permute-start(bf16[1040,128]{1,0:T(8,128)(2,1)S(1)} %get-tuple-element.20.refs_4_), channel_id=1, source_target_pairs={{0,8},{4,20},{8,0},{12,28},{16,24},{20,4},{24,16},{28,12},{1,9},{5... | collective-permute-start | bytes 798728 | tf_op jit(solution)/shard_map/ppermute | solution.py:68
  4.2 7.2 %collective-permute-start = (bf16[1040,128]{1,0:T(8,128)(2,1)S(1)}, bf16[1040,128]{1,0:T(8,128)(2,1)S(1)}, u32[]{:S(2)}, u32[]{:S(2)}) collective-permute-start(bf16[1040,128]{1,0:T(8,128)(2,1)S(1)} %get-tuple-element.19.refs_3_), channel_id=1, source_target_pairs={{0,8},{4,20},{8,0},{12,28},{16,24},{20,4},{24,16},{28,12},{1,9},{5... | collective-permute-start | bytes 798728 | tf_op jit(solution)/shard_map/ppermute | solution.py:68
  4.2 13.9 %collective-permute-start.6 = (bf16[2048,768]{1,0:T(8,128)(2,1)}, bf16[2048,768]{1,0:T(8,128)(2,1)S(1)}, u32[]{:S(2)}, u32[]{:S(2)}) collective-permute-start(bf16[2048,768]{1,0:T(8,128)(2,1)} %bitcast.7), channel_id=1, source_target_pairs={{0,4},{4,0},{8,12},{12,8},{16,20},{20,16},{24,28},{28,24},{1,5},{5... | collective-permute-start | bytes 9437192 | tf_op jit(solution)/shard_map/ppermute | solution.py:68
  4.5 13.6 %collective-permute-start.7 = (bf16[768,2048]{1,0:T(8,128)(2,1)}, bf16[768,2048]{1,0:T(8,128)(2,1)S(1)}, u32[]{:S(2)}, u32[]{:S(2)}) collective-permute-start(bf16[768,2048]{1,0:T(8,128)(2,1)} %bitcast.9), channel_id=1, source_target_pairs={{0,4},{4,0},{8,12},{12,8},{16,20},{20,16},{24,28},{28,24},{1,5},{5... | collective-permute-start | bytes 9437192 | tf_op jit(solution)/shard_map/ppermute | solution.py:68
  8.6 6.5 %collective-permute-start.5 = (bf16[1040,128]{1,0:T(8,128)(2,1)S(1)}, bf16[1040,128]{1,0:T(8,128)(2,1)S(1)}, u32[]{:S(2)}, u32[]{:S(2)}) collective-permute-start(bf16[1040,128]{1,0:T(8,128)(2,1)S(1)} %collective-permute-done.1.refs_1_), channel_id=1, source_target_pairs={{0,16},{4,12},{8,24},{12,4},{16,0},{20,28},{24,8},{28,20},{1,17},{... | collective-permute-start | bytes 798728 | tf_op jit(solution)/shard_map/ppermute | solution.py:68
  11.4 6.6 %collective-permute-start.4 = (bf16[1040,128]{1,0:T(8,128)(2,1)S(1)}, bf16[1040,128]{1,0:T(8,128)(2,1)S(1)}, u32[]{:S(2)}, u32[]{:S(2)}) collective-permute-start(bf16[1040,128]{1,0:T(8,128)(2,1)S(1)} %collective-permute-done.refs_0_), channel_id=1, source_target_pairs={{0,16},{4,12},{8,24},{12,4},{16,0},{20,28},{24,8},{28,20},{1,17},{... | collective-permute-start | bytes 798728 | tf_op jit(solution)/shard_map/ppermute | solution.py:68
  13.7 12.1 %collective-permute-start.3 = (bf16[2064,128]{1,0:T(8,128)(2,1)S(1)}, bf16[2064,128]{1,0:T(8,128)(2,1)S(1)}, u32[]{:S(2)}, u32[]{:S(2)}) collective-permute-start(bf16[2064,128]{1,0:T(8,128)(2,1)S(1)} %get-tuple-element.32.refs_0_), channel_id=1, source_target_pairs={{0,16},{4,12},{8,24},{12,4},{16,0},{20,28},{24,8},{28,20},{1,17},{... | collective-permute-start | bytes 1585160 | tf_op jit(solution)/shard_map/ppermute | solution.py:68
  20.8 9.2 %collective-permute-start.8 = (bf16[128,2048]{1,0:T(8,128)(2,1)S(1)}, bf16[128,2048]{1,0:T(8,128)(2,1)S(1)}, u32[]{:S(2)}, u32[]{:S(2)}) collective-permute-start(bf16[128,2048]{1,0:T(8,128)(2,1)S(1)} %shard_map.67), channel_id=1, source_target_pairs={{0,8},{4,20},{8,0},{12,28},{16,24},{20,4},{24,16},{28,12},{1,9},{5... | collective-permute-start | bytes 1572872 | tf_op jit(solution)/shard_map/ppermute | solution.py:68
  25.7 13.2 %collective-permute-start.9 = (bf16[128,2048]{1,0:T(8,128)(2,1)S(1)}, bf16[128,2048]{1,0:T(8,128)(2,1)S(1)}, u32[]{:S(2)}, u32[]{:S(2)}) collective-permute-start(bf16[128,2048]{1,0:T(8,128)(2,1)S(1)} %shard_map.68), channel_id=1, source_target_pairs={{0,8},{4,20},{8,0},{12,28},{16,24},{20,4},{24,16},{28,12},{1,9},{5... | collective-permute-start | bytes 1572872 | tf_op jit(solution)/shard_map/ppermute | solution.py:68
  30.2 10.3 %collective-permute-start.10 = (bf16[128,2048]{1,0:T(8,128)(2,1)S(1)}, bf16[128,2048]{1,0:T(8,128)(2,1)S(1)}, u32[]{:S(2)}, u32[]{:S(2)}) collective-permute-start(bf16[128,2048]{1,0:T(8,128)(2,1)S(1)} %add_convert_fusion), channel_id=1, source_target_pairs={{0,16},{4,12},{8,24},{12,4},{16,0},{20,28},{24,8},{28,20},{1,17},{... | collective-permute-start | bytes 1572872 | tf_op jit(solution)/shard_map/ppermute | solution.py:68

commit v7 on v6

--- a/solution.py
+++ b/solution.py
@@ -63,7 +63,7 @@
 
 
 def hop(block, way):
-    bits = {CORE: (CORE, CORE), FIRST: (XBIT, YBIT), SECOND: (YBIT, XBIT)}[way]
+    bits = {CORE: (CORE, CORE), FIRST: (YBIT, XBIT), SECOND: (XBIT, YBIT)}[way]
     pairs = [(i, i ^ bits[i & CORE]) for i in range(lax.axis_size(AXIS))]
     return lax.ppermute(block, AXIS, pairs)
 
@@ -108,7 +108,7 @@
     for k in range(ids_ref.shape[0]):
         away = ids_buf[k : k + 1, :] ^ me
         turned = (away & CORE) | ((away & XBIT) << 1) | ((away & YBIT) >> 1)
-        away = jnp.where(me & CORE == 0, away, turned)
+        away = jnp.where(me & CORE == 0, turned, away)
         route += jnp.where(row == away, gates[k : k + 1, :], 0.0)
     route = route.astype(jnp.bfloat16)
     for out_ref in out_refs:

time: 41.7 us -> 41.7 us (level)
  no operation moved by 1% of the time
where the time goes in v7:
time: 41.7 us; the launch traced here: 41.4 us
  Pallas kernels  17 us (41%)
  starting transfers between devices  12.1 us (29%)
  waiting for transfers between devices  12.1 us (29%)
    ppermute x11, waiting for transfers between devices, hop(): return lax.ppermute(block, AXIS, pairs)  12.1 us
    ppermute x11, starting transfers between devices, hop(): return lax.ppermute(block, AXIS, pairs)  12.1 us
    pallas_call x4, Pallas kernels, ffn(): pl.pallas_call(functools.partial(ffn_body, steps, len(blocks)), out_shape...  11.1 us
    pallas_call x1, Pallas kernels, fetch(): pl.pallas_call(functools.partial(fetch_body, n, width // LANES), out_shap...  3.78 us
    pallas_call x1, Pallas kernels, label(): pl.pallas_call(label_body, out_shape=[vmem_out((length, LANES)) for lengt...  1.14 us
    pallas_call x1, Pallas kernels, finish(): pl.pallas_call(finish_body, out_shape=jax.ShapeDtypeStruct(shape, jnp.bfl...  0.85 us
  transfers between devices with their start and end apart: 11, of which 6 were waited for; matrix products, arithmetic and copies ran while one was open for 0% of the time, Pallas kernels for 39%

profile of v7, /device:TPU:0, one launch (start us, length us, event | category | flops | bytes accessed | tf_op | source)
XLA Modules:
  0.0 41.4 jit_solution(10925544048892673835)
XLA Ops:
  0.0 0.5 %collective-permute-start.2 = (bf16[2048,768]{1,0:T(8,128)(2,1)}, bf16[2048,768]{1,0:T(8,128)(2,1)S(1)}, u32[]{:S(2)}, u32[]{:S(2)}) collective-permute-start(bf16[2048,768]{1,0:T(8,128)(2,1)} %bitcast.5), channel_id=1, source_target_pairs={{0,4},{4,0},{8,12},{12,8},{16,20},{20,16},{24,28},{28,24},{1,5},{5... | collective-permute-start | bytes 9437192 | tf_op jit(solution)/shard_map/ppermute | solution.py:68
  0.5 1.1 %shard_map.64 = (bf16[1040,128]{1,0:T(8,128)(2,1)S(1)}, bf16[1040,128]{1,0:T(8,128)(2,1)S(1)}) custom-call(bf16[128,2048]{1,0:T(8,128)(2,1)} %tokens_ref.1, s32[4,128]{1,0:T(4,128)} %bitcast.11, bf16[4,128]{1,0:T(4,128)(2,1)} %bitcast.12), custom_call_target="tpu_custom_call" | custom-call | tf_op jit(solution)/shard_map/pallas_call | solution.py:128
  1.6 2.6 %collective-permute-start.1 = (bf16[1040,128]{1,0:T(8,128)(2,1)S(1)}, bf16[1040,128]{1,0:T(8,128)(2,1)S(1)}, u32[]{:S(2)}, u32[]{:S(2)}) collective-permute-start(bf16[1040,128]{1,0:T(8,128)(2,1)S(1)} %get-tuple-element.20.refs_4_), channel_id=1, source_target_pairs={{0,16},{4,12},{8,24},{12,4},{16,0},{20,28},{24,8},{28,20},{1,17},{... | collective-permute-start | bytes 798728 | tf_op jit(solution)/shard_map/ppermute | solution.py:68
  4.2 0.1 collective-permute-start
  4.3 0.2 collective-permute-start.6
  4.5 0.3 collective-permute-start.7
  4.8 3.8 %shard_map.65 = (bf16[2048,768]{1,0:T(8,128)(2,1)S(1)}, bf16[2048,768]{1,0:T(8,128)(2,1)S(1)}, bf16[768,2048]{1,0:T(8,128)(2,1)S(1)}, bf16[2064,128]{1,0:T(8,128)(2,1)S(1)}) custom-call(bf16[2048,768]{1,0:T(8,128)(2,1)} %bitcast.6, bf16[2048,768]{1,0:T(8,128)(2,1)} %bitcast.8, bf16[768,2048]{1,0:T(8,128)(2,1)} %bitcast.10, ...), custom_call_target="tpu_custom_call" | custom-call | bytes 18874368 | tf_op jit(solution)/shard_map/pallas_call | solution.py:223
  8.6 0.0 collective-permute-done.1.refs_1_
  8.6 2.0 %collective-permute-start.5 = (bf16[1040,128]{1,0:T(8,128)(2,1)S(1)}, bf16[1040,128]{1,0:T(8,128)(2,1)S(1)}, u32[]{:S(2)}, u32[]{:S(2)}) collective-permute-start(bf16[1040,128]{1,0:T(8,128)(2,1)S(1)} %collective-permute-done.1.refs_1_), channel_id=1, source_target_pairs={{0,8},{4,20},{8,0},{12,28},{16,24},{20,4},{24,16},{28,12},{1,9},{5... | collective-permute-start | bytes 798728 | tf_op jit(solution)/shard_map/ppermute | solution.py:68
  10.6 0.9 %collective-permute-done.refs_0_ = bf16[1040,128]{1,0:T(8,128)(2,1)S(1)} collective-permute-done((bf16[1040,128]{1,0:T(8,128)(2,1)S(1)}, bf16[1040,128]{1,0:T(8,128)(2,1)S(1)}, u32[]{:S(2)}, u32[]{:S(2)}) %collective-permute-start) | collective-permute-done | bytes 266272 | tf_op jit(solution)/shard_map/ppermute | solution.py:68
  11.4 2.2 %collective-permute-start.4 = (bf16[1040,128]{1,0:T(8,128)(2,1)S(1)}, bf16[1040,128]{1,0:T(8,128)(2,1)S(1)}, u32[]{:S(2)}, u32[]{:S(2)}) collective-permute-start(bf16[1040,128]{1,0:T(8,128)(2,1)S(1)} %collective-permute-done.refs_0_), channel_id=1, source_target_pairs={{0,8},{4,20},{8,0},{12,28},{16,24},{20,4},{24,16},{28,12},{1,9},{5... | collective-permute-start | bytes 798728 | tf_op jit(solution)/shard_map/ppermute | solution.py:68
  13.6 0.0 collective-permute-done.2.refs_5_.refs_4_
  13.6 0.0 collective-permute-start.3
  13.7 1.4 %collective-permute-done.5.refs_1_ = bf16[1040,128]{1,0:T(8,128)(2,1)S(1)} collective-permute-done((bf16[1040,128]{1,0:T(8,128)(2,1)S(1)}, bf16[1040,128]{1,0:T(8,128)(2,1)S(1)}, u32[]{:S(2)}, u32[]{:S(2)}) %collective-permute-start.5) | collective-permute-done | bytes 266272 | tf_op jit(solution)/shard_map/ppermute | solution.py:68
  15.1 3.0 %collective-permute-done.4.refs_0_ = bf16[1040,128]{1,0:T(8,128)(2,1)S(1)} collective-permute-done((bf16[1040,128]{1,0:T(8,128)(2,1)S(1)}, bf16[1040,128]{1,0:T(8,128)(2,1)S(1)}, u32[]{:S(2)}, u32[]{:S(2)}) %collective-permute-start.4) | collective-permute-done | bytes 266272 | tf_op jit(solution)/shard_map/ppermute | solution.py:68
  18.1 0.0 collective-permute-done.6.refs_6_.refs_5_
  18.1 0.0 collective-permute-done.7.refs_7_.refs_6_
  18.1 2.7 %shard_map.67 = bf16[128,2048]{1,0:T(8,128)(2,1)S(1)} custom-call(bf16[1040,128]{1,0:T(8,128)(2,1)S(1)} %get-tuple-element.26.refs_0_, bf16[1040,128]{1,0:T(8,128)(2,1)S(1)} %get-tuple-element.27.refs_1_, bf16[2048,768]{1,0:T(8,128)(2,1)S(1)} %get-tuple-element.22.refs_2_.refs_1_, bf16[2048,768]{1,0:T(8,128)(2,1)S(1)} %get-tuple-element.28.refs_3_.refs_2_, ...), custom_call_target="tpu_custom_call" | custom-call | flops 2415919104 | bytes 19922944 | tf_op jit(solution)/shard_map/pallas_call | solution.py:274
  20.8 2.1 %collective-permute-start.8 = (bf16[128,2048]{1,0:T(8,128)(2,1)S(1)}, bf16[128,2048]{1,0:T(8,128)(2,1)S(1)}, u32[]{:S(2)}, u32[]{:S(2)}) collective-permute-start(bf16[128,2048]{1,0:T(8,128)(2,1)S(1)} %shard_map.67), channel_id=1, source_target_pairs={{0,16},{4,12},{8,24},{12,4},{16,0},{20,28},{24,8},{28,20},{1,17},{... | collective-permute-start | bytes 1572872 | tf_op jit(solution)/shard_map/ppermute | solution.py:68
  22.9 2.8 %shard_map.68 = bf16[128,2048]{1,0:T(8,128)(2,1)S(1)} custom-call(bf16[1040,128]{1,0:T(8,128)(2,1)S(1)} %collective-permute-done.refs_0_, bf16[1040,128]{1,0:T(8,128)(2,1)S(1)} %collective-permute-done.1.refs_1_, bf16[2048,768]{1,0:T(8,128)(2,1)S(1)} %get-tuple-element.22.refs_2_.refs_1_, bf16[2048,768]{1,0:T(8,128)(2,1)S(1)} %get-tuple-element.28.refs_3_.refs_2_, ...), custom_call_target="tpu_custom_call" | custom-call | flops 2415919104 | bytes 19922944 | tf_op jit(solution)/shard_map/pallas_call | solution.py:274
  25.7 0.1 collective-permute-start.9
  25.8 0.0 collective-permute-done.3.refs_0_
  25.8 2.8 %shard_map.69 = bf16[128,2048]{1,0:T(8,128)(2,1)S(1)} custom-call(bf16[2064,128]{1,0:T(8,128)(2,1)S(1)} %collective-permute-done.3.refs_0_, bf16[2048,768]{1,0:T(8,128)(2,1)S(1)} %get-tuple-element.22.refs_2_.refs_1_, bf16[2048,768]{1,0:T(8,128)(2,1)S(1)} %get-tuple-element.28.refs_3_.refs_2_, bf16[768,2048]{1,0:T(8,128)(2,1)S(1)} %get-tuple-element.29.refs_4_.refs_3_, ...), custom_call_target="tpu_custom_call" | custom-call | flops 2415919104 | bytes 19922944 | tf_op jit(solution)/shard_map/pallas_call | solution.py:274
  28.6 1.5 %collective-permute-done.8 = bf16[128,2048]{1,0:T(8,128)(2,1)S(1)} collective-permute-done((bf16[128,2048]{1,0:T(8,128)(2,1)S(1)}, bf16[128,2048]{1,0:T(8,128)(2,1)S(1)}, u32[]{:S(2)}, u32[]{:S(2)}) %collective-permute-start.8) | collective-permute-done | bytes 524320 | tf_op jit(solution)/shard_map/ppermute | solution.py:68
  30.1 0.1 add_convert_fusion
  30.2 2.1 %collective-permute-start.10 = (bf16[128,2048]{1,0:T(8,128)(2,1)S(1)}, bf16[128,2048]{1,0:T(8,128)(2,1)S(1)}, u32[]{:S(2)}, u32[]{:S(2)}) collective-permute-start(bf16[128,2048]{1,0:T(8,128)(2,1)S(1)} %add_convert_fusion), channel_id=1, source_target_pairs={{0,8},{4,20},{8,0},{12,28},{16,24},{20,4},{24,16},{28,12},{1,9},{5... | collective-permute-start | bytes 1572872 | tf_op jit(solution)/shard_map/ppermute | solution.py:68
  32.3 2.8 %shard_map.70.a_ref = bf16[128,2048]{1,0:T(8,128)(2,1)S(1)} custom-call(bf16[2064,128]{1,0:T(8,128)(2,1)S(1)} %get-tuple-element.32.refs_0_, bf16[2048,768]{1,0:T(8,128)(2,1)S(1)} %get-tuple-element.22.refs_2_.refs_1_, bf16[2048,768]{1,0:T(8,128)(2,1)S(1)} %get-tuple-element.28.refs_3_.refs_2_, bf16[768,2048]{1,0:T(8,128)(2,1)S(1)} %get-tuple-element.29.refs_4_.refs_3_, ...), custom_call_target="tpu_custom_call" | custom-call | flops 2415919104 | bytes 19922944 | tf_op jit(solution)/shard_map/pallas_call | solution.py:274
  35.1 3.7 %collective-permute-done.9.b_ref = bf16[128,2048]{1,0:T(8,128)(2,1)S(1)} collective-permute-done((bf16[128,2048]{1,0:T(8,128)(2,1)S(1)}, bf16[128,2048]{1,0:T(8,128)(2,1)S(1)}, u32[]{:S(2)}, u32[]{:S(2)}) %collective-permute-start.9) | collective-permute-done | bytes 524320 | tf_op jit(solution)/shard_map/ppermute | solution.py:68
  38.8 0.1 shard_map.71.refs_0_
  39.0 1.6 %collective-permute-done.10.refs_1_ = bf16[128,2048]{1,0:T(8,128)(2,1)S(1)} collective-permute-done((bf16[128,2048]{1,0:T(8,128)(2,1)S(1)}, bf16[128,2048]{1,0:T(8,128)(2,1)S(1)}, u32[]{:S(2)}, u32[]{:S(2)}) %collective-permute-start.10) | collective-permute-done | bytes 524320 | tf_op jit(solution)/shard_map/ppermute | solution.py:68
  40.5 0.9 %shard_map.72 = bf16[128,2048]{1,0:T(8,128)(2,1)} custom-call(f32[128,2048]{1,0:T(8,128)S(1)} %shard_map.71.refs_0_, bf16[128,2048]{1,0:T(8,128)(2,1)S(1)} %collective-permute-done.10.refs_1_), custom_call_target="tpu_custom_call" | custom-call | tf_op jit(solution)/shard_map/pallas_call | solution.py:159
  (1 shorter events, 0.0 us)
Async XLA Ops:
  0.0 13.6 %collective-permute-start.2 = (bf16[2048,768]{1,0:T(8,128)(2,1)}, bf16[2048,768]{1,0:T(8,128)(2,1)S(1)}, u32[]{:S(2)}, u32[]{:S(2)}) collective-permute-start(bf16[2048,768]{1,0:T(8,128)(2,1)} %bitcast.5), channel_id=1, source_target_pairs={{0,4},{4,0},{8,12},{12,8},{16,20},{20,16},{24,28},{28,24},{1,5},{5... | collective-permute-start | bytes 9437192 | tf_op jit(solution)/shard_map/ppermute | solution.py:68
  1.6 7.0 %collective-permute-start.1 = (bf16[1040,128]{1,0:T(8,128)(2,1)S(1)}, bf16[1040,128]{1,0:T(8,128)(2,1)S(1)}, u32[]{:S(2)}, u32[]{:S(2)}) collective-permute-start(bf16[1040,128]{1,0:T(8,128)(2,1)S(1)} %get-tuple-element.20.refs_4_), channel_id=1, source_target_pairs={{0,16},{4,12},{8,24},{12,4},{16,0},{20,28},{24,8},{28,20},{1,17},{... | collective-permute-start | bytes 798728 | tf_op jit(solution)/shard_map/ppermute | solution.py:68
  4.2 7.2 %collective-permute-start = (bf16[1040,128]{1,0:T(8,128)(2,1)S(1)}, bf16[1040,128]{1,0:T(8,128)(2,1)S(1)}, u32[]{:S(2)}, u32[]{:S(2)}) collective-permute-start(bf16[1040,128]{1,0:T(8,128)(2,1)S(1)} %get-tuple-element.19.refs_3_), channel_id=1, source_target_pairs={{0,16},{4,12},{8,24},{12,4},{16,0},{20,28},{24,8},{28,20},{1,17},{... | collective-permute-start | bytes 798728 | tf_op jit(solution)/shard_map/ppermute | solution.py:68
  4.3 13.8 %collective-permute-start.6 = (bf16[2048,768]{1,0:T(8,128)(2,1)}, bf16[2048,768]{1,0:T(8,128)(2,1)S(1)}, u32[]{:S(2)}, u32[]{:S(2)}) collective-permute-start(bf16[2048,768]{1,0:T(8,128)(2,1)} %bitcast.7), channel_id=1, source_target_pairs={{0,4},{4,0},{8,12},{12,8},{16,20},{20,16},{24,28},{28,24},{1,5},{5... | collective-permute-start | bytes 9437192 | tf_op jit(solution)/shard_map/ppermute | solution.py:68
  4.5 13.6 %collective-permute-start.7 = (bf16[768,2048]{1,0:T(8,128)(2,1)}, bf16[768,2048]{1,0:T(8,128)(2,1)S(1)}, u32[]{:S(2)}, u32[]{:S(2)}) collective-permute-start(bf16[768,2048]{1,0:T(8,128)(2,1)} %bitcast.9), channel_id=1, source_target_pairs={{0,4},{4,0},{8,12},{12,8},{16,20},{20,16},{24,28},{28,24},{1,5},{5... | collective-permute-start | bytes 9437192 | tf_op jit(solution)/shard_map/ppermute | solution.py:68
  8.6 6.5 %collective-permute-start.5 = (bf16[1040,128]{1,0:T(8,128)(2,1)S(1)}, bf16[1040,128]{1,0:T(8,128)(2,1)S(1)}, u32[]{:S(2)}, u32[]{:S(2)}) collective-permute-start(bf16[1040,128]{1,0:T(8,128)(2,1)S(1)} %collective-permute-done.1.refs_1_), channel_id=1, source_target_pairs={{0,8},{4,20},{8,0},{12,28},{16,24},{20,4},{24,16},{28,12},{1,9},{5... | collective-permute-start | bytes 798728 | tf_op jit(solution)/shard_map/ppermute | solution.py:68
  11.4 6.6 %collective-permute-start.4 = (bf16[1040,128]{1,0:T(8,128)(2,1)S(1)}, bf16[1040,128]{1,0:T(8,128)(2,1)S(1)}, u32[]{:S(2)}, u32[]{:S(2)}) collective-permute-start(bf16[1040,128]{1,0:T(8,128)(2,1)S(1)} %collective-permute-done.refs_0_), channel_id=1, source_target_pairs={{0,8},{4,20},{8,0},{12,28},{16,24},{20,4},{24,16},{28,12},{1,9},{5... | collective-permute-start | bytes 798728 | tf_op jit(solution)/shard_map/ppermute | solution.py:68
  13.6 12.1 %collective-permute-start.3 = (bf16[2064,128]{1,0:T(8,128)(2,1)S(1)}, bf16[2064,128]{1,0:T(8,128)(2,1)S(1)}, u32[]{:S(2)}, u32[]{:S(2)}) collective-permute-start(bf16[2064,128]{1,0:T(8,128)(2,1)S(1)} %get-tuple-element.32.refs_0_), channel_id=1, source_target_pairs={{0,8},{4,20},{8,0},{12,28},{16,24},{20,4},{24,16},{28,12},{1,9},{5... | collective-permute-start | bytes 1585160 | tf_op jit(solution)/shard_map/ppermute | solution.py:68
  20.8 9.3 %collective-permute-start.8 = (bf16[128,2048]{1,0:T(8,128)(2,1)S(1)}, bf16[128,2048]{1,0:T(8,128)(2,1)S(1)}, u32[]{:S(2)}, u32[]{:S(2)}) collective-permute-start(bf16[128,2048]{1,0:T(8,128)(2,1)S(1)} %shard_map.67), channel_id=1, source_target_pairs={{0,16},{4,12},{8,24},{12,4},{16,0},{20,28},{24,8},{28,20},{1,17},{... | collective-permute-start | bytes 1572872 | tf_op jit(solution)/shard_map/ppermute | solution.py:68
  25.7 13.1 %collective-permute-start.9 = (bf16[128,2048]{1,0:T(8,128)(2,1)S(1)}, bf16[128,2048]{1,0:T(8,128)(2,1)S(1)}, u32[]{:S(2)}, u32[]{:S(2)}) collective-permute-start(bf16[128,2048]{1,0:T(8,128)(2,1)S(1)} %shard_map.68), channel_id=1, source_target_pairs={{0,16},{4,12},{8,24},{12,4},{16,0},{20,28},{24,8},{28,20},{1,17},{... | collective-permute-start | bytes 1572872 | tf_op jit(solution)/shard_map/ppermute | solution.py:68
  30.2 10.3 %collective-permute-start.10 = (bf16[128,2048]{1,0:T(8,128)(2,1)S(1)}, bf16[128,2048]{1,0:T(8,128)(2,1)S(1)}, u32[]{:S(2)}, u32[]{:S(2)}) collective-permute-start(bf16[128,2048]{1,0:T(8,128)(2,1)S(1)} %add_convert_fusion), channel_id=1, source_target_pairs={{0,8},{4,20},{8,0},{12,28},{16,24},{20,4},{24,16},{28,12},{1,9},{5... | collective-permute-start | bytes 1572872 | tf_op jit(solution)/shard_map/ppermute | solution.py:68

commit v8 on v7

--- a/solution.py
+++ b/solution.py
@@ -77,7 +77,7 @@
 
 
 MIB = 1 << 20
-PARTS = 4
+PARTS = 2
 LANES = 128
 WEIGHT_ROWS = 16
 VMEM_SPEC = pl.BlockSpec(memory_space=pltpu.VMEM)
@@ -297,7 +297,7 @@
     own = (w_gate[0], w_up[0], w_down[0])
     *fetched, home = fetch(own, halves, width)
     swapped = [hop(w, CORE) for w in own]
-    near = [after(half, fetched[0]) for half in near]
+    near[1] = after(near[1], fetched[0])
     far = stage([hop(half, SECOND) for half in near], 28000000000)
     side = [hop(after(home, *near, swapped[0]), SECOND)]
 

time: 41.7 us -> 41.7 us (level)
  no operation moved by 1% of the time
where the time goes in v8:
time: 41.7 us; the launch traced here: 41.4 us
  Pallas kernels  17 us (41%)
  starting transfers between devices  12.1 us (29%)
  waiting for transfers between devices  12.1 us (29%)
    ppermute x11, waiting for transfers between devices, hop(): return lax.ppermute(block, AXIS, pairs)  12.1 us
    ppermute x11, starting transfers between devices, hop(): return lax.ppermute(block, AXIS, pairs)  12.1 us
    pallas_call x4, Pallas kernels, ffn(): pl.pallas_call(functools.partial(ffn_body, steps, len(blocks)), out_shape...  11.1 us
    pallas_call x1, Pallas kernels, fetch(): pl.pallas_call(functools.partial(fetch_body, n, width // LANES), out_shap...  3.78 us
    pallas_call x1, Pallas kernels, label(): pl.pallas_call(label_body, out_shape=[vmem_out((length, LANES)) for lengt...  1.14 us
    pallas_call x1, Pallas kernels, finish(): pl.pallas_call(finish_body, out_shape=jax.ShapeDtypeStruct(shape, jnp.bfl...  0.87 us
  transfers between devices with their start and end apart: 11, of which 6 were waited for; matrix products, arithmetic and copies ran while one was open for 0% of the time, Pallas kernels for 39%

profile of v8, /device:TPU:0, one launch (start us, length us, event | category | flops | bytes accessed | tf_op | source)
XLA Modules:
  0.0 41.4 jit_solution(9728676189427436895)
XLA Ops:
  0.0 0.5 %collective-permute-start.2 = (bf16[2048,768]{1,0:T(8,128)(2,1)}, bf16[2048,768]{1,0:T(8,128)(2,1)S(1)}, u32[]{:S(2)}, u32[]{:S(2)}) collective-permute-start(bf16[2048,768]{1,0:T(8,128)(2,1)} %bitcast.5), channel_id=1, source_target_pairs={{0,4},{4,0},{8,12},{12,8},{16,20},{20,16},{24,28},{28,24},{1,5},{5... | collective-permute-start | bytes 9437192 | tf_op jit(solution)/shard_map/ppermute | solution.py:68
  0.5 1.1 %shard_map.64 = (bf16[1040,128]{1,0:T(8,128)(2,1)S(1)}, bf16[1040,128]{1,0:T(8,128)(2,1)S(1)}) custom-call(bf16[128,2048]{1,0:T(8,128)(2,1)} %tokens_ref.1, s32[4,128]{1,0:T(4,128)} %bitcast.11, bf16[4,128]{1,0:T(4,128)(2,1)} %bitcast.12), custom_call_target="tpu_custom_call" | custom-call | tf_op jit(solution)/shard_map/pallas_call | solution.py:128
  1.6 2.6 %collective-permute-start.1 = (bf16[1040,128]{1,0:T(8,128)(2,1)S(1)}, bf16[1040,128]{1,0:T(8,128)(2,1)S(1)}, u32[]{:S(2)}, u32[]{:S(2)}) collective-permute-start(bf16[1040,128]{1,0:T(8,128)(2,1)S(1)} %get-tuple-element.19.refs_4_), channel_id=1, source_target_pairs={{0,16},{4,12},{8,24},{12,4},{16,0},{20,28},{24,8},{28,20},{1,17},{... | collective-permute-start | bytes 798728 | tf_op jit(solution)/shard_map/ppermute | solution.py:68
  4.2 0.1 collective-permute-start
  4.3 0.2 collective-permute-start.6
  4.5 0.3 collective-permute-start.7
  4.8 3.8 %shard_map.65 = (bf16[2048,768]{1,0:T(8,128)(2,1)S(1)}, bf16[2048,768]{1,0:T(8,128)(2,1)S(1)}, bf16[768,2048]{1,0:T(8,128)(2,1)S(1)}, bf16[2064,128]{1,0:T(8,128)(2,1)S(1)}) custom-call(bf16[2048,768]{1,0:T(8,128)(2,1)} %bitcast.6, bf16[2048,768]{1,0:T(8,128)(2,1)} %bitcast.8, bf16[768,2048]{1,0:T(8,128)(2,1)} %bitcast.10, ...), custom_call_target="tpu_custom_call" | custom-call | bytes 18874368 | tf_op jit(solution)/shard_map/pallas_call | solution.py:223
  8.6 0.0 collective-permute-done.1.refs_1_
  8.6 2.0 %collective-permute-start.5 = (bf16[1040,128]{1,0:T(8,128)(2,1)S(1)}, bf16[1040,128]{1,0:T(8,128)(2,1)S(1)}, u32[]{:S(2)}, u32[]{:S(2)}) collective-permute-start(bf16[1040,128]{1,0:T(8,128)(2,1)S(1)} %collective-permute-done.1.refs_1_), channel_id=1, source_target_pairs={{0,8},{4,20},{8,0},{12,28},{16,24},{20,4},{24,16},{28,12},{1,9},{5... | collective-permute-start | bytes 798728 | tf_op jit(solution)/shard_map/ppermute | solution.py:68
  10.6 0.9 %collective-permute-done.refs_0_ = bf16[1040,128]{1,0:T(8,128)(2,1)S(1)} collective-permute-done((bf16[1040,128]{1,0:T(8,128)(2,1)S(1)}, bf16[1040,128]{1,0:T(8,128)(2,1)S(1)}, u32[]{:S(2)}, u32[]{:S(2)}) %collective-permute-start) | collective-permute-done | bytes 266272 | tf_op jit(solution)/shard_map/ppermute | solution.py:68
  11.4 2.2 %collective-permute-start.4 = (bf16[1040,128]{1,0:T(8,128)(2,1)S(1)}, bf16[1040,128]{1,0:T(8,128)(2,1)S(1)}, u32[]{:S(2)}, u32[]{:S(2)}) collective-permute-start(bf16[1040,128]{1,0:T(8,128)(2,1)S(1)} %collective-permute-done.refs_0_), channel_id=1, source_target_pairs={{0,8},{4,20},{8,0},{12,28},{16,24},{20,4},{24,16},{28,12},{1,9},{5... | collective-permute-start | bytes 798728 | tf_op jit(solution)/shard_map/ppermute | solution.py:68
  13.6 0.0 collective-permute-done.2.refs_5_.refs_4_
  13.6 0.0 collective-permute-start.3
  13.7 1.4 %collective-permute-done.5.refs_1_ = bf16[1040,128]{1,0:T(8,128)(2,1)S(1)} collective-permute-done((bf16[1040,128]{1,0:T(8,128)(2,1)S(1)}, bf16[1040,128]{1,0:T(8,128)(2,1)S(1)}, u32[]{:S(2)}, u32[]{:S(2)}) %collective-permute-start.5) | collective-permute-done | bytes 266272 | tf_op jit(solution)/shard_map/ppermute | solution.py:68
  15.1 3.0 %collective-permute-done.4.refs_0_ = bf16[1040,128]{1,0:T(8,128)(2,1)S(1)} collective-permute-done((bf16[1040,128]{1,0:T(8,128)(2,1)S(1)}, bf16[1040,128]{1,0:T(8,128)(2,1)S(1)}, u32[]{:S(2)}, u32[]{:S(2)}) %collective-permute-start.4) | collective-permute-done | bytes 266272 | tf_op jit(solution)/shard_map/ppermute | solution.py:68
  18.1 0.0 collective-permute-done.6.refs_6_.refs_5_
  18.1 0.0 collective-permute-done.7.refs_7_.refs_6_
  18.1 2.7 %shard_map.67 = bf16[128,2048]{1,0:T(8,128)(2,1)S(1)} custom-call(bf16[1040,128]{1,0:T(8,128)(2,1)S(1)} %get-tuple-element.24.refs_0_, bf16[1040,128]{1,0:T(8,128)(2,1)S(1)} %get-tuple-element.25.refs_1_, bf16[2048,768]{1,0:T(8,128)(2,1)S(1)} %get-tuple-element.21.refs_2_.refs_1_, bf16[2048,768]{1,0:T(8,128)(2,1)S(1)} %get-tuple-element.26.refs_3_.refs_2_, ...), custom_call_target="tpu_custom_call" | custom-call | flops 2415919104 | bytes 19922944 | tf_op jit(solution)/shard_map/pallas_call | solution.py:274
  20.8 2.1 %collective-permute-start.8 = (bf16[128,2048]{1,0:T(8,128)(2,1)S(1)}, bf16[128,2048]{1,0:T(8,128)(2,1)S(1)}, u32[]{:S(2)}, u32[]{:S(2)}) collective-permute-start(bf16[128,2048]{1,0:T(8,128)(2,1)S(1)} %shard_map.67), channel_id=1, source_target_pairs={{0,16},{4,12},{8,24},{12,4},{16,0},{20,28},{24,8},{28,20},{1,17},{... | collective-permute-start | bytes 1572872 | tf_op jit(solution)/shard_map/ppermute | solution.py:68
  22.9 2.8 %shard_map.68 = bf16[128,2048]{1,0:T(8,128)(2,1)S(1)} custom-call(bf16[1040,128]{1,0:T(8,128)(2,1)S(1)} %collective-permute-done.refs_0_, bf16[1040,128]{1,0:T(8,128)(2,1)S(1)} %collective-permute-done.1.refs_1_, bf16[2048,768]{1,0:T(8,128)(2,1)S(1)} %get-tuple-element.21.refs_2_.refs_1_, bf16[2048,768]{1,0:T(8,128)(2,1)S(1)} %get-tuple-element.26.refs_3_.refs_2_, ...), custom_call_target="tpu_custom_call" | custom-call | flops 2415919104 | bytes 19922944 | tf_op jit(solution)/shard_map/pallas_call | solution.py:274
  25.7 0.1 collective-permute-start.9
  25.8 0.0 collective-permute-done.3.refs_0_
  25.8 2.8 %shard_map.69 = bf16[128,2048]{1,0:T(8,128)(2,1)S(1)} custom-call(bf16[2064,128]{1,0:T(8,128)(2,1)S(1)} %collective-permute-done.3.refs_0_, bf16[2048,768]{1,0:T(8,128)(2,1)S(1)} %get-tuple-element.21.refs_2_.refs_1_, bf16[2048,768]{1,0:T(8,128)(2,1)S(1)} %get-tuple-element.26.refs_3_.refs_2_, bf16[768,2048]{1,0:T(8,128)(2,1)S(1)} %get-tuple-element.27.refs_4_.refs_3_, ...), custom_call_target="tpu_custom_call" | custom-call | flops 2415919104 | bytes 19922944 | tf_op jit(solution)/shard_map/pallas_call | solution.py:274
  28.6 1.5 %collective-permute-done.8 = bf16[128,2048]{1,0:T(8,128)(2,1)S(1)} collective-permute-done((bf16[128,2048]{1,0:T(8,128)(2,1)S(1)}, bf16[128,2048]{1,0:T(8,128)(2,1)S(1)}, u32[]{:S(2)}, u32[]{:S(2)}) %collective-permute-start.8) | collective-permute-done | bytes 524320 | tf_op jit(solution)/shard_map/ppermute | solution.py:68
  30.1 0.1 add_convert_fusion
  30.2 2.1 %collective-permute-start.10 = (bf16[128,2048]{1,0:T(8,128)(2,1)S(1)}, bf16[128,2048]{1,0:T(8,128)(2,1)S(1)}, u32[]{:S(2)}, u32[]{:S(2)}) collective-permute-start(bf16[128,2048]{1,0:T(8,128)(2,1)S(1)} %add_convert_fusion), channel_id=1, source_target_pairs={{0,8},{4,20},{8,0},{12,28},{16,24},{20,4},{24,16},{28,12},{1,9},{5... | collective-permute-start | bytes 1572872 | tf_op jit(solution)/shard_map/ppermute | solution.py:68
  32.3 2.8 %shard_map.70.a_ref = bf16[128,2048]{1,0:T(8,128)(2,1)S(1)} custom-call(bf16[2064,128]{1,0:T(8,128)(2,1)S(1)} %get-tuple-element.30.refs_0_, bf16[2048,768]{1,0:T(8,128)(2,1)S(1)} %get-tuple-element.21.refs_2_.refs_1_, bf16[2048,768]{1,0:T(8,128)(2,1)S(1)} %get-tuple-element.26.refs_3_.refs_2_, bf16[768,2048]{1,0:T(8,128)(2,1)S(1)} %get-tuple-element.27.refs_4_.refs_3_, ...), custom_call_target="tpu_custom_call" | custom-call | flops 2415919104 | bytes 19922944 | tf_op jit(solution)/shard_map/pallas_call | solution.py:274
  35.1 3.7 %collective-permute-done.9.b_ref = bf16[128,2048]{1,0:T(8,128)(2,1)S(1)} collective-permute-done((bf16[128,2048]{1,0:T(8,128)(2,1)S(1)}, bf16[128,2048]{1,0:T(8,128)(2,1)S(1)}, u32[]{:S(2)}, u32[]{:S(2)}) %collective-permute-start.9) | collective-permute-done | bytes 524320 | tf_op jit(solution)/shard_map/ppermute | solution.py:68
  38.8 0.1 shard_map.71.refs_0_
  39.0 1.6 %collective-permute-done.10.refs_1_ = bf16[128,2048]{1,0:T(8,128)(2,1)S(1)} collective-permute-done((bf16[128,2048]{1,0:T(8,128)(2,1)S(1)}, bf16[128,2048]{1,0:T(8,128)(2,1)S(1)}, u32[]{:S(2)}, u32[]{:S(2)}) %collective-permute-start.10) | collective-permute-done | bytes 524320 | tf_op jit(solution)/shard_map/ppermute | solution.py:68
  40.5 0.9 %shard_map.72 = bf16[128,2048]{1,0:T(8,128)(2,1)} custom-call(f32[128,2048]{1,0:T(8,128)S(1)} %shard_map.71.refs_0_, bf16[128,2048]{1,0:T(8,128)(2,1)S(1)} %collective-permute-done.10.refs_1_), custom_call_target="tpu_custom_call" | custom-call | tf_op jit(solution)/shard_map/pallas_call | solution.py:159
  (1 shorter events, 0.0 us)
Async XLA Ops:
  0.0 13.6 %collective-permute-start.2 = (bf16[2048,768]{1,0:T(8,128)(2,1)}, bf16[2048,768]{1,0:T(8,128)(2,1)S(1)}, u32[]{:S(2)}, u32[]{:S(2)}) collective-permute-start(bf16[2048,768]{1,0:T(8,128)(2,1)} %bitcast.5), channel_id=1, source_target_pairs={{0,4},{4,0},{8,12},{12,8},{16,20},{20,16},{24,28},{28,24},{1,5},{5... | collective-permute-start | bytes 9437192 | tf_op jit(solution)/shard_map/ppermute | solution.py:68
  1.6 7.0 %collective-permute-start.1 = (bf16[1040,128]{1,0:T(8,128)(2,1)S(1)}, bf16[1040,128]{1,0:T(8,128)(2,1)S(1)}, u32[]{:S(2)}, u32[]{:S(2)}) collective-permute-start(bf16[1040,128]{1,0:T(8,128)(2,1)S(1)} %get-tuple-element.19.refs_4_), channel_id=1, source_target_pairs={{0,16},{4,12},{8,24},{12,4},{16,0},{20,28},{24,8},{28,20},{1,17},{... | collective-permute-start | bytes 798728 | tf_op jit(solution)/shard_map/ppermute | solution.py:68
  4.2 7.2 %collective-permute-start = (bf16[1040,128]{1,0:T(8,128)(2,1)S(1)}, bf16[1040,128]{1,0:T(8,128)(2,1)S(1)}, u32[]{:S(2)}, u32[]{:S(2)}) collective-permute-start(bf16[1040,128]{1,0:T(8,128)(2,1)S(1)} %get-tuple-element.18.refs_3_), channel_id=1, source_target_pairs={{0,16},{4,12},{8,24},{12,4},{16,0},{20,28},{24,8},{28,20},{1,17},{... | collective-permute-start | bytes 798728 | tf_op jit(solution)/shard_map/ppermute | solution.py:68
  4.3 13.8 %collective-permute-start.6 = (bf16[2048,768]{1,0:T(8,128)(2,1)}, bf16[2048,768]{1,0:T(8,128)(2,1)S(1)}, u32[]{:S(2)}, u32[]{:S(2)}) collective-permute-start(bf16[2048,768]{1,0:T(8,128)(2,1)} %bitcast.7), channel_id=1, source_target_pairs={{0,4},{4,0},{8,12},{12,8},{16,20},{20,16},{24,28},{28,24},{1,5},{5... | collective-permute-start | bytes 9437192 | tf_op jit(solution)/shard_map/ppermute | solution.py:68
  4.5 13.6 %collective-permute-start.7 = (bf16[768,2048]{1,0:T(8,128)(2,1)}, bf16[768,2048]{1,0:T(8,128)(2,1)S(1)}, u32[]{:S(2)}, u32[]{:S(2)}) collective-permute-start(bf16[768,2048]{1,0:T(8,128)(2,1)} %bitcast.9), channel_id=1, source_target_pairs={{0,4},{4,0},{8,12},{12,8},{16,20},{20,16},{24,28},{28,24},{1,5},{5... | collective-permute-start | bytes 9437192 | tf_op jit(solution)/shard_map/ppermute | solution.py:68
  8.6 6.5 %collective-permute-start.5 = (bf16[1040,128]{1,0:T(8,128)(2,1)S(1)}, bf16[1040,128]{1,0:T(8,128)(2,1)S(1)}, u32[]{:S(2)}, u32[]{:S(2)}) collective-permute-start(bf16[1040,128]{1,0:T(8,128)(2,1)S(1)} %collective-permute-done.1.refs_1_), channel_id=1, source_target_pairs={{0,8},{4,20},{8,0},{12,28},{16,24},{20,4},{24,16},{28,12},{1,9},{5... | collective-permute-start | bytes 798728 | tf_op jit(solution)/shard_map/ppermute | solution.py:68
  11.4 6.6 %collective-permute-start.4 = (bf16[1040,128]{1,0:T(8,128)(2,1)S(1)}, bf16[1040,128]{1,0:T(8,128)(2,1)S(1)}, u32[]{:S(2)}, u32[]{:S(2)}) collective-permute-start(bf16[1040,128]{1,0:T(8,128)(2,1)S(1)} %collective-permute-done.refs_0_), channel_id=1, source_target_pairs={{0,8},{4,20},{8,0},{12,28},{16,24},{20,4},{24,16},{28,12},{1,9},{5... | collective-permute-start | bytes 798728 | tf_op jit(solution)/shard_map/ppermute | solution.py:68
  13.6 12.1 %collective-permute-start.3 = (bf16[2064,128]{1,0:T(8,128)(2,1)S(1)}, bf16[2064,128]{1,0:T(8,128)(2,1)S(1)}, u32[]{:S(2)}, u32[]{:S(2)}) collective-permute-start(bf16[2064,128]{1,0:T(8,128)(2,1)S(1)} %get-tuple-element.30.refs_0_), channel_id=1, source_target_pairs={{0,8},{4,20},{8,0},{12,28},{16,24},{20,4},{24,16},{28,12},{1,9},{5... | collective-permute-start | bytes 1585160 | tf_op jit(solution)/shard_map/ppermute | solution.py:68
  20.8 9.3 %collective-permute-start.8 = (bf16[128,2048]{1,0:T(8,128)(2,1)S(1)}, bf16[128,2048]{1,0:T(8,128)(2,1)S(1)}, u32[]{:S(2)}, u32[]{:S(2)}) collective-permute-start(bf16[128,2048]{1,0:T(8,128)(2,1)S(1)} %shard_map.67), channel_id=1, source_target_pairs={{0,16},{4,12},{8,24},{12,4},{16,0},{20,28},{24,8},{28,20},{1,17},{... | collective-permute-start | bytes 1572872 | tf_op jit(solution)/shard_map/ppermute | solution.py:68
  25.7 13.1 %collective-permute-start.9 = (bf16[128,2048]{1,0:T(8,128)(2,1)S(1)}, bf16[128,2048]{1,0:T(8,128)(2,1)S(1)}, u32[]{:S(2)}, u32[]{:S(2)}) collective-permute-start(bf16[128,2048]{1,0:T(8,128)(2,1)S(1)} %shard_map.68), channel_id=1, source_target_pairs={{0,16},{4,12},{8,24},{12,4},{16,0},{20,28},{24,8},{28,20},{1,17},{... | collective-permute-start | bytes 1572872 | tf_op jit(solution)/shard_map/ppermute | solution.py:68
  30.2 10.3 %collective-permute-start.10 = (bf16[128,2048]{1,0:T(8,128)(2,1)S(1)}, bf16[128,2048]{1,0:T(8,128)(2,1)S(1)}, u32[]{:S(2)}, u32[]{:S(2)}) collective-permute-start(bf16[128,2048]{1,0:T(8,128)(2,1)S(1)} %add_convert_fusion), channel_id=1, source_target_pairs={{0,8},{4,20},{8,0},{12,28},{16,24},{20,4},{24,16},{28,12},{1,9},{5... | collective-permute-start | bytes 1572872 | tf_op jit(solution)/shard_map/ppermute | solution.py:68
